TPU v7x, 256 devices: a whole 4x4x8 slice. The times are simulated.
256 devices in a mesh: xfer: 32 (over x, y, core), head: 8 (over z).
Axes of the slice: x: 4, y: 4, z: 8, core: 2. Of those that a mesh axis runs over, the one named last changes fastest.
Arguments:
- kv_pool: bfloat16 [8192, 64, 576], P(('xfer', 'head')), may hold values from -8 to 8
- lengths: int32 [256], replicated, may hold values from 2 to 15936, as said below
- start_device: int32 [256], replicated, may hold values from 0 to 255, as said below
- page_table: int32 [256, 256], replicated, may hold values from 0 to 31, as said below
- queries: bfloat16 [512, 128, 192], P('xfer', 'head'), may hold values from -100 to 100
- new_latent: bfloat16 [512, 576], P('xfer'), may hold values from -100 to 100
- key_up: bfloat16 [128, 128, 512], P('head'), may hold values from -0.25 to 0.25
- value_up: bfloat16 [128, 512, 128], P('head'), may hold values from -0.25 to 0.25
- out_proj: bfloat16 [16384, 7168], P('head', 'xfer'), may hold values from -0.046875 to 0.046875
Outputs:
- attn_out: bfloat16 [512, 7168], P('head', 'xfer')
Inputs may be any that keep to these rules, and one draw needn't show every extreme that they name: `lengths`: request r belongs to decode owner xfer index r // 8. The pages of one owner's requests number 256 // 2 to 256, exactly 256 for some owner, so one owner has at most one page on any device. Page j of request r lies on device (start_device[r] + j) mod 256. `page_table`: entries past a request's pages are 0; two pages on one device never share a slot.
All inputs are finite; a program needn't handle non-finite values.
Results may differ from a plain program's by a relative error of at most 0.0058.
Values may be sent and summed in bfloat16 or wider, within the bound.
A program may use at most 128 MiB of HBM per device.

v0:
```python
import jax
import jax.numpy as jnp
from jax import lax
from jax.sharding import PartitionSpec as P

STEPS = 2


def copy_for_each(array, axis):
    copies = jnp.broadcast_to(array, (lax.axis_size(axis), *array.shape))
    return lax.all_to_all(copies, axis, split_axis=0, concat_axis=0, tiled=True)


def of_everyone(array, axis):
    return copy_for_each(array, axis).max(axis=0)


def sent_together(arrays, axis, dim, along):
    columns = [a.reshape(*a.shape[:along], -1) for a in arrays]
    both = jnp.concatenate(columns, axis=along)
    out, at, done = (lax.psum_scatter(both, axis, scatter_dimension=dim, tiled=True), 0, [])
    for a, column in zip(arrays, columns):
        piece = out[..., at : at + column.shape[along]]
        done.append(piece.reshape(*piece.shape[:along], *a.shape[along:]))
        at += column.shape[along]
    return tuple(done)


def in_order(blocks, dim):
    blocks = jnp.moveaxis(blocks, 0, dim)
    dims = blocks.shape
    return blocks.reshape(*dims[:dim], dims[dim] * dims[dim + 1], *dims[dim + 2 :])


def gather_directly(array, axis, dim):
    blocks = copy_for_each(array, axis)
    return in_order(blocks, dim)


def split_up(array, dim, peers):
    before, after = (array.shape[:dim], array.shape[dim + 1 :])
    return jnp.moveaxis(array.reshape(*before, peers, -1, *after), dim, 0)


def sum_at_owner(array, axis, dim):
    peers = lax.axis_size(axis)
    blocks = lax.all_to_all(split_up(array, dim, peers), axis, 0, 0, tiled=True)
    return jnp.sum(blocks, axis=0)


def score_parts(qfull, key_rows, key_visible, fresh, fresh_visible, score_scale):
    cached = (
        jnp.einsum("rhc,kc->rhk", qfull, key_rows, preferred_element_type=jnp.float32) * score_scale
    )
    cached = jnp.where(key_visible[:, None, :], cached, -jnp.inf)
    recent = (
        jnp.einsum("rhc,kc->rhk", qfull, fresh, preferred_element_type=jnp.float32) * score_scale
    )
    recent = jnp.where(fresh_visible[:, None, :], recent, -jnp.inf)
    return (cached, recent)


def weighted_sums(cached, recent, row_top, key_rows, fresh, lat_rank):
    cached_w = jnp.exp(cached - row_top[..., None])
    recent_w = jnp.exp(recent - row_top[..., None])
    total = jnp.sum(cached_w, axis=-1) + jnp.sum(recent_w, axis=-1)
    summed = jnp.einsum(
        "rhk,kc->rhc",
        cached_w.astype(jnp.bfloat16),
        key_rows[:, :lat_rank],
        preferred_element_type=jnp.float32,
    )
    summed = summed + jnp.einsum(
        "rhk,kc->rhc",
        recent_w.astype(jnp.bfloat16),
        fresh[:, :lat_rank],
        preferred_element_type=jnp.float32,
    )
    return (summed, total)


def body(
    kv_pool, lengths, start_device, page_table, queries, new_latent, key_up, value_up, out_proj
):
    owners = lax.axis_size("xfer")
    groups = lax.axis_size("head")
    devices = owners * groups
    owner_idx = lax.axis_index("xfer")
    member = lax.axis_index("head")
    local_device = owner_idx * groups + member
    page_len = kv_pool.shape[1]
    latent = kv_pool.shape[2]
    lat_rank = value_up.shape[1]
    nope = key_up.shape[1]
    per_owner = lengths.shape[0] // owners
    table_width = page_table.shape[1]
    score_scale = queries.shape[2] ** (-0.5)
    page_counts = (lengths + page_len - 1) // page_len
    column = jnp.arange(table_width, dtype=jnp.int32)
    located = ((start_device[:, None] + column[None, :]) % devices == local_device) & (
        column[None, :] < page_counts[:, None]
    )
    chosen = (
        jnp.sum(jnp.where(located, page_table, 0), axis=1).reshape(owners, per_owner).sum(axis=1)
    )
    outgoing = jnp.take(kv_pool, chosen, axis=0)
    arrived = lax.all_to_all(outgoing, "xfer", split_axis=0, concat_axis=0, tiled=True)
    first_req = owner_idx * per_owner
    my_lengths = lax.dynamic_slice_in_dim(lengths, first_req, per_owner, 0)
    my_starts = lax.dynamic_slice_in_dim(start_device, first_req, per_owner, 0)
    token_offset = jnp.arange(page_len, dtype=jnp.int32)
    row_count = queries.shape[0]
    row_ids = jnp.arange(row_count, dtype=jnp.int32)
    fresh_visible = (row_ids[:, None] // STEPS == row_ids[None, :] // STEPS) & (
        row_ids[None, :] <= row_ids[:, None]
    )
    absorbed = jnp.einsum(
        "rhn,hnc->rhc", queries[:, :, :nope], key_up, preferred_element_type=jnp.float32
    ).astype(jnp.bfloat16)
    qfull = jnp.concatenate([absorbed, queries[:, :, nope:]], axis=-1)
    every_head = lax.all_gather(qfull, "head", axis=1, tiled=True)
    devices_of = jnp.arange(owners, dtype=jnp.int32) * groups + member
    key_rows = arrived.reshape(-1, latent)
    own_fresh = fresh_visible & (member == 0)
    page_pos = (devices_of[None, :] - my_starts[:, None]) % devices
    token_pos = page_pos[:, :, None] * page_len + token_offset[None, None, :]
    visible = (token_pos < my_lengths[:, None, None]).reshape(per_owner, -1)
    cached, recent = score_parts(
        every_head, key_rows, jnp.repeat(visible, STEPS, axis=0), new_latent, own_fresh, score_scale
    )
    local_top = jnp.maximum(jnp.max(cached, axis=-1), jnp.max(recent, axis=-1))
    row_top = of_everyone(local_top, "head")
    summed, total = weighted_sums(cached, recent, row_top, key_rows, new_latent, lat_rank)
    summed, total = sent_together((summed, total), "head", 1, 2)
    latent_out = (summed / total[..., None]).astype(jnp.bfloat16)
    head_out = jnp.einsum(
        "rhc,hcv->rhv", latent_out, value_up, preferred_element_type=jnp.float32
    ).astype(jnp.bfloat16)
    head_out = head_out.reshape(row_count, -1)
    every_row = gather_directly(head_out, "xfer", 0)
    return sum_at_owner(
        jnp.dot(every_row, out_proj, preferred_element_type=jnp.float32), "head", 0
    ).astype(jnp.bfloat16)


def solution(mesh):
    in_specs = (
        P(("xfer", "head"), None, None),
        P(),
        P(),
        P(),
        P("xfer", "head", None),
        P("xfer", None),
        P("head", None, None),
        P("head", None, None),
        P("head", "xfer"),
    )
    out_specs = P("head", "xfer")
    return jax.shard_map(body, mesh=mesh, in_specs=in_specs, out_specs=out_specs, check_vma=False)
```

profile of v0, /device:TPU:1, one launch (start us, length us, event | category | flops | bytes accessed | tf_op | source)
XLA Modules:
  0.0 245.4 jit_solution(15916643114462213111)
XLA Ops:
  6.5 0.0 copy-start
  6.5 0.0 all-gather.2.cloned.1.call-start
  6.6 1.0 slice.18
  7.6 0.8 slice.19
  8.4 2.0 fusion.13
  10.4 0.8 pad_maximum_fusion.1
  11.2 0.0 all-gather.2.cloned.1.call-update
  11.2 0.0 copy-done.5
  11.2 0.0 copy-done.4
  11.3 0.3 select_reduce_fusion
  11.6 0.1 reshape.208
  11.6 0.1 reduce_sum.48
  11.8 2.4 gather_fusion
  14.2 3.6 %broadcast_select_fusion = bf16[32,64,576]{2,1,0:T(8,128)(2,1)} fusion(bf16[32,64,576]{2,1,0:T(8,128)(2,1)} %gather_fusion, pred[32]{0:T(512)(128)(4,1)S(1)} %compare_and_fusion), kind=kLoop, calls=%fused_computation.12 | loop fusion | flops 1179648 | bytes 4718624 | tf_op jit(solution)/shard_map/jit(_take)/select_n | solution.py:106
  17.8 8.6 %all-to-all-start = ((bf16[32,64,576]{2,1,0:T(8,128)(2,1)}), bf16[32,64,576]{2,1,0:T(8,128)(2,1)}, u32[]{:S(2)}, u32[]{:S(2)}) async-start(bf16[32,64,576]{2,1,0:T(8,128)(2,1)} %broadcast_select_fusion), calls=%async_computation | async-start | bytes 5242880 | tf_op jit(solution)/shard_map/all_to_all | solution.py:107
  26.4 0.0 reduce-scatter.2.cloned.1.call-start
  26.5 0.1 dynamic_slice.6
  26.5 0.1 dynamic_slice.7
  26.6 0.1 fusion.41
  26.7 0.1 add.129
  26.8 0.1 add.130
  26.9 0.1 add.132
  27.0 0.1 add_compare_fusion
  27.1 0.1 broadcast_in_dim.63
  27.1 0.1 broadcast_in_dim.64
  27.2 0.1 fusion.40
  27.3 33.0 %all-to-all-done = bf16[32,64,576]{2,1,0:T(8,128)(2,1)} async-done(((bf16[32,64,576]{2,1,0:T(8,128)(2,1)}), bf16[32,64,576]{2,1,0:T(8,128)(2,1)}, u32[]{:S(2)}, u32[]{:S(2)}) %all-to-all-start) | async-done | bytes 2359328 | tf_op jit(solution)/shard_map/all_to_all | solution.py:107
  60.4 12.6 %fusion = (f32[16,128]{1,0:T(8,128)S(1)}, f32[16,128,2048]{2,1,0:T(8,128)}) fusion(pred[16,2048]{1,0:T(8,128)(4,1)S(1)} %broadcast_in_dim.64, bf16[2048,576,1]{1,0,2:T(8,128)(2,1)} %bitcast.4, bf16[16,128,576]{2,0,1:T(8,128)(2,1)} %all-gather.2.cloned.1.call-done), kind=kOutput, calls=%fused_computation.3 | convolution fusion | flops 4844419072 | bytes 21536768 | tf_op jit(solution)/shard_map/rhc,kc->rhk/dot_general | solution.py:53
  73.0 0.0 copy-done.6
  73.0 0.9 fusion.46
  73.9 15.2 %all_to_all.20 = f32[8,16,128]{2,1,0:T(8,128)S(1)} all-to-all(f32[8,16,128]{2,1,0:T(8,128)S(1)} %broadcast_in_dim.71), channel_id=1, replica_groups=mesh['xfer'=32,'head'=8] {'head'}, dimensions={0} | all-to-all | bytes 131072 | tf_op jit(solution)/shard_map/all_to_all | solution.py:11
  89.1 9.0 %fusion.1 = f32[16,128]{1,0:T(8,128)S(1)} fusion(f32[16,128,2048]{2,1,0:T(8,128)} %get-tuple-element.6, f32[16,128]{1,0:T(8,128)S(1)} %reduce_max.29, pred[16,2048]{1,0:T(8,128)(4,1)S(1)} %broadcast_in_dim.64), kind=kLoop, calls=%fused_computation.4 | loop fusion | flops 16775168 | bytes 16826368 | tf_op jit(solution)/shard_map/reduce_sum | solution.py:66
  98.1 1.6 copy-done.1
  99.8 6.2 %fusion.3 = f32[16,128,512]{2,1,0:T(8,128)S(1)} fusion(f32[16,128,2048]{2,1,0:T(8,128)S(1)} %copy-done.1, f32[16,128]{1,0:T(8,128)S(1)} %reduce_max.29, pred[16,2048]{1,0:T(8,128)(4,1)S(1)} %broadcast_in_dim.64, bf16[2048,576]{1,0:T(8,128)(2,1)} %bitcast.3), kind=kOutput, calls=%fused_computation.6 | convolution fusion | flops 4311744512 | bytes 23109632 | tf_op jit(solution)/shard_map/rhk,kc->rhc/dot_general | solution.py:67
  106.0 2.8 %convolution_add_fusion = f32[16,128,512]{2,1,0:T(8,128)} fusion(f32[16,128,512]{2,1,0:T(8,128)S(1)} %fusion.3, f32[16,128,16]{1,2,0:T(8,128)S(1)} %get-tuple-element.8, f32[16,128]{1,0:T(8,128)S(1)} %reduce_max.29, bf16[16,576]{1,0:T(8,128)(2,1)S(1)} %copy-done.3), kind=kOutput, calls=%fused_computation.17 | convolution fusion | flops 34668544 | bytes 8544256 | tf_op jit(solution)/shard_map/rhk,kc->rhc/dot_general | solution.py:73
  108.8 1.4 copy.38
  110.2 5.4 %pad_maximum_fusion = f32[16,128,513]{2,1,0:T(8,128)} fusion(f32[16,128,1]{2,1,0:T(8,128)} %copy.38, f32[16,128,512]{2,1,0:T(8,128)} %convolution_add_fusion), kind=kLoop, calls=%fused_computation.11 | loop fusion | flops 1050624 | bytes 8404992 | tf_op jit(solution)/shard_map/concatenate | solution.py:20
  115.5 0.0 reduce-scatter.2.cloned.1.call-update
  115.6 59.7 %reduce-scatter.2.cloned.1.call-done = f32[16,16,513]{2,1,0:T(8,128)} async-done(((f32[16,128,513]{2,1,0:T(8,128)}), f32[16,16,513]{2,1,0:T(8,128)}) %reduce-scatter.2.cloned.1.call-update) | async-done | bytes 525328 | tf_op jit(solution)/shard_map/reduce_scatter | solution.py:21
  175.2 1.0 slice_reduce_fusion
  176.2 1.1 fusion.23
  177.4 2.1 fusion.20
  179.5 0.2 broadcast_in_dim.72
  179.7 0.0 copy-start.7
  179.7 35.6 %all_to_all.21 = bf16[32,16,2048]{2,1,0:T(8,128)(2,1)S(1)} all-to-all(bf16[32,16,2048]{2,1,0:T(8,128)(2,1)S(1)} %broadcast_in_dim.72), channel_id=1, replica_groups=mesh['xfer'=32,'head'=8] {'xfer'}, dimensions={0} | all-to-all | bytes 4194304 | tf_op jit(solution)/shard_map/all_to_all | solution.py:11
  215.3 0.8 fusion.21
  216.1 21.8 %all_to_all.22 = f32[8,64,224]{2,1,0:T(8,128)S(1)} all-to-all(f32[8,64,224]{2,1,0:T(8,128)S(1)} %fusion.21), channel_id=1, replica_groups=mesh['xfer'=32,'head'=8] {'head'}, dimensions={0} | all-to-all | bytes 917504 | tf_op jit(solution)/shard_map/all_to_all | solution.py:47
  237.9 0.7 reduce_sum.52
  (25 shorter events, 0.2 us)
Async XLA Ops:
  6.5 5.3 %copy-start = (bf16[32,64,576]{2,1,0:T(8,128)(2,1)S(1)}, bf16[32,64,576]{2,1,0:T(8,128)(2,1)}, u32[]{:S(2)}) copy-start(bf16[32,64,576]{2,1,0:T(8,128)(2,1)} %param.9) | copy-start | bytes 7077892
  6.5 4.7 %copy-start.5 = (s32[256]{0:T(256)S(1)}, s32[256]{0:T(256)}, u32[]{:S(2)}) copy-start(s32[256]{0:T(256)} %param.10) | copy-start | bytes 3076
  6.5 4.7 %copy-start.4 = (s32[256]{0:T(256)S(1)}, s32[256]{0:T(256)}, u32[]{:S(2)}) copy-start(s32[256]{0:T(256)} %param.11) | copy-start | bytes 3076
  6.5 4.7 %copy-start.2 = (s32[256,256]{1,0:T(8,128)S(1)}, s32[256,256]{1,0:T(8,128)}, u32[]{:S(2)}) copy-start(s32[256,256]{1,0:T(8,128)} %param.12) | copy-start | bytes 786436
  6.5 53.8 %all-gather.2.cloned.1.call-start = ((), (), s32[]{:S(2)}) async-start(), calls=%async_computation.5 | async-start | bytes 2949120 | tf_op jit(solution)/shard_map/all_gather | solution.py:121
  17.8 42.6 %all-to-all-start = ((bf16[32,64,576]{2,1,0:T(8,128)(2,1)}), bf16[32,64,576]{2,1,0:T(8,128)(2,1)}, u32[]{:S(2)}, u32[]{:S(2)}) async-start(bf16[32,64,576]{2,1,0:T(8,128)(2,1)} %broadcast_select_fusion), calls=%async_computation | async-start | bytes 5242880 | tf_op jit(solution)/shard_map/all_to_all | solution.py:107
  26.4 148.8 %reduce-scatter.2.cloned.1.call-start = ((), (), s32[]{:S(2)}) async-start(), calls=%async_computation.6 | async-start | bytes 5898240 | tf_op jit(solution)/shard_map/reduce_scatter | solution.py:21
  60.4 12.6 %copy-start.3 = (bf16[16,576]{1,0:T(8,128)(2,1)S(1)}, bf16[16,576]{1,0:T(8,128)(2,1)}, u32[]{:S(2)}) copy-start(bf16[16,576]{1,0:T(8,128)(2,1)} %param.14) | copy-start | bytes 55300
  60.4 12.6 %copy-start.6 = (bf16[16,128,576]{2,0,1:T(8,128)(2,1)S(1)}, bf16[16,128,576]{2,0,1:T(8,128)(2,1)}, u32[]{:S(2)}) copy-start(bf16[16,128,576]{2,0,1:T(8,128)(2,1)} %all-gather.2.cloned.1.call-done) | copy-start | bytes 7077892
  89.1 10.7 %copy-start.1 = (f32[16,128,2048]{2,1,0:T(8,128)S(1)}, f32[16,128,2048]{2,1,0:T(8,128)}, u32[]{:S(2)}) copy-start(f32[16,128,2048]{2,1,0:T(8,128)} %get-tuple-element.6) | copy-start | bytes 50331652
  179.7 35.6 %copy-start.7 = (bf16[2048,224]{0,1:T(8,128)(2,1)S(1)}, bf16[2048,224]{0,1:T(8,128)(2,1)}, u32[]{:S(2)}) copy-start(bf16[2048,224]{0,1:T(8,128)(2,1)} %param.17) | copy-start | bytes 2752516
Sparse Core Ops, SparseCore 0:
  11.3 43.1 all-gather.1
  115.7 59.4 reduce-scatter.1
where the time goes:
time: 246 us; the launch traced here: 245 us
  waiting for transfers between devices  92.7 us (38%)
  blocking collectives  72.5 us (29%)
  matrix products  27.3 us (11%)
  other arithmetic  21.3 us (9%)
  between operations  13.7 us (6%)
  local copies, waits for them, and re-layouts  9.15 us (4%)
  starting transfers between devices  8.71 us (4%)
    reduce_scatter x1, waiting for transfers between devices, sent_together(): lax.psum_scatter(both, axis, scatter_dimension=dim, tiled=True)  59.7 us
    all_to_all x2, blocking collectives, copy_for_each(): return lax.all_to_all(copies, axis, split_axis=0, concat_axis=0, tiled=True)  50.8 us
    all_to_all x1, waiting for transfers between devices, body(): lax.all_to_all(outgoing, 'xfer', split_axis=0, concat_axis=0, tiled=True)  33 us
    all_to_all x1, blocking collectives, sum_at_owner(): blocks = lax.all_to_all(split_up(array, dim, peers), axis, 0, 0, tiled=True)  21.8 us
    dot_general x1, matrix products, score_parts(): jnp.einsum('rhc,kc->rhk', qfull, key_rows, preferred_element_type=jnp.flo...  12.6 us
    reduce_sum x2, other arithmetic, weighted_sums(): total = jnp.sum(cached_w, axis=-1) + jnp.sum(recent_w, axis=-1)  9.07 us
    all_to_all x1, starting transfers between devices, body(): lax.all_to_all(outgoing, 'xfer', split_axis=0, concat_axis=0, tiled=True)  8.64 us
    dot_general x1, matrix products, weighted_sums(): jnp.einsum('rhk,kc->rhc', cached_w.astype(jnp.bfloat16), key_rows[:, :lat...  6.22 us
  transfers between devices with their start and end apart: 3, of which 2 were waited for; matrix products, arithmetic and copies ran while one was open for 3% of the time, Pallas kernels for 0%

commit v1 on v0

v1 whole, which is shorter than its diff:
```python
import functools

import jax
import jax.numpy as jnp
from jax import lax
from jax.experimental import pallas as pl
from jax.experimental.pallas import tpu as pltpu
from jax.sharding import PartitionSpec as P

MESH = pl.DeviceIdType.MESH
STEPS = 2
LOW = -1e30
BLOCK = 256
MIB = 1024 * 1024


def pick_kernel(chosen, pool, out, sems):
    def begin(o, c):
        pltpu.make_async_copy(pool.at[chosen[o]], out.at[o], sems.at[o]).start()
        return c

    def end(o, c):
        pltpu.make_async_copy(pool.at[chosen[o]], out.at[o], sems.at[o]).wait()
        return c

    lax.fori_loop(0, out.shape[0], begin, 0)
    lax.fori_loop(0, out.shape[0], end, 0)


def pick_pages(chosen, pool):
    n = chosen.shape[0]
    return pl.pallas_call(
        pick_kernel,
        grid_spec=pltpu.PrefetchScalarGridSpec(
            num_scalar_prefetch=1,
            grid=(),
            in_specs=[pl.BlockSpec(memory_space=pl.ANY)],
            out_specs=pl.BlockSpec(memory_space=pl.ANY),
            scratch_shapes=[pltpu.SemaphoreType.DMA((n,))],
        ),
        out_shape=jax.ShapeDtypeStruct((n, *pool.shape[1:]), pool.dtype),
    )(chosen, pool)


def attend_kernel(scale, page, lengths, starts, place, q, keys, acc, stats, m_s, l_s):
    member = place[0]
    requests = lengths.shape[0]
    rows = q.shape[1] // requests
    many = q.shape[0] * rows
    latent = q.shape[2]
    rank = acc.shape[2]
    lane = lax.broadcasted_iota(jnp.int32, (1, BLOCK), 1)
    odd = lax.broadcasted_iota(jnp.int32, (many, 128), 1) % 2
    per_block = BLOCK // page
    blocks = keys.shape[0] // BLOCK
    for r in range(requests):
        length, start = lengths[r], starts[r]
        pages = (length + page - 1) // page
        skip = (member - start) & 7
        slot = ((start + skip) & 255) >> 3
        count = jnp.maximum(pages - skip + 7, 0) >> 3
        first = slot // per_block
        n = jnp.minimum((slot % per_block + count + per_block - 1) // per_block, blocks)
        n = jnp.where(count > 0, n, 0)
        part = slice(r * rows, (r + 1) * rows)
        acc[:, part, :] = jnp.zeros((q.shape[0], rows, rank), jnp.float32)
        m_s[...] = jnp.full(m_s.shape, LOW, jnp.float32)
        l_s[...] = jnp.zeros(l_s.shape, jnp.float32)

        def step(i, c):
            b = (first + i) & (blocks - 1)
            k = keys[pl.ds(pl.multiple_of(b * BLOCK, BLOCK), BLOCK), :]
            mine = q[:, part, :].reshape(many, latent)
            s = (
                lax.dot_general(
                    mine, k, (((1,), (1,)), ((), ())), preferred_element_type=jnp.float32
                )
                * scale
            )
            at = ((b * per_block + lane // page) * 8 + member - start) & 255
            s = jnp.where(at * page + lane % page < length, s, LOW)
            m_old = m_s[:, :1]
            m_new = jnp.maximum(m_old, jnp.max(s, axis=1, keepdims=True))
            keep = jnp.exp(m_old - m_new)
            w = jnp.exp(s - m_new)
            l_s[...] = l_s[...] * keep + jnp.sum(w, axis=1, keepdims=True)
            m_s[...] = jnp.broadcast_to(m_new, m_s.shape)
            more = jnp.dot(
                w.astype(jnp.bfloat16), k[:, :rank], preferred_element_type=jnp.float32
            )
            old = acc[:, part, :].reshape(many, rank)
            acc[:, part, :] = (old * keep + more).reshape(q.shape[0], rows, rank)
            return c

        lax.fori_loop(0, n, step, 0)
        both = jnp.where(odd == 0, m_s[...], l_s[...])
        stats[:, part, :] = both.reshape(q.shape[0], rows, 128)


def attend(lengths, starts, place, q, keys, page, rank, scale):
    smem = pl.BlockSpec(memory_space=pltpu.SMEM)
    vmem = pl.BlockSpec(memory_space=pltpu.VMEM)
    many = q.shape[0] * q.shape[1] // lengths.shape[0]
    return pl.pallas_call(
        functools.partial(attend_kernel, scale, page),
        in_specs=[smem, smem, smem, vmem, vmem],
        out_specs=[vmem, vmem],
        out_shape=[
            jax.ShapeDtypeStruct((*q.shape[:2], rank), jnp.float32),
            jax.ShapeDtypeStruct((*q.shape[:2], 128), jnp.float32),
        ],
        scratch_shapes=[pltpu.VMEM((many, 128), jnp.float32)] * 2,
        compiler_params=pltpu.CompilerParams(vmem_limit_bytes=40 * MIB),
    )(lengths, starts, place, q, keys)


def combine(m_a, l_a, acc_a, m_b, l_b, acc_b):
    m = jnp.maximum(m_a, m_b)
    f_a, f_b = jnp.exp(m_a - m), jnp.exp(m_b - m)
    return m, l_a * f_a + l_b * f_b, acc_a * f_a + acc_b * f_b


def finish_kernel(
    scale, acc, stats, q_own, fresh, value_up, out_proj, out,
    sent, sent_st, got, got_st, own, own_st, held, share, parts, z_send, z_recv, x_send, x_recv, o_send, o_recv,
):
    z = lax.axis_index("head")
    xfer = lax.axis_index("xfer")
    x, y, core = xfer // 8, (xfer // 2) % 4, xfer % 2
    groups = 8
    rank = acc.shape[2]
    half_rows = acc.shape[1]

    def near(dx, dy, flip):
        c = 1 - core if flip else core
        return ((lax.rem(x + dx, 4) * 4 + lax.rem(y + dy, 4)) * 2 + c, z)

    def along(k):
        return (xfer, lax.rem(z + k, groups))

    barrier = pltpu.get_barrier_semaphore()
    peers = [along(k) for k in range(1, 8)]
    peers += [near(k, 0, False) for k in range(1, 4)] + [near(0, k, False) for k in range(1, 4)]
    peers += [near(0, 0, True)]
    for peer in peers:
        pl.semaphore_signal(barrier, inc=1, device_id=peer, device_id_type=MESH)
    pl.semaphore_wait(barrier, len(peers))

    def z_copies(way, half, hop):
        to = along(1 if way == 0 else 7)
        return [
            pltpu.make_async_remote_copy(
                src_ref=src.at[way, half, hop],
                dst_ref=dst.at[way, half, hop],
                send_sem=z_send.at[way, half, hop, i],
                recv_sem=z_recv.at[way, half, hop, i],
                device_id=to,
                device_id_type=MESH,
            )
            for i, (src, dst) in enumerate(((sent, got), (sent_st, got_st)))
        ]

    def index_of(way, half, distance):
        d = lax.rem(z + distance if way == 0 else z + groups - distance, groups)
        return d * 2 + half

    odd = lax.broadcasted_iota(jnp.int32, (half_rows, 128), 1) % 2

    def arrived(way, half, hop):
        for c in z_copies(way, half, hop):
            c.wait_recv()
        st = jnp.tile(got_st[way, half, hop], (half_rows // 8, 1)).T
        return st[:, 0:1], st[:, 1:2], got[way, half, hop].astype(jnp.float32)

    started = []

    def send_on(way, half, hop):
        at = index_of(way, half, 4 - hop)
        mine = stats[at]
        if hop == (0 if way == half else 1):
            sent[way, half, hop] = acc[at].astype(jnp.bfloat16)
            sent_st[way, half, hop] = mine.T[0:8]
        else:
            m, l, total = combine(*arrived(way, half, hop - 1), mine[:, 0:1], mine[:, 1:2], acc[at])
            sent[way, half, hop] = total.astype(jnp.bfloat16)
            sent_st[way, half, hop] = jnp.where(odd == 0, m, l).T[0:8]
        for c in z_copies(way, half, hop):
            c.start()
            started.append(c)

    def take_fresh(half):
        rows = slice(half * half_rows, (half + 1) * half_rows)
        s = (
            lax.dot_general(
                q_own[rows, :], fresh[...], (((1,), (1,)), ((), ())), preferred_element_type=jnp.float32
            )
            * scale
        )
        row = lax.broadcasted_iota(jnp.int32, s.shape, 0) // 8
        col = lax.broadcasted_iota(jnp.int32, s.shape, 1)
        s = jnp.where((row // STEPS == col // STEPS) & (col <= row), s, LOW)
        m = jnp.max(s, axis=1, keepdims=True)
        w = jnp.exp(s - m)
        l = jnp.sum(w, axis=1, keepdims=True)
        more = jnp.dot(w.astype(jnp.bfloat16), fresh[:, :rank], preferred_element_type=jnp.float32)
        at = z * 2 + half
        mine = stats[at]
        m, l, total = combine(m, l, more, mine[:, 0:1], mine[:, 1:2], acc[at])
        own[half] = total
        own_st[half] = jnp.where(odd == 0, m, l)

    send_on(0, 0, 0)
    send_on(1, 1, 0)
    send_on(0, 1, 1)
    send_on(1, 0, 1)
    take_fresh(0)
    take_fresh(1)
    for hop in (1, 2, 3):
        send_on(0, 0, hop)
        send_on(1, 1, hop)
        if hop < 3:
            send_on(0, 1, hop + 1)
            send_on(1, 0, hop + 1)

    def spread(half, kind, a, b, block, to):
        return pltpu.make_async_remote_copy(
            src_ref=held.at[half, block],
            dst_ref=held.at[half, block],
            send_sem=x_send.at[half, kind, a, b],
            recv_sem=x_recv.at[half, kind, a, b],
            device_id=to,
            device_id_type=MESH,
        )

    def block_of(half, a, b):
        dx, dy = (a, b) if half == 0 else (b, a)
        return (lax.rem(x + 4 - dx, 4) * 4 + lax.rem(y + 4 - dy, 4)) * 2

    def to_first(half, k):
        return near(k, 0, False) if half == 0 else near(0, k, False)

    def to_second(half, k):
        return near(0, k, False) if half == 0 else near(k, 0, False)

    def start(copy):
        copy.start()
        started.append(copy)

    def pass_second(half, a):
        for k in range(1, 4):
            start(spread(half, 1, a, k, block_of(half, a, 0) + core, to_second(half, k)))

    def pass_core(half, a, b):
        start(spread(half, 2, a, b, block_of(half, a, b) + core, near(0, 0, True)))

    for half in (1, 0):
        m, l, total = own_st[half][:, 0:1], own_st[half][:, 1:2], own[half]
        for way in (0, 1):
            m, l, total = combine(m, l, total, *arrived(way, half, 3))
        latent = (total / l).astype(jnp.bfloat16)
        heads = half_rows // fresh.shape[0]
        for h in range(heads):
            full = jnp.dot(latent, value_up[half * heads + h], preferred_element_type=jnp.float32)
            picked = full.reshape(fresh.shape[0], heads, -1)[:, h, :]
            width = picked.shape[1]
            held[half, xfer, :, h * width : (h + 1) * width] = picked.astype(jnp.bfloat16)
        for k in range(1, 4):
            start(spread(half, 0, 0, k, xfer, to_first(half, k)))
        pass_second(half, 0)
        pass_core(half, 0, 0)
    for a in range(1, 4):
        for half in (1, 0):
            spread(half, 0, 0, a, xfer, near(0, 0, True)).wait_recv()
            pass_second(half, a)
            pass_core(half, a, 0)
    for a in range(4):
        for b in range(1, 4):
            for half in (1, 0):
                spread(half, 1, a, b, xfer, near(0, 0, True)).wait_recv()
                pass_core(half, a, b)
    for half in (1, 0):
        for a in range(4):
            for b in range(4):
                spread(half, 2, a, b, xfer, near(0, 0, True)).wait_recv()

    rows = out.shape[0]
    depth = held.shape[3]
    total = None
    for half in (0, 1):
        left = held[half].reshape(-1, depth)
        right = out_proj[half * depth : (half + 1) * depth, :]
        piece = jnp.dot(left, right, preferred_element_type=jnp.float32)
        total = piece if total is None else total + piece
    parts[...] = total.reshape(parts.shape)

    def final(k):
        return pltpu.make_async_remote_copy(
            src_ref=share.at[0, k],
            dst_ref=share.at[1, k],
            send_sem=o_send.at[k],
            recv_sem=o_recv.at[k],
            device_id=along(k),
            device_id_type=MESH,
        )

    for k in (4, 3, 5, 2, 6, 1, 7):
        share[0, k] = parts[lax.rem(z + k, groups)].astype(jnp.bfloat16)
        start(final(k))
    done = parts[z]
    for k in (1, 7, 2, 6, 3, 5, 4):
        final(k).wait_recv()
        done += share[1, k].astype(jnp.float32)
    out[...] = done.astype(jnp.bfloat16)
    for c in started:
        c.wait_send()


def finish(acc, stats, q_own, fresh, value_up, out_proj, owners, groups, scale):
    vmem = pl.BlockSpec(memory_space=pltpu.VMEM)
    rows = fresh.shape[0]
    half_rows, rank = acc.shape[1:]
    depth, width = out_proj.shape
    piece = owners * rows // groups
    dma = pltpu.SemaphoreType.DMA
    return pl.pallas_call(
        functools.partial(finish_kernel, scale),
        in_specs=[vmem] * 6,
        out_specs=vmem,
        out_shape=jax.ShapeDtypeStruct((piece, width), jnp.bfloat16),
        scratch_shapes=[
            pltpu.VMEM((2, 2, 4, half_rows, rank), jnp.bfloat16),
            pltpu.VMEM((2, 2, 4, 8, 128), jnp.float32),
            pltpu.VMEM((2, 2, 4, half_rows, rank), jnp.bfloat16),
            pltpu.VMEM((2, 2, 4, 8, 128), jnp.float32),
            pltpu.VMEM((2, half_rows, rank), jnp.float32),
            pltpu.VMEM((2, half_rows, 128), jnp.float32),
            pltpu.VMEM((2, owners, rows, depth // 2), jnp.bfloat16),
            pltpu.VMEM((2, groups, piece, width), jnp.bfloat16),
            pltpu.VMEM((groups, piece, width), jnp.float32),
            dma((2, 2, 4, 2)),
            dma((2, 2, 4, 2)),
            dma((2, 3, 4, 4)),
            dma((2, 3, 4, 4)),
            dma((groups,)),
            dma((groups,)),
        ],
        compiler_params=pltpu.CompilerParams(
            collective_id=1, has_side_effects=True, vmem_limit_bytes=48 * MIB
        ),
    )(acc, stats, q_own, fresh, value_up, out_proj)


def body(
    kv_pool, lengths, start_device, page_table, queries, new_latent, key_up, value_up, out_proj
):
    owners = lax.axis_size("xfer")
    groups = lax.axis_size("head")
    devices = owners * groups
    owner_idx = lax.axis_index("xfer")
    member = lax.axis_index("head")
    local_device = owner_idx * groups + member
    page_len = kv_pool.shape[1]
    latent = kv_pool.shape[2]
    lat_rank = value_up.shape[1]
    nope = key_up.shape[1]
    per_owner = lengths.shape[0] // owners
    table_width = page_table.shape[1]
    row_count, heads = queries.shape[:2]
    score_scale = queries.shape[2] ** (-0.5)
    page_counts = (lengths + page_len - 1) // page_len
    column = jnp.arange(table_width, dtype=jnp.int32)
    located = ((start_device[:, None] + column[None, :]) % devices == local_device) & (
        column[None, :] < page_counts[:, None]
    )
    chosen = (
        jnp.sum(jnp.where(located, page_table, 0), axis=1).reshape(owners, per_owner).sum(axis=1)
    )
    outgoing = pick_pages(chosen, kv_pool)
    arrived = lax.all_to_all(outgoing, "xfer", split_axis=0, concat_axis=0, tiled=True)
    first_req = owner_idx * per_owner
    my_lengths = lax.dynamic_slice_in_dim(lengths, first_req, per_owner, 0)
    my_starts = lax.dynamic_slice_in_dim(start_device, first_req, per_owner, 0)
    absorbed = jnp.einsum(
        "rhn,hnc->rhc", queries[:, :, :nope], key_up, preferred_element_type=jnp.float32
    ).astype(jnp.bfloat16)
    qfull = jnp.concatenate([absorbed, queries[:, :, nope:]], axis=-1)
    qfull = qfull.reshape(row_count, 2, heads // 2, latent).transpose(1, 0, 2, 3)
    q_own = qfull.reshape(row_count * heads, latent)
    every = lax.all_gather(q_own, "head", axis=0, tiled=True)
    every = every.reshape(groups * 2, row_count * heads // 2, latent)
    acc, stats = attend(
        my_lengths, my_starts, member.reshape(1), every, arrived.reshape(-1, latent),
        page_len, lat_rank, score_scale,
    )
    return finish(acc, stats, q_own, new_latent, value_up, out_proj, owners, groups, score_scale)


def solution(mesh):
    in_specs = (
        P(("xfer", "head"), None, None),
        P(),
        P(),
        P(),
        P("xfer", "head", None),
        P("xfer", None),
        P("head", None, None),
        P("head", None, None),
        P("head", "xfer"),
    )
    out_specs = P("head", "xfer")
    return jax.shard_map(body, mesh=mesh, in_specs=in_specs, out_specs=out_specs, check_vma=False)
```

time: 246 us -> 215 us (0.87)
  Pallas kernels: 0 us -> 150 us
  blocking collectives: 72.5 us -> 0 us
  waiting for transfers between devices: 92.7 us -> 32.4 us
  matrix products: 27.3 us -> 0.37 us
  other arithmetic: 21.3 us -> 1.08 us
    pallas_call x0 -> x3, Pallas kernels: none -> 150 us  [the longest x1 81.5 us: pick_pages(): pl.pallas_call(pick_kernel, grid_spec=pltpu.PrefetchScalarGridSpec(num_sc...]
    all_to_all x3 -> x0, blocking collectives: 72.5 us -> none  [the longest x2 50.8 us: copy_for_each(): return lax.all_to_all(copies, axis, split_axis=0, concat_axis=0, tiled=True)]
    reduce_scatter x1 -> x0, waiting for transfers between devices: 59.7 us -> none  [sent_together(): lax.psum_scatter(both, axis, scatter_dimension=dim, tiled=True)]
    dot_general x6 -> x0, matrix products: 25.3 us -> none  [the longest x1 12.6 us: score_parts(): jnp.einsum('rhc,kc->rhk', qfull, key_rows, preferred_element_type=jnp.flo...]
    reduce_sum x3 -> x0, other arithmetic: 9.72 us -> none  [the longest x2 9.07 us: weighted_sums(): total = jnp.sum(cached_w, axis=-1) + jnp.sum(recent_w, axis=-1)]
    concatenate x1 -> x0, other arithmetic: 5.38 us -> none  [sent_together(): both = jnp.concatenate(columns, axis=along)]
    unnamed x17 -> x21, local copies, waits for them, and re-layouts: 1.68 us -> 5.8 us
    select_n x3 -> x0, other arithmetic: 3.59 us -> none  [the longest x2 3.59 us: body(): outgoing = jnp.take(kv_pool, chosen, axis=0)]
  transfers between devices with their start and end apart: 3 -> 2, of which waited for: 2 -> 1; matrix products, arithmetic and copies ran while one was open for 3% -> 1% of each run, Pallas kernels for 0% -> 38%
where the time goes in v1:
time: 215 us
  Pallas kernels  150 us (70%)
  waiting for transfers between devices  32.4 us (15%)
  between operations  13.5 us (6%)
  starting transfers between devices  8.68 us (4%)
  local copies, waits for them, and re-layouts  8.66 us (4%)
    pallas_call x1, Pallas kernels, pick_pages(): pl.pallas_call(pick_kernel, grid_spec=pltpu.PrefetchScalarGridSpec(num_sc...  81.5 us
    pallas_call x1, Pallas kernels, finish(): pl.pallas_call(functools.partial(finish_kernel, scale), in_specs=[vmem] *...  56.1 us
    all_to_all x1, waiting for transfers between devices, body(): lax.all_to_all(outgoing, 'xfer', split_axis=0, concat_axis=0, tiled=True)  32.3 us
    pallas_call x1, Pallas kernels, attend(): pl.pallas_call(functools.partial(attend_kernel, scale, page), in_specs=[s...  12.4 us
    all_to_all x1, starting transfers between devices, body(): lax.all_to_all(outgoing, 'xfer', split_axis=0, concat_axis=0, tiled=True)  8.65 us
    unnamed x21, local copies, waits for them, and re-layouts  5.8 us
  transfers between devices with their start and end apart: 2, of which 1 were waited for; matrix products, arithmetic and copies ran while one was open for 1% of the time, Pallas kernels for 38%

profile of v1, /device:TPU:1, one launch (start us, length us, event | category | flops | bytes accessed | tf_op | source)
XLA Modules:
  0.0 214.6 jit_solution(16320061598674195178)
XLA Ops:
  6.5 0.0 copy-start
  6.5 0.0 copy-start.8
  6.5 0.0 copy-start.7
  6.5 0.0 copy-start.6
  6.5 0.0 all-gather.2.cloned.1.call-start
  6.6 1.0 slice.6
  7.6 0.8 slice.7
  8.4 0.0 copy-done
  8.5 0.4 fusion
  8.9 0.8 copy.16
  9.7 0.0 all-gather.2.cloned.1.call-update
  9.7 0.0 copy-done.8
  9.7 0.0 copy-done.7
  9.7 0.0 copy-done.6
  9.8 0.3 select_reduce_fusion
  10.1 0.1 reshape.24
  10.1 0.7 reduce_sum.19.chosen
  10.9 81.5 %shard_map.91 = bf16[32,64,576]{2,1,0:T(8,128)(2,1)} custom-call(s32[32]{0:T(128)} %reduce_sum.19.chosen, bf16[32,64,576]{2,1,0:T(8,128)(2,1)} %pool.1), custom_call_target="tpu_custom_call" | custom-call | tf_op jit(solution)/shard_map/pallas_call | solution.py:32
  92.3 8.6 %all-to-all-start = ((bf16[32,64,576]{2,1,0:T(8,128)(2,1)}), bf16[32,64,576]{2,1,0:T(8,128)(2,1)}, u32[]{:S(2)}, u32[]{:S(2)}) async-start(bf16[32,64,576]{2,1,0:T(8,128)(2,1)} %shard_map.91), calls=%async_computation | async-start | bytes 5242880 | tf_op jit(solution)/shard_map/all_to_all | solution.py:379
  101.0 0.1 dynamic_slice.6.lengths
  101.1 0.1 dynamic_slice.7.starts
  101.1 1.5 copy.17.out_proj
  102.6 32.3 %all-to-all-done = bf16[32,64,576]{2,1,0:T(8,128)(2,1)} async-done(((bf16[32,64,576]{2,1,0:T(8,128)(2,1)}), bf16[32,64,576]{2,1,0:T(8,128)(2,1)}, u32[]{:S(2)}, u32[]{:S(2)}) %all-to-all-start) | async-done | bytes 2359328 | tf_op jit(solution)/shard_map/all_to_all | solution.py:379
  134.9 0.0 all-gather.2.cloned.1.call-done
  134.9 0.0 copy-start.3
  134.9 1.7 copy-done.3
  136.7 0.0 copy-start.2
  136.7 0.0 copy-start.4
  136.7 0.0 copy-start.5
  136.7 12.4 %shard_map.92 = (f32[16,128,512]{2,1,0:T(8,128)S(1)}, f32[16,128,128]{2,1,0:T(8,128)S(1)}) custom-call(s32[8]{0:T(128)S(1)} %dynamic_slice.6.lengths, s32[8]{0:T(128)S(1)} %dynamic_slice.7.starts, s32[1]{0:T(128)} %bitcast.place, bf16[16,128,576]{2,1,0:T(8,128)(2,1)S(1)} %bitcast.12, bf16[2048,576]{1,0:T(8,128)(2,1)} %bitcast.6.keys), custom_call_target="tpu_custom_call" | custom-call | tf_op jit(solution)/shard_map/pallas_call | solution.py:104
  149.1 0.0 copy-start.1
  149.1 1.9 copy-done.1
  151.0 0.0 copy-done.2
  151.0 0.0 copy-done.4
  151.0 0.0 copy-done.5
  151.0 56.1 %shard_map.93 = bf16[64,224]{1,0:T(8,128)(2,1)S(1)} custom-call(f32[16,128,512]{2,1,0:T(8,128)} %copy-done.1, f32[16,128,128]{2,1,0:T(8,128)S(1)} %get-tuple-element.8.stats, bf16[256,576]{1,0:T(8,128)(2,1)S(1)} %bitcast.11, bf16[16,576]{1,0:T(8,128)(2,1)S(1)} %copy-done.5, bf16[16,512,128]{2,1,0:T(8,128)(2,1)S(1)} %copy-done.4, ...), custom_call_target="tpu_custom_call" | custom-call | tf_op jit(solution)/shard_map/pallas_call | solution.py:325
  207.1 0.6 copy.23
  (3 shorter events, 0.1 us)
Async XLA Ops:
  6.5 1.9 copy-start
  6.5 3.2 %copy-start.8 = (s32[256]{0:T(256)S(1)}, s32[256]{0:T(256)}, u32[]{:S(2)}) copy-start(s32[256]{0:T(256)} %param.10) | copy-start | bytes 3076
  6.5 3.2 %copy-start.7 = (s32[256]{0:T(256)S(1)}, s32[256]{0:T(256)}, u32[]{:S(2)}) copy-start(s32[256]{0:T(256)} %param.11) | copy-start | bytes 3076
  6.5 3.2 %copy-start.6 = (s32[256,256]{1,0:T(8,128)S(1)}, s32[256,256]{1,0:T(8,128)}, u32[]{:S(2)}) copy-start(s32[256,256]{1,0:T(8,128)} %param.12) | copy-start | bytes 786436
  6.5 128.4 %all-gather.2.cloned.1.call-start = ((), (), s32[]{:S(2)}) async-start(), calls=%async_computation.1 | async-start | bytes 2949120 | tf_op jit(solution)/shard_map/all_gather | solution.py:389
  92.3 42.6 %all-to-all-start = ((bf16[32,64,576]{2,1,0:T(8,128)(2,1)}), bf16[32,64,576]{2,1,0:T(8,128)(2,1)}, u32[]{:S(2)}, u32[]{:S(2)}) async-start(bf16[32,64,576]{2,1,0:T(8,128)(2,1)} %shard_map.91), calls=%async_computation | async-start | bytes 5242880 | tf_op jit(solution)/shard_map/all_to_all | solution.py:379
  134.9 1.7 copy-start.3
  136.7 14.4 %copy-start.2 = (bf16[16,2,8,576]{3,2,0,1:T(8,128)(2,1)S(1)}, bf16[16,2,8,576]{3,2,0,1:T(8,128)(2,1)}, u32[]{:S(2)}) copy-start(bf16[16,2,8,576]{3,2,0,1:T(8,128)(2,1)} %copy.16) | copy-start | bytes 884740
  136.7 14.4 %copy-start.4 = (bf16[16,512,128]{2,1,0:T(8,128)(2,1)S(1)}, bf16[16,512,128]{2,1,0:T(8,128)(2,1)}, u32[]{:S(2)}) copy-start(bf16[16,512,128]{2,1,0:T(8,128)(2,1)} %value_up.1) | copy-start | bytes 6291460
  136.7 14.4 %copy-start.5 = (bf16[16,576]{1,0:T(8,128)(2,1)S(1)}, bf16[16,576]{1,0:T(8,128)(2,1)}, u32[]{:S(2)}) copy-start(bf16[16,576]{1,0:T(8,128)(2,1)} %fresh.1) | copy-start | bytes 55300
  149.1 1.9 copy-start.1
Sparse Core Ops, SparseCore 0:
  9.8 92.3 all-gather.1

commit v2 on v1

--- a/solution.py
+++ b/solution.py
@@ -35,10 +35,11 @@
             num_scalar_prefetch=1,
             grid=(),
             in_specs=[pl.BlockSpec(memory_space=pl.ANY)],
-            out_specs=pl.BlockSpec(memory_space=pl.ANY),
+            out_specs=pl.BlockSpec(memory_space=pltpu.VMEM),
             scratch_shapes=[pltpu.SemaphoreType.DMA((n,))],
         ),
         out_shape=jax.ShapeDtypeStruct((n, *pool.shape[1:]), pool.dtype),
+        compiler_params=pltpu.CompilerParams(vmem_limit_bytes=16 * MIB),
     )(chosen, pool)
 
 

time: 215 us -> 141 us (0.66)
  Pallas kernels: 150 us -> 73.2 us
  local copies, waits for them, and re-layouts: 8.66 us -> 11.9 us
    pallas_call x1, Pallas kernels: 81.5 us -> 4.69 us  [pick_pages(): pl.pallas_call(pick_kernel, grid_spec=pltpu.PrefetchScalarGridSpec(num_sc...]
    unnamed x21 -> x25, local copies, waits for them, and re-layouts: 5.8 us -> 9.02 us
  transfers between devices with their start and end apart: 2 -> 2, of which waited for: 1 -> 1; matrix products, arithmetic and copies ran while one was open for 1% -> 2% of each run, Pallas kernels for 38% -> 3%
where the time goes in v2:
time: 141 us
  Pallas kernels  73.2 us (52%)
  waiting for transfers between devices  32.4 us (23%)
  between operations  13.5 us (10%)
  local copies, waits for them, and re-layouts  11.9 us (8%)
  starting transfers between devices  8.67 us (6%)
    pallas_call x1, Pallas kernels, finish(): pl.pallas_call(functools.partial(finish_kernel, scale), in_specs=[vmem] *...  56.9 us
    all_to_all x1, waiting for transfers between devices, body(): lax.all_to_all(outgoing, 'xfer', split_axis=0, concat_axis=0, tiled=True)  32.3 us
    pallas_call x1, Pallas kernels, attend(): pl.pallas_call(functools.partial(attend_kernel, scale, page), in_specs=[s...  11.6 us
    unnamed x25, local copies, waits for them, and re-layouts  9.02 us
    all_to_all x1, starting transfers between devices, body(): lax.all_to_all(outgoing, 'xfer', split_axis=0, concat_axis=0, tiled=True)  8.64 us
    pallas_call x1, Pallas kernels, pick_pages(): pl.pallas_call(pick_kernel, grid_spec=pltpu.PrefetchScalarGridSpec(num_sc...  4.69 us
  transfers between devices with their start and end apart: 2, of which 1 were waited for; matrix products, arithmetic and copies ran while one was open for 2% of the time, Pallas kernels for 3%

profile of v2, /device:TPU:1, one launch (start us, length us, event | category | flops | bytes accessed | tf_op | source)
XLA Modules:
  0.0 140.5 jit_solution(17545957914749491334)
XLA Ops:
  6.5 0.0 copy-start
  6.5 0.0 copy-start.10
  6.5 0.0 copy-start.9
  6.5 0.0 copy-start.8
  6.5 0.0 all-gather.2.cloned.1.call-start
  6.6 1.0 slice.6
  7.6 0.8 slice.7
  8.4 0.0 copy-done
  8.5 0.4 fusion
  8.9 0.8 copy.16
  9.7 0.0 all-gather.2.cloned.1.call-update
  9.7 0.0 copy-done.10
  9.7 0.0 copy-done.9
  9.8 0.0 copy-done.8
  9.8 0.3 select_reduce_fusion
  10.1 0.1 reshape.24
  10.1 0.1 reduce_sum.19.chosen
  10.3 0.0 copy-start.5
  10.3 1.7 %copy-done.5 = bf16[32,64,576]{2,1,0:T(8,128)(2,1)S(1)} copy-done((bf16[32,64,576]{2,1,0:T(8,128)(2,1)S(1)}, bf16[32,64,576]{2,1,0:T(8,128)(2,1)}, u32[]{:S(2)}) %copy-start.5) | copy-done | bytes 2359320
  12.0 4.7 %shard_map.91 = bf16[32,64,576]{2,1,0:T(8,128)(2,1)S(1)} custom-call(s32[32]{0:T(128)S(1)} %reduce_sum.19.chosen, bf16[32,64,576]{2,1,0:T(8,128)(2,1)S(1)} %copy-done.5), custom_call_target="tpu_custom_call" | custom-call | tf_op jit(solution)/shard_map/pallas_call | solution.py:32
  16.7 0.0 copy-start.1
  16.7 1.5 %copy-done.1 = bf16[32,64,576]{2,1,0:T(8,128)(2,1)} copy-done((bf16[32,64,576]{2,1,0:T(8,128)(2,1)}, bf16[32,64,576]{2,1,0:T(8,128)(2,1)S(1)}, u32[]{:S(2)}) %copy-start.1) | copy-done | bytes 2359320
  18.2 8.6 %all-to-all-start = ((bf16[32,64,576]{2,1,0:T(8,128)(2,1)}), bf16[32,64,576]{2,1,0:T(8,128)(2,1)}, u32[]{:S(2)}, u32[]{:S(2)}) async-start(bf16[32,64,576]{2,1,0:T(8,128)(2,1)} %copy-done.1), calls=%async_computation | async-start | bytes 5242880 | tf_op jit(solution)/shard_map/all_to_all | solution.py:380
  26.9 0.1 dynamic_slice.6.lengths
  26.9 0.1 dynamic_slice.7.starts
  27.0 1.5 %copy.17.out_proj = bf16[2048,224]{1,0:T(8,128)(2,1)S(1)} copy(bf16[2048,224]{0,1:T(8,128)(2,1)} %param.17) | data formatting | bytes 1835008 | tf_op args[8]
  28.5 32.3 %all-to-all-done = bf16[32,64,576]{2,1,0:T(8,128)(2,1)} async-done(((bf16[32,64,576]{2,1,0:T(8,128)(2,1)}), bf16[32,64,576]{2,1,0:T(8,128)(2,1)}, u32[]{:S(2)}, u32[]{:S(2)}) %all-to-all-start) | async-done | bytes 2359328 | tf_op jit(solution)/shard_map/all_to_all | solution.py:380
  60.8 0.0 all-gather.2.cloned.1.call-done
  60.8 0.0 copy-start.4
  60.8 1.7 %copy-done.4 = bf16[2048,576]{1,0:T(8,128)(2,1)S(1)} copy-done((bf16[2048,576]{1,0:T(8,128)(2,1)S(1)}, bf16[2048,576]{1,0:T(8,128)(2,1)}, u32[]{:S(2)}) %copy-start.4) | copy-done | bytes 2359320
  62.5 0.0 copy-start.3
  62.5 0.0 copy-start.6
  62.6 0.0 copy-start.7
  62.6 11.6 %shard_map.92 = (f32[16,128,512]{2,1,0:T(8,128)S(1)}, f32[16,128,128]{2,1,0:T(8,128)S(1)}) custom-call(s32[8]{0:T(128)S(1)} %dynamic_slice.6.lengths, s32[8]{0:T(128)S(1)} %dynamic_slice.7.starts, s32[1]{0:T(128)} %bitcast.place, bf16[16,128,576]{2,1,0:T(8,128)(2,1)S(1)} %bitcast.12, bf16[2048,576]{1,0:T(8,128)(2,1)} %bitcast.6.keys), custom_call_target="tpu_custom_call" | custom-call | tf_op jit(solution)/shard_map/pallas_call | solution.py:105
  74.2 0.0 copy-start.2
  74.2 1.9 %copy-done.2 = f32[16,128,512]{2,1,0:T(8,128)} copy-done((f32[16,128,512]{2,1,0:T(8,128)}, f32[16,128,512]{2,1,0:T(8,128)S(1)}, u32[]{:S(2)}) %copy-start.2) | copy-done | bytes 4194328
  76.1 0.0 copy-done.3
  76.1 0.0 copy-done.6
  76.1 0.0 copy-done.7
  76.1 56.9 %shard_map.93 = bf16[64,224]{1,0:T(8,128)(2,1)S(1)} custom-call(f32[16,128,512]{2,1,0:T(8,128)} %copy-done.2, f32[16,128,128]{2,1,0:T(8,128)S(1)} %get-tuple-element.8.stats, bf16[256,576]{1,0:T(8,128)(2,1)S(1)} %bitcast.11, bf16[16,576]{1,0:T(8,128)(2,1)S(1)} %copy-done.7, bf16[16,512,128]{2,1,0:T(8,128)(2,1)S(1)} %copy-done.6, ...), custom_call_target="tpu_custom_call" | custom-call | tf_op jit(solution)/shard_map/pallas_call | solution.py:326
  133.0 0.6 copy.23
  (3 shorter events, 0.1 us)
Async XLA Ops:
  6.5 1.9 %copy-start = (bf16[16,128,512]{2,1,0:T(8,128)(2,1)S(1)}, bf16[16,128,512]{2,1,0:T(8,128)(2,1)}, u32[]{:S(2)}) copy-start(bf16[16,128,512]{2,1,0:T(8,128)(2,1)} %param.15) | copy-start | bytes 6291460
  6.5 3.2 %copy-start.10 = (s32[256]{0:T(256)S(1)}, s32[256]{0:T(256)}, u32[]{:S(2)}) copy-start(s32[256]{0:T(256)} %param.10) | copy-start | bytes 3076
  6.5 3.2 %copy-start.9 = (s32[256]{0:T(256)S(1)}, s32[256]{0:T(256)}, u32[]{:S(2)}) copy-start(s32[256]{0:T(256)} %param.11) | copy-start | bytes 3076
  6.5 3.2 %copy-start.8 = (s32[256,256]{1,0:T(8,128)S(1)}, s32[256,256]{1,0:T(8,128)}, u32[]{:S(2)}) copy-start(s32[256,256]{1,0:T(8,128)} %param.12) | copy-start | bytes 786436
  6.5 54.3 %all-gather.2.cloned.1.call-start = ((), (), s32[]{:S(2)}) async-start(), calls=%async_computation.1 | async-start | bytes 2949120 | tf_op jit(solution)/shard_map/all_gather | solution.py:390
  10.3 1.8 %copy-start.5 = (bf16[32,64,576]{2,1,0:T(8,128)(2,1)S(1)}, bf16[32,64,576]{2,1,0:T(8,128)(2,1)}, u32[]{:S(2)}) copy-start(bf16[32,64,576]{2,1,0:T(8,128)(2,1)} %pool.1) | copy-start | bytes 7077892
  16.7 1.5 %copy-start.1 = (bf16[32,64,576]{2,1,0:T(8,128)(2,1)}, bf16[32,64,576]{2,1,0:T(8,128)(2,1)S(1)}, u32[]{:S(2)}) copy-start(bf16[32,64,576]{2,1,0:T(8,128)(2,1)S(1)} %shard_map.91) | copy-start | bytes 7077892
  18.2 42.6 %all-to-all-start = ((bf16[32,64,576]{2,1,0:T(8,128)(2,1)}), bf16[32,64,576]{2,1,0:T(8,128)(2,1)}, u32[]{:S(2)}, u32[]{:S(2)}) async-start(bf16[32,64,576]{2,1,0:T(8,128)(2,1)} %copy-done.1), calls=%async_computation | async-start | bytes 5242880 | tf_op jit(solution)/shard_map/all_to_all | solution.py:380
  60.8 1.7 %copy-start.4 = (bf16[2048,576]{1,0:T(8,128)(2,1)S(1)}, bf16[2048,576]{1,0:T(8,128)(2,1)}, u32[]{:S(2)}) copy-start(bf16[2048,576]{1,0:T(8,128)(2,1)} %all-gather.2.cloned.1.call-done) | copy-start | bytes 7077892
  62.5 13.6 %copy-start.3 = (bf16[16,2,8,576]{3,2,0,1:T(8,128)(2,1)S(1)}, bf16[16,2,8,576]{3,2,0,1:T(8,128)(2,1)}, u32[]{:S(2)}) copy-start(bf16[16,2,8,576]{3,2,0,1:T(8,128)(2,1)} %copy.16) | copy-start | bytes 884740
  62.5 13.6 %copy-start.6 = (bf16[16,512,128]{2,1,0:T(8,128)(2,1)S(1)}, bf16[16,512,128]{2,1,0:T(8,128)(2,1)}, u32[]{:S(2)}) copy-start(bf16[16,512,128]{2,1,0:T(8,128)(2,1)} %value_up.1) | copy-start | bytes 6291460
  62.6 13.6 %copy-start.7 = (bf16[16,576]{1,0:T(8,128)(2,1)S(1)}, bf16[16,576]{1,0:T(8,128)(2,1)}, u32[]{:S(2)}) copy-start(bf16[16,576]{1,0:T(8,128)(2,1)} %fresh.1) | copy-start | bytes 55300
  74.2 2.0 %copy-start.2 = (f32[16,128,512]{2,1,0:T(8,128)}, f32[16,128,512]{2,1,0:T(8,128)S(1)}, u32[]{:S(2)}) copy-start(f32[16,128,512]{2,1,0:T(8,128)S(1)} %get-tuple-element.7.acc) | copy-start | bytes 12582916
Sparse Core Ops, SparseCore 0:
  9.8 44.0 all-gather.1

commit v3 on v1

--- a/solution.py
+++ b/solution.py
@@ -14,32 +14,146 @@
 MIB = 1024 * 1024
 
 
-def pick_kernel(chosen, pool, out, sems):
+FAR = ((2, 2), (2, 1), (1, 2), (2, 3), (3, 2), (2, 0), (0, 2), (1, 1), (3, 3), (1, 3), (3, 1), (1, 0), (3, 0), (0, 1), (0, 3))
+OFFSETS = tuple((*d, 0) for d in FAR) + tuple((*d, 1) for d in FAR) + ((0, 0, 1),)
+
+
+def prepare_kernel(chosen, pool, queries, key_up, pages, q_own, sems, nope_s, wide_s):
+    def copy(o):
+        return pltpu.make_async_copy(pool.at[chosen[o]], pages.at[o], sems.at[o])
+
     def begin(o, c):
-        pltpu.make_async_copy(pool.at[chosen[o]], out.at[o], sems.at[o]).start()
+        copy(o).start()
         return c
 
     def end(o, c):
-        pltpu.make_async_copy(pool.at[chosen[o]], out.at[o], sems.at[o]).wait()
+        copy(o).wait()
         return c
 
-    lax.fori_loop(0, out.shape[0], begin, 0)
-    lax.fori_loop(0, out.shape[0], end, 0)
-
-
-def pick_pages(chosen, pool):
+    lax.fori_loop(0, pages.shape[0], begin, 0)
+    rows, heads, width = queries.shape
+    nope, rank = key_up.shape[1:]
+    half = heads // 2
+    flat = queries[...].reshape(rows * heads, width).astype(jnp.float32)
+    nope_s[...] = flat[:, :nope]
+    rope = flat[:, nope:].reshape(rows, 2, half, width - nope)
+    for h in range(heads):
+        mine = nope_s[pl.ds(h, rows, stride=heads), :].astype(jnp.bfloat16)
+        full = jnp.dot(mine, key_up[h], preferred_element_type=jnp.float32)
+        at = pl.ds((h // half) * rows * half + h % half, rows, stride=half)
+        for c in range(rank // 128):
+            wide_s[c, at, :] = full[:, c * 128 : (c + 1) * 128]
+    for c in range(rank // 128):
+        q_own[:, c * 128 : (c + 1) * 128] = wide_s[c].astype(jnp.bfloat16)
+    for i in range(2):
+        part = rope[:, i].reshape(rows * half, width - nope)
+        q_own[i * rows * half : (i + 1) * rows * half, rank:] = part.astype(jnp.bfloat16)
+    lax.fori_loop(0, pages.shape[0], end, 0)
+
+
+def prepare(chosen, pool, queries, key_up):
     n = chosen.shape[0]
+    rows, heads, width = queries.shape
+    nope, rank = key_up.shape[1:]
+    vmem = pl.BlockSpec(memory_space=pltpu.VMEM)
     return pl.pallas_call(
-        pick_kernel,
-        grid_spec=pltpu.PrefetchScalarGridSpec(
-            num_scalar_prefetch=1,
-            grid=(),
-            in_specs=[pl.BlockSpec(memory_space=pl.ANY)],
-            out_specs=pl.BlockSpec(memory_space=pl.ANY),
-            scratch_shapes=[pltpu.SemaphoreType.DMA((n,))],
+        prepare_kernel,
+        in_specs=[pl.BlockSpec(memory_space=pltpu.SMEM), pl.BlockSpec(memory_space=pl.ANY), vmem, vmem],
+        out_specs=[vmem, vmem],
+        out_shape=[
+            jax.ShapeDtypeStruct((n, *pool.shape[1:]), pool.dtype),
+            jax.ShapeDtypeStruct((rows * heads, rank + width - nope), queries.dtype),
+        ],
+        scratch_shapes=[
+            pltpu.SemaphoreType.DMA((n,)),
+            pltpu.VMEM((rows * heads, nope), jnp.float32),
+            pltpu.VMEM((rank // 128, rows * heads, 128), jnp.float32),
+        ],
+        compiler_params=pltpu.CompilerParams(vmem_limit_bytes=56 * MIB),
+    )(chosen, pool, queries, key_up)
+
+
+def exchange_kernel(pages, q_own, keys, q_all, p_send, p_recv, z_send, z_recv, own_sem):
+    z = lax.axis_index("head")
+    xfer = lax.axis_index("xfer")
+    x, y, core = xfer // 8, (xfer // 2) % 4, xfer % 2
+    groups = q_all.shape[0]
+
+    def at(offset):
+        dx, dy, dc = offset
+        return (lax.rem(x + dx, 4) * 4 + lax.rem(y + dy, 4)) * 2 + lax.rem(core + dc, 2)
+
+    right, left = (xfer, lax.rem(z + 1, groups)), (xfer, lax.rem(z + groups - 1, groups))
+    barrier = pltpu.get_barrier_semaphore()
+    peers = [right, left] + [(at(offset), z) for offset in OFFSETS]
+    for peer in peers:
+        pl.semaphore_signal(barrier, inc=1, device_id=peer, device_id_type=MESH)
+    pl.semaphore_wait(barrier, len(peers))
+
+    def hop(way, j):
+        block = lax.rem(z + groups - (j - 1), groups) if way == 0 else lax.rem(z + j - 1, groups)
+        src, dst = (q_own if j == 1 else q_all.at[block]), q_all.at[block]
+        if j == groups // 2:
+            src, dst = src.at[way], dst.at[way]
+        return pltpu.make_async_remote_copy(
+            src_ref=src,
+            dst_ref=dst,
+            send_sem=z_send.at[way, j],
+            recv_sem=z_recv.at[way, j],
+            device_id=right if way == 0 else left,
+            device_id_type=MESH,
+        )
+
+    def page(i, offset):
+        to = at(offset)
+        return pltpu.make_async_remote_copy(
+            src_ref=pages.at[to],
+            dst_ref=keys.at[xfer],
+            send_sem=p_send.at[i],
+            recv_sem=p_recv.at[i],
+            device_id=(to, z),
+            device_id_type=MESH,
+        )
+
+    mine = [
+        pltpu.make_async_copy(q_own, q_all.at[z], own_sem.at[0]),
+        pltpu.make_async_copy(pages.at[xfer], keys.at[xfer], own_sem.at[1]),
+    ]
+    hops = [hop(way, j) for j in range(1, groups // 2 + 1) for way in (0, 1)]
+    copies = [page(i, offset) for i, offset in enumerate(OFFSETS)]
+    for c in hops[:2] + copies + mine:
+        c.start()
+    for j in range(1, groups // 2):
+        for way in (0, 1):
+            hops[(j - 1) * 2 + way].wait_recv()
+            hops[j * 2 + way].start()
+    for c in hops[-2:]:
+        c.wait_recv()
+    for c in copies:
+        c.wait_recv()
+    for c in mine:
+        c.wait()
+    for c in hops + copies:
+        c.wait_send()
+
+
+def exchange(pages, q_own, groups):
+    vmem = pl.BlockSpec(memory_space=pltpu.VMEM)
+    dma = pltpu.SemaphoreType.DMA
+    n = pages.shape[0]
+    return pl.pallas_call(
+        exchange_kernel,
+        in_specs=[vmem, vmem],
+        out_specs=[vmem, vmem],
+        out_shape=[
+            jax.ShapeDtypeStruct(pages.shape, pages.dtype),
+            jax.ShapeDtypeStruct((groups, *q_own.shape), q_own.dtype),
+        ],
+        scratch_shapes=[dma((n,)), dma((n,)), dma((2, 8)), dma((2, 8)), dma((2,))],
+        compiler_params=pltpu.CompilerParams(
+            collective_id=0, has_side_effects=True, vmem_limit_bytes=40 * MIB
         ),
-        out_shape=jax.ShapeDtypeStruct((n, *pool.shape[1:]), pool.dtype),
-    )(chosen, pool)
+    )(pages, q_own)
 
 
 def attend_kernel(scale, page, lengths, starts, place, q, keys, acc, stats, m_s, l_s):
@@ -362,7 +476,6 @@
     page_len = kv_pool.shape[1]
     latent = kv_pool.shape[2]
     lat_rank = value_up.shape[1]
-    nope = key_up.shape[1]
     per_owner = lengths.shape[0] // owners
     table_width = page_table.shape[1]
     row_count, heads = queries.shape[:2]
@@ -375,18 +488,11 @@
     chosen = (
         jnp.sum(jnp.where(located, page_table, 0), axis=1).reshape(owners, per_owner).sum(axis=1)
     )
-    outgoing = pick_pages(chosen, kv_pool)
-    arrived = lax.all_to_all(outgoing, "xfer", split_axis=0, concat_axis=0, tiled=True)
     first_req = owner_idx * per_owner
     my_lengths = lax.dynamic_slice_in_dim(lengths, first_req, per_owner, 0)
     my_starts = lax.dynamic_slice_in_dim(start_device, first_req, per_owner, 0)
-    absorbed = jnp.einsum(
-        "rhn,hnc->rhc", queries[:, :, :nope], key_up, preferred_element_type=jnp.float32
-    ).astype(jnp.bfloat16)
-    qfull = jnp.concatenate([absorbed, queries[:, :, nope:]], axis=-1)
-    qfull = qfull.reshape(row_count, 2, heads // 2, latent).transpose(1, 0, 2, 3)
-    q_own = qfull.reshape(row_count * heads, latent)
-    every = lax.all_gather(q_own, "head", axis=0, tiled=True)
+    pages, q_own = prepare(chosen, kv_pool, queries, key_up)
+    arrived, every = exchange(pages, q_own.reshape(2, row_count * heads // 2, latent), groups)
     every = every.reshape(groups * 2, row_count * heads // 2, latent)
     acc, stats = attend(
         my_lengths, my_starts, member.reshape(1), every, arrived.reshape(-1, latent),

time: 215 us -> 128 us (0.60)
  Pallas kernels: 150 us -> 112 us
  waiting for transfers between devices: 32.4 us -> 0 us
  between operations: 13.5 us -> 0.13 us
  starting transfers between devices: 8.68 us -> 0 us
  local copies, waits for them, and re-layouts: 8.66 us -> 12.9 us
    pallas_call x1 -> x2, Pallas kernels: 81.5 us -> 45.3 us  [the longest x1 39.8 us: exchange(): pl.pallas_call(exchange_kernel, in_specs=[vmem, vmem], out_specs=[vmem, v...]
    all_to_all x1 -> x0, waiting for transfers between devices: 32.3 us -> none  [body(): lax.all_to_all(outgoing, 'xfer', split_axis=0, concat_axis=0, tiled=True)]
    all_to_all x1 -> x0, starting transfers between devices: 8.65 us -> none  [body(): lax.all_to_all(outgoing, 'xfer', split_axis=0, concat_axis=0, tiled=True)]
    unnamed x21 -> x26, local copies, waits for them, and re-layouts: 5.8 us -> 12.6 us
  transfers between devices with their start and end apart: 2 -> 0, of which waited for: 1 -> 0; matrix products, arithmetic and copies ran while one was open for 1% -> 0% of each run, Pallas kernels for 38% -> 0%
where the time goes in v3:
time: 128 us; the launch traced here: 127 us
  Pallas kernels  112 us (88%)
  local copies, waits for them, and re-layouts  12.9 us (10%)
  other arithmetic  2.66 us (2%)
    pallas_call x1, Pallas kernels, finish(): pl.pallas_call(functools.partial(finish_kernel, scale), in_specs=[vmem] *...  55.9 us
    pallas_call x1, Pallas kernels, exchange(): pl.pallas_call(exchange_kernel, in_specs=[vmem, vmem], out_specs=[vmem, v...  39.8 us
    unnamed x26, local copies, waits for them, and re-layouts  12.6 us
    pallas_call x1, Pallas kernels, attend(): pl.pallas_call(functools.partial(attend_kernel, scale, page), in_specs=[s...  10.3 us
    pallas_call x1, Pallas kernels, prepare(): pl.pallas_call(prepare_kernel, in_specs=[pl.BlockSpec(memory_space=pltpu....  5.53 us

profile of v3, /device:TPU:1, one launch (start us, length us, event | category | flops | bytes accessed | tf_op | source)
XLA Modules:
  0.0 127.1 jit_solution(16988042575637556424)
XLA Ops:
  0.0 0.7 and_select_fusion
  0.7 1.2 select_reduce_fusion
  1.9 0.1 reshape.18
  2.0 0.7 reduce_sum.19.chosen
  2.7 5.5 %shard_map.91 = (bf16[32,64,576]{2,1,0:T(8,128)(2,1)}, bf16[256,576]{1,0:T(8,128)(2,1)}) custom-call(s32[32]{0:T(128)} %reduce_sum.19.chosen, bf16[32,64,576]{2,1,0:T(8,128)(2,1)} %pool.1, bf16[16,16,192]{2,1,0:T(8,128)(2,1)} %queries.1, bf16[16,128,512]{2,1,0:T(8,128)(2,1)} %key_up.1), custom_call_target="tpu_custom_call" | custom-call | tf_op jit(solution)/shard_map/pallas_call | solution.py:59
  8.3 0.0 copy-start.11
  8.3 0.0 copy-start.10
  8.3 0.0 copy-start.3
  8.3 1.7 %copy-done.3 = bf16[32,64,576]{2,1,0:T(8,128)(2,1)S(1)} copy-done((bf16[32,64,576]{2,1,0:T(8,128)(2,1)S(1)}, bf16[32,64,576]{2,1,0:T(8,128)(2,1)}, u32[]{:S(2)}) %copy-start.3) | copy-done | bytes 2359320
  10.1 0.0 copy-start.5
  10.1 1.0 copy-done.5
  11.0 39.8 %shard_map.92 = (bf16[32,64,576]{2,1,0:T(8,128)(2,1)S(1)}, bf16[8,2,128,576]{3,2,1,0:T(8,128)(2,1)S(1)}) custom-call(bf16[32,64,576]{2,1,0:T(8,128)(2,1)S(1)} %copy-done.3, bf16[2,128,576]{2,1,0:T(8,128)(2,1)S(1)} %bitcast.6), custom_call_target="tpu_custom_call" | custom-call | tf_op jit(solution)/shard_map/pallas_call | solution.py:144
  50.8 0.0 copy-start.1
  50.8 1.5 %copy-done.1 = bf16[8,2,128,576]{3,2,1,0:T(8,128)(2,1)} copy-done((bf16[8,2,128,576]{3,2,1,0:T(8,128)(2,1)}, bf16[8,2,128,576]{3,2,1,0:T(8,128)(2,1)S(1)}, u32[]{:S(2)}) %copy-start.1) | copy-done | bytes 2359320
  52.3 0.0 copy-done.11
  52.3 0.1 dynamic_slice.6.lengths
  52.4 0.0 copy-done.10
  52.4 0.1 dynamic_slice.7.starts
  52.5 0.0 copy-start.2
  52.5 1.7 %copy-done.2 = bf16[8,2,128,576]{3,2,1,0:T(8,128)(2,1)S(1)} copy-done((bf16[8,2,128,576]{3,2,1,0:T(8,128)(2,1)S(1)}, bf16[8,2,128,576]{3,2,1,0:T(8,128)(2,1)}, u32[]{:S(2)}) %copy-start.2) | copy-done | bytes 2359320
  54.2 0.0 copy-start.6
  54.2 0.0 copy-start.9
  54.2 10.3 %shard_map.93 = (f32[16,128,512]{2,1,0:T(8,128)S(1)}, f32[16,128,128]{2,1,0:T(8,128)S(1)}) custom-call(s32[8]{0:T(128)S(1)} %dynamic_slice.6.lengths, s32[8]{0:T(128)S(1)} %dynamic_slice.7.starts, s32[1]{0:T(128)} %bitcast.place, bf16[16,128,576]{2,1,0:T(8,128)(2,1)S(1)} %bitcast.5, bf16[2048,576]{1,0:T(8,128)(2,1)S(1)} %bitcast.4), custom_call_target="tpu_custom_call" | custom-call | tf_op jit(solution)/shard_map/pallas_call | solution.py:218
  64.5 0.0 copy-start
  64.5 1.9 %copy-done = f32[16,128,512]{2,1,0:T(8,128)} copy-done((f32[16,128,512]{2,1,0:T(8,128)}, f32[16,128,512]{2,1,0:T(8,128)S(1)}, u32[]{:S(2)}) %copy-start) | copy-done | bytes 4194328
  66.4 0.0 copy-start.7
  66.4 1.0 copy-done.7
  67.4 0.0 copy-start.8
  67.4 1.5 %copy.11.out_proj = bf16[2048,224]{1,0:T(8,128)(2,1)S(1)} copy(bf16[2048,224]{0,1:T(8,128)(2,1)} %param.17) | data formatting | bytes 1835008 | tf_op args[8]
  68.9 0.0 copy-done.6
  69.0 0.0 copy-done.9
  69.0 0.0 copy-done.8
  69.0 0.0 copy-start.4
  69.0 1.6 %copy-done.4 = bf16[16,512,128]{2,1,0:T(8,128)(2,1)S(1)} copy-done((bf16[16,512,128]{2,1,0:T(8,128)(2,1)S(1)}, bf16[16,512,128]{2,1,0:T(8,128)(2,1)}, u32[]{:S(2)}) %copy-start.4) | copy-done | bytes 2097176
  70.6 55.9 %shard_map.94 = bf16[64,224]{1,0:T(8,128)(2,1)S(1)} custom-call(f32[16,128,512]{2,1,0:T(8,128)} %copy-done, f32[16,128,128]{2,1,0:T(8,128)S(1)} %copy-done.8, bf16[256,576]{1,0:T(8,128)(2,1)S(1)} %copy-done.6, bf16[16,576]{1,0:T(8,128)(2,1)S(1)} %copy-done.9, bf16[16,512,128]{2,1,0:T(8,128)(2,1)S(1)} %copy-done.4, bf16[2048,224]{1,0:T(8,128)(2,1)S(1)} %copy.11.out_proj), custom_call_target="tpu_custom_call" | custom-call | tf_op jit(solution)/shard_map/pallas_call | solution.py:439
  126.5 0.6 copy.13
Async XLA Ops:
  8.3 44.0 %copy-start.11 = (s32[256]{0:T(256)S(1)}, s32[256]{0:T(256)}, u32[]{:S(2)}) copy-start(s32[256]{0:T(256)} %param.10) | copy-start | bytes 3076
  8.3 44.1 %copy-start.10 = (s32[256]{0:T(256)S(1)}, s32[256]{0:T(256)}, u32[]{:S(2)}) copy-start(s32[256]{0:T(256)} %param.11) | copy-start | bytes 3076
  8.3 1.8 %copy-start.3 = (bf16[32,64,576]{2,1,0:T(8,128)(2,1)S(1)}, bf16[32,64,576]{2,1,0:T(8,128)(2,1)}, u32[]{:S(2)}) copy-start(bf16[32,64,576]{2,1,0:T(8,128)(2,1)} %get-tuple-element.11.pages) | copy-start | bytes 7077892
  10.1 1.0 copy-start.5
  50.8 1.5 %copy-start.1 = (bf16[8,2,128,576]{3,2,1,0:T(8,128)(2,1)}, bf16[8,2,128,576]{3,2,1,0:T(8,128)(2,1)S(1)}, u32[]{:S(2)}) copy-start(bf16[8,2,128,576]{3,2,1,0:T(8,128)(2,1)S(1)} %get-tuple-element.13) | copy-start | bytes 7077892
  52.5 1.7 %copy-start.2 = (bf16[8,2,128,576]{3,2,1,0:T(8,128)(2,1)S(1)}, bf16[8,2,128,576]{3,2,1,0:T(8,128)(2,1)}, u32[]{:S(2)}) copy-start(bf16[8,2,128,576]{3,2,1,0:T(8,128)(2,1)} %copy-done.1) | copy-start | bytes 7077892
  54.2 14.7 %copy-start.6 = (bf16[256,576]{1,0:T(8,128)(2,1)S(1)}, bf16[256,576]{1,0:T(8,128)(2,1)}, u32[]{:S(2)}) copy-start(bf16[256,576]{1,0:T(8,128)(2,1)} %get-tuple-element.12.q_own) | copy-start | bytes 884740
  54.2 14.8 %copy-start.9 = (bf16[16,576]{1,0:T(8,128)(2,1)S(1)}, bf16[16,576]{1,0:T(8,128)(2,1)}, u32[]{:S(2)}) copy-start(bf16[16,576]{1,0:T(8,128)(2,1)} %fresh.1) | copy-start | bytes 55300
  64.5 1.9 %copy-start = (f32[16,128,512]{2,1,0:T(8,128)}, f32[16,128,512]{2,1,0:T(8,128)S(1)}, u32[]{:S(2)}) copy-start(f32[16,128,512]{2,1,0:T(8,128)S(1)} %get-tuple-element.15.acc) | copy-start | bytes 12582916
  66.4 1.0 copy-start.7
  67.4 1.6 %copy-start.8 = (f32[16,128,128]{2,1,0:T(8,128)S(1)}, f32[16,128,128]{2,1,0:T(8,128)}, u32[]{:S(2)}) copy-start(f32[16,128,128]{2,1,0:T(8,128)} %copy-done.7) | copy-start | bytes 3145732
  69.0 1.6 %copy-start.4 = (bf16[16,512,128]{2,1,0:T(8,128)(2,1)S(1)}, bf16[16,512,128]{2,1,0:T(8,128)(2,1)}, u32[]{:S(2)}) copy-start(bf16[16,512,128]{2,1,0:T(8,128)(2,1)} %value_up.1) | copy-start | bytes 6291460

commit v4 on v3

--- a/solution.py
+++ b/solution.py
@@ -73,7 +73,7 @@
     )(chosen, pool, queries, key_up)
 
 
-def exchange_kernel(pages, q_own, keys, q_all, p_send, p_recv, z_send, z_recv, own_sem):
+def exchange_kernel(pages, q_own, keys, q_all, q_s, page_s, p_send, p_recv, z_send, z_recv, own_sem):
     z = lax.axis_index("head")
     xfer = lax.axis_index("xfer")
     x, y, core = xfer // 8, (xfer // 2) % 4, xfer % 2
@@ -83,6 +83,12 @@
         dx, dy, dc = offset
         return (lax.rem(x + dx, 4) * 4 + lax.rem(y + dy, 4)) * 2 + lax.rem(core + dc, 2)
 
+    mine = [
+        pltpu.make_async_copy(q_own, q_s, own_sem.at[0]),
+        pltpu.make_async_copy(pages.at[xfer], page_s, own_sem.at[1]),
+    ]
+    for c in mine:
+        c.start()
     right, left = (xfer, lax.rem(z + 1, groups)), (xfer, lax.rem(z + groups - 1, groups))
     barrier = pltpu.get_barrier_semaphore()
     peers = [right, left] + [(at(offset), z) for offset in OFFSETS]
@@ -92,7 +98,7 @@
 
     def hop(way, j):
         block = lax.rem(z + groups - (j - 1), groups) if way == 0 else lax.rem(z + j - 1, groups)
-        src, dst = (q_own if j == 1 else q_all.at[block]), q_all.at[block]
+        src, dst = (q_s if j == 1 else q_all.at[block]), q_all.at[block]
         if j == groups // 2:
             src, dst = src.at[way], dst.at[way]
         return pltpu.make_async_remote_copy(
@@ -115,13 +121,17 @@
             device_id_type=MESH,
         )
 
-    mine = [
-        pltpu.make_async_copy(q_own, q_all.at[z], own_sem.at[0]),
-        pltpu.make_async_copy(pages.at[xfer], keys.at[xfer], own_sem.at[1]),
-    ]
     hops = [hop(way, j) for j in range(1, groups // 2 + 1) for way in (0, 1)]
     copies = [page(i, offset) for i, offset in enumerate(OFFSETS)]
-    for c in hops[:2] + copies + mine:
+    for c in mine:
+        c.wait()
+    for c in hops[:2] + copies:
+        c.start()
+    mine = [
+        pltpu.make_async_copy(q_s, q_all.at[z], own_sem.at[2]),
+        pltpu.make_async_copy(page_s, keys.at[xfer], own_sem.at[3]),
+    ]
+    for c in mine:
         c.start()
     for j in range(1, groups // 2):
         for way in (0, 1):
@@ -138,93 +148,135 @@
 
 
 def exchange(pages, q_own, groups):
-    vmem = pl.BlockSpec(memory_space=pltpu.VMEM)
+    hbm = pl.BlockSpec(memory_space=pl.ANY)
     dma = pltpu.SemaphoreType.DMA
     n = pages.shape[0]
     return pl.pallas_call(
         exchange_kernel,
-        in_specs=[vmem, vmem],
-        out_specs=[vmem, vmem],
+        in_specs=[hbm, hbm],
+        out_specs=[hbm, hbm],
         out_shape=[
             jax.ShapeDtypeStruct(pages.shape, pages.dtype),
             jax.ShapeDtypeStruct((groups, *q_own.shape), q_own.dtype),
         ],
-        scratch_shapes=[dma((n,)), dma((n,)), dma((2, 8)), dma((2, 8)), dma((2,))],
+        scratch_shapes=[
+            pltpu.VMEM(q_own.shape, q_own.dtype),
+            pltpu.VMEM(pages.shape[1:], pages.dtype),
+            dma((n,)),
+            dma((n,)),
+            dma((2, 8)),
+            dma((2, 8)),
+            dma((4,)),
+        ],
         compiler_params=pltpu.CompilerParams(
-            collective_id=0, has_side_effects=True, vmem_limit_bytes=40 * MIB
+            collective_id=0, has_side_effects=True, vmem_limit_bytes=56 * MIB
         ),
     )(pages, q_own)
 
 
-def attend_kernel(scale, page, lengths, starts, place, q, keys, acc, stats, m_s, l_s):
+def attend_kernel(scale, lengths, starts, place, q, keys, acc, stats, q_s, k_s, acc_s, st_s, m_s, l_s, k_sem, q_sem, o_sem):
     member = place[0]
     requests = lengths.shape[0]
+    slots, page, latent = keys.shape
     rows = q.shape[1] // requests
     many = q.shape[0] * rows
-    latent = q.shape[2]
     rank = acc.shape[2]
+    width = BLOCK // page
+    loads = [
+        pltpu.make_async_copy(keys, k_s.at[pl.ds(0, slots)], k_sem.at[0]),
+        pltpu.make_async_copy(keys.at[pl.ds(0, width)], k_s.at[pl.ds(slots, width)], k_sem.at[1]),
+    ]
+    q_loads = [
+        pltpu.make_async_copy(q.at[:, pl.ds(r * rows, rows)], q_s.at[r], q_sem.at[r]) for r in range(requests)
+    ]
+    for c in loads + q_loads:
+        c.start()
     lane = lax.broadcasted_iota(jnp.int32, (1, BLOCK), 1)
     odd = lax.broadcasted_iota(jnp.int32, (many, 128), 1) % 2
-    per_block = BLOCK // page
-    blocks = keys.shape[0] // BLOCK
+    for c in loads:
+        c.wait()
+    stores = []
     for r in range(requests):
         length, start = lengths[r], starts[r]
         pages = (length + page - 1) // page
         skip = (member - start) & 7
         slot = ((start + skip) & 255) >> 3
         count = jnp.maximum(pages - skip + 7, 0) >> 3
-        first = slot // per_block
-        n = jnp.minimum((slot % per_block + count + per_block - 1) // per_block, blocks)
-        n = jnp.where(count > 0, n, 0)
-        part = slice(r * rows, (r + 1) * rows)
-        acc[:, part, :] = jnp.zeros((q.shape[0], rows, rank), jnp.float32)
-        m_s[...] = jnp.full(m_s.shape, LOW, jnp.float32)
-        l_s[...] = jnp.zeros(l_s.shape, jnp.float32)
+        q_loads[r].wait()
+
+        def window(i):
+            first = (slot + i * width) & (slots - 1)
+            k = k_s[pl.ds(first, width)].reshape(BLOCK, latent)
+            s = lax.dot_general(
+                q_s[r].reshape(many, latent), k, (((1,), (1,)), ((), ())), preferred_element_type=jnp.float32
+            )
+            nth = i * width + lane // page
+            seen = (nth < count) & ((skip + nth * 8) * page + lane % page < length)
+            return jnp.where(seen, s * scale, LOW), seen, k[:, :rank]
+
+        def weigh(w, v):
+            return jnp.dot(w.astype(jnp.bfloat16), v, preferred_element_type=jnp.float32)
+
+        s, seen, v = window(0)
+        m = jnp.max(s, axis=1, keepdims=True)
+        w = jnp.where(seen, jnp.exp(s - m), 0.0)
+        m_s[...] = jnp.broadcast_to(m, m_s.shape)
+        l_s[...] = jnp.broadcast_to(jnp.sum(w, axis=1, keepdims=True), l_s.shape)
+        acc_s[r] = weigh(w, v).reshape(acc_s.shape[1:])
 
         def step(i, c):
-            b = (first + i) & (blocks - 1)
-            k = keys[pl.ds(pl.multiple_of(b * BLOCK, BLOCK), BLOCK), :]
-            mine = q[:, part, :].reshape(many, latent)
-            s = (
-                lax.dot_general(
-                    mine, k, (((1,), (1,)), ((), ())), preferred_element_type=jnp.float32
-                )
-                * scale
-            )
-            at = ((b * per_block + lane // page) * 8 + member - start) & 255
-            s = jnp.where(at * page + lane % page < length, s, LOW)
+            s, _, v = window(i)
             m_old = m_s[:, :1]
             m_new = jnp.maximum(m_old, jnp.max(s, axis=1, keepdims=True))
             keep = jnp.exp(m_old - m_new)
             w = jnp.exp(s - m_new)
             l_s[...] = l_s[...] * keep + jnp.sum(w, axis=1, keepdims=True)
             m_s[...] = jnp.broadcast_to(m_new, m_s.shape)
-            more = jnp.dot(
-                w.astype(jnp.bfloat16), k[:, :rank], preferred_element_type=jnp.float32
-            )
-            old = acc[:, part, :].reshape(many, rank)
-            acc[:, part, :] = (old * keep + more).reshape(q.shape[0], rows, rank)
+            old = acc_s[r].reshape(many, rank)
+            acc_s[r] = (old * keep + weigh(w, v)).reshape(acc_s.shape[1:])
             return c
 
-        lax.fori_loop(0, n, step, 0)
-        both = jnp.where(odd == 0, m_s[...], l_s[...])
-        stats[:, part, :] = both.reshape(q.shape[0], rows, 128)
-
-
-def attend(lengths, starts, place, q, keys, page, rank, scale):
+        lax.fori_loop(1, (count + width - 1) // width, step, 0)
+        st_s[r] = jnp.where(odd == 0, m_s[...], l_s[...]).reshape(st_s.shape[1:])
+        part = pl.ds(r * rows, rows)
+        stores += [
+            pltpu.make_async_copy(acc_s.at[r], acc.at[:, part], o_sem.at[0, r]),
+            pltpu.make_async_copy(st_s.at[r], stats.at[:, part], o_sem.at[1, r]),
+        ]
+        for c in stores[-2:]:
+            c.start()
+    for c in stores:
+        c.wait()
+
+
+def attend(lengths, starts, place, q, keys, rank, scale):
     smem = pl.BlockSpec(memory_space=pltpu.SMEM)
-    vmem = pl.BlockSpec(memory_space=pltpu.VMEM)
-    many = q.shape[0] * q.shape[1] // lengths.shape[0]
+    hbm = pl.BlockSpec(memory_space=pl.ANY)
+    requests = lengths.shape[0]
+    chunks, rows = q.shape[0], q.shape[1] // requests
+    many = chunks * rows
+    slots, page, latent = keys.shape
+    dma = pltpu.SemaphoreType.DMA
     return pl.pallas_call(
-        functools.partial(attend_kernel, scale, page),
-        in_specs=[smem, smem, smem, vmem, vmem],
-        out_specs=[vmem, vmem],
+        functools.partial(attend_kernel, scale),
+        in_specs=[smem, smem, smem, hbm, hbm],
+        out_specs=[hbm, hbm],
         out_shape=[
             jax.ShapeDtypeStruct((*q.shape[:2], rank), jnp.float32),
             jax.ShapeDtypeStruct((*q.shape[:2], 128), jnp.float32),
         ],
-        scratch_shapes=[pltpu.VMEM((many, 128), jnp.float32)] * 2,
-        compiler_params=pltpu.CompilerParams(vmem_limit_bytes=40 * MIB),
+        scratch_shapes=[
+            pltpu.VMEM((requests, chunks, rows, latent), q.dtype),
+            pltpu.VMEM((slots + BLOCK // page, page, latent), keys.dtype),
+            pltpu.VMEM((requests, chunks, rows, rank), jnp.float32),
+            pltpu.VMEM((requests, chunks, rows, 128), jnp.float32),
+            pltpu.VMEM((many, 128), jnp.float32),
+            pltpu.VMEM((many, 128), jnp.float32),
+            dma((2,)),
+            dma((requests,)),
+            dma((2, requests)),
+        ],
+        compiler_params=pltpu.CompilerParams(vmem_limit_bytes=56 * MIB),
     )(lengths, starts, place, q, keys)
 
 
@@ -235,8 +287,8 @@
 
 
 def finish_kernel(
-    scale, acc, stats, q_own, fresh, value_up, out_proj, out,
-    sent, sent_st, got, got_st, own, own_st, held, share, parts, z_send, z_recv, x_send, x_recv, o_send, o_recv,
+    scale, acc_h, stats_h, q_own_h, fresh_h, value_up_h, out_proj_h, out,
+    acc, stats, q_own, fresh, value_up, out_proj, acc_sem, in_sem, sent, sent_st, got, got_st, own, own_st, held, share, parts, z_send, z_recv, x_send, x_recv, o_send, o_recv,
 ):
     z = lax.axis_index("head")
     xfer = lax.axis_index("xfer")
@@ -244,6 +296,22 @@
     groups = 8
     rank = acc.shape[2]
     half_rows = acc.shape[1]
+    loads = [
+        pltpu.make_async_copy(src, dst, in_sem.at[i])
+        for i, (src, dst) in enumerate(
+            ((stats_h, stats), (q_own_h, q_own), (fresh_h, fresh), (value_up_h, value_up), (out_proj_h, out_proj))
+        )
+    ]
+
+    def load_acc(at):
+        return pltpu.make_async_copy(acc_h.at[at], acc.at[at], acc_sem.at[at])
+
+    loads[0].start()
+    for distance in (4, 3, 5, 0, 2, 6, 1, 7):
+        for half in (0, 1):
+            load_acc(lax.rem(z + distance, groups) * 2 + half).start()
+    for c in loads[1:]:
+        c.start()
 
     def near(dx, dy, flip):
         c = 1 - core if flip else core
@@ -291,6 +359,7 @@
     def send_on(way, half, hop):
         at = index_of(way, half, 4 - hop)
         mine = stats[at]
+        load_acc(at).wait()
         if hop == (0 if way == half else 1):
             sent[way, half, hop] = acc[at].astype(jnp.bfloat16)
             sent_st[way, half, hop] = mine.T[0:8]
@@ -319,14 +388,18 @@
         more = jnp.dot(w.astype(jnp.bfloat16), fresh[:, :rank], preferred_element_type=jnp.float32)
         at = z * 2 + half
         mine = stats[at]
+        load_acc(at).wait()
         m, l, total = combine(m, l, more, mine[:, 0:1], mine[:, 1:2], acc[at])
         own[half] = total
         own_st[half] = jnp.where(odd == 0, m, l)
 
+    loads[0].wait()
     send_on(0, 0, 0)
     send_on(1, 1, 0)
     send_on(0, 1, 1)
     send_on(1, 0, 1)
+    loads[1].wait()
+    loads[2].wait()
     take_fresh(0)
     take_fresh(1)
     for hop in (1, 2, 3):
@@ -367,6 +440,7 @@
     def pass_core(half, a, b):
         start(spread(half, 2, a, b, block_of(half, a, b) + core, near(0, 0, True)))
 
+    loads[3].wait()
     for half in (1, 0):
         m, l, total = own_st[half][:, 0:1], own_st[half][:, 1:2], own[half]
         for way in (0, 1):
@@ -397,13 +471,13 @@
             for b in range(4):
                 spread(half, 2, a, b, xfer, near(0, 0, True)).wait_recv()
 
-    rows = out.shape[0]
+    loads[4].wait()
     depth = held.shape[3]
     total = None
     for half in (0, 1):
         left = held[half].reshape(-1, depth)
-        right = out_proj[half * depth : (half + 1) * depth, :]
-        piece = jnp.dot(left, right, preferred_element_type=jnp.float32)
+        right = out_proj[:, half * depth : (half + 1) * depth]
+        piece = lax.dot_general(left, right, (((1,), (1,)), ((), ())), preferred_element_type=jnp.float32)
         total = piece if total is None else total + piece
     parts[...] = total.reshape(parts.shape)
 
@@ -431,17 +505,21 @@
 
 def finish(acc, stats, q_own, fresh, value_up, out_proj, owners, groups, scale):
     vmem = pl.BlockSpec(memory_space=pltpu.VMEM)
+    operands = (acc, stats, q_own, fresh, value_up, out_proj)
     rows = fresh.shape[0]
     half_rows, rank = acc.shape[1:]
-    depth, width = out_proj.shape
+    width, depth = out_proj.shape
     piece = owners * rows // groups
     dma = pltpu.SemaphoreType.DMA
     return pl.pallas_call(
         functools.partial(finish_kernel, scale),
-        in_specs=[vmem] * 6,
+        in_specs=[pl.BlockSpec(memory_space=pl.ANY)] * 6,
         out_specs=vmem,
         out_shape=jax.ShapeDtypeStruct((piece, width), jnp.bfloat16),
         scratch_shapes=[
+            *(pltpu.VMEM(a.shape, a.dtype) for a in operands),
+            dma((2 * groups,)),
+            dma((5,)),
             pltpu.VMEM((2, 2, 4, half_rows, rank), jnp.bfloat16),
             pltpu.VMEM((2, 2, 4, 8, 128), jnp.float32),
             pltpu.VMEM((2, 2, 4, half_rows, rank), jnp.bfloat16),
@@ -459,9 +537,9 @@
             dma((groups,)),
         ],
         compiler_params=pltpu.CompilerParams(
-            collective_id=1, has_side_effects=True, vmem_limit_bytes=48 * MIB
+            collective_id=1, has_side_effects=True, vmem_limit_bytes=56 * MIB
         ),
-    )(acc, stats, q_own, fresh, value_up, out_proj)
+    )(*operands)
 
 
 def body(
@@ -495,10 +573,10 @@
     arrived, every = exchange(pages, q_own.reshape(2, row_count * heads // 2, latent), groups)
     every = every.reshape(groups * 2, row_count * heads // 2, latent)
     acc, stats = attend(
-        my_lengths, my_starts, member.reshape(1), every, arrived.reshape(-1, latent),
-        page_len, lat_rank, score_scale,
+        my_lengths, my_starts, member.reshape(1), every, arrived,
+        lat_rank, score_scale,
     )
-    return finish(acc, stats, q_own, new_latent, value_up, out_proj, owners, groups, score_scale)
+    return finish(acc, stats, q_own, new_latent, value_up, out_proj.T, owners, groups, score_scale)
 
 
 def solution(mesh):

time: 128 us -> 121 us (0.945)
  local copies, waits for them, and re-layouts: 12.9 us -> 3.98 us
  Pallas kernels: 112 us -> 114 us
    unnamed x26 -> x1, local copies, waits for them, and re-layouts: 12.6 us -> 1.38 us
    pallas_call x3, Pallas kernels: 106 us -> 109 us  [the longest x1 55.8 us: finish(): pl.pallas_call(functools.partial(finish_kernel, scale), in_specs=[pl.Bloc...]
where the time goes in v4:
time: 121 us
  Pallas kernels  114 us (94%)
  local copies, waits for them, and re-layouts  3.98 us (3%)
  other arithmetic  2.58 us (2%)
    pallas_call x1, Pallas kernels, finish(): pl.pallas_call(functools.partial(finish_kernel, scale), in_specs=[pl.Bloc...  55.8 us
    pallas_call x1, Pallas kernels, exchange(): pl.pallas_call(exchange_kernel, in_specs=[hbm, hbm], out_specs=[hbm, hbm]...  42.3 us
    pallas_call x1, Pallas kernels, attend(): pl.pallas_call(functools.partial(attend_kernel, scale), in_specs=[smem, s...  10.7 us
    pallas_call x1, Pallas kernels, prepare(): pl.pallas_call(prepare_kernel, in_specs=[pl.BlockSpec(memory_space=pltpu....  5.37 us

profile of v4, /device:TPU:1, one launch (start us, length us, event | category | flops | bytes accessed | tf_op | source)
XLA Modules:
  0.0 120.8 jit_solution(18038937915613891406)
XLA Ops:
  0.0 1.3 %dynamic_slice.6.lengths = s32[8]{0:T(128)} dynamic-slice(s32[256]{0:T(256)} %param.10, s32[]{:T(128)S(6)} %select_n.20), dynamic_slice_sizes={8} | dynamic-slice | bytes 68 | tf_op jit(solution)/shard_map/dynamic_slice | solution.py:570
  1.3 1.3 %dynamic_slice.7.starts = s32[8]{0:T(128)} dynamic-slice(s32[256]{0:T(256)} %param.11, s32[]{:T(128)S(6)} %select_n.20), dynamic_slice_sizes={8} | dynamic-slice | bytes 68 | tf_op jit(solution)/shard_map/dynamic_slice | solution.py:571
  2.5 0.7 and_select_fusion
  3.2 1.2 %select_reduce_fusion = s32[256]{0:T(256)S(1)} fusion(s32[256,256]{1,0:T(8,128)} %param.12, s32[256]{0:T(256)S(1)} %and_select_fusion, s32[]{:T(128)S(6)} %add.39, s32[256]{0:T(256)} %param.11), kind=kLoop, calls=%fused_computation.5 | loop fusion | flops 1113856 | bytes 265220 | tf_op jit(solution)/shard_map/reduce_sum | solution.py:567
  4.5 0.1 reshape.15
  4.5 0.7 reduce_sum.19.chosen
  5.2 5.4 %shard_map.91 = (bf16[32,64,576]{2,1,0:T(8,128)(2,1)}, bf16[256,576]{1,0:T(8,128)(2,1)}) custom-call(s32[32]{0:T(128)} %reduce_sum.19.chosen, bf16[32,64,576]{2,1,0:T(8,128)(2,1)} %pool.1, bf16[16,16,192]{2,1,0:T(8,128)(2,1)} %queries.1, bf16[16,128,512]{2,1,0:T(8,128)(2,1)} %key_up.1), custom_call_target="tpu_custom_call" | custom-call | tf_op jit(solution)/shard_map/pallas_call | solution.py:59
  10.6 42.3 %shard_map.92 = (bf16[32,64,576]{2,1,0:T(8,128)(2,1)}, bf16[8,2,128,576]{3,2,1,0:T(8,128)(2,1)}) custom-call(bf16[32,64,576]{2,1,0:T(8,128)(2,1)} %get-tuple-element.11.pages, bf16[2,128,576]{2,1,0:T(8,128)(2,1)} %bitcast.5), custom_call_target="tpu_custom_call" | custom-call | tf_op jit(solution)/shard_map/pallas_call | solution.py:154
  52.9 10.7 %shard_map.93 = (f32[16,128,512]{2,1,0:T(8,128)}, f32[16,128,128]{2,1,0:T(8,128)}) custom-call(s32[8]{0:T(128)} %dynamic_slice.6.lengths, s32[8]{0:T(128)} %dynamic_slice.7.starts, s32[1]{0:T(128)} %bitcast.place, bf16[16,128,576]{2,1,0:T(8,128)(2,1)} %bitcast.4, bf16[32,64,576]{2,1,0:T(8,128)(2,1)} %get-tuple-element.14.keys), custom_call_target="tpu_custom_call" | custom-call | tf_op jit(solution)/shard_map/pallas_call | solution.py:260
  63.6 55.8 %shard_map.94 = bf16[64,224]{1,0:T(8,128)(2,1)} custom-call(f32[16,128,512]{2,1,0:T(8,128)} %get-tuple-element.15.acc_h, f32[16,128,128]{2,1,0:T(8,128)} %get-tuple-element.16.stats_h, bf16[256,576]{1,0:T(8,128)(2,1)} %get-tuple-element.12.q_own_h, bf16[16,576]{1,0:T(8,128)(2,1)} %fresh_h.1, bf16[16,512,128]{2,1,0:T(8,128)(2,1)} %value_up_h.1, ...), custom_call_target="tpu_custom_call" | custom-call | tf_op jit(solution)/shard_map/pallas_call | solution.py:514
  119.4 1.4 %copy.11 = bf16[64,224]{1,0:T(8,128)(2,1)} copy(bf16[64,224]{1,0:T(8,128)(2,1)} %shard_map.94) | data formatting | bytes 57344

commit v5 on v4

--- a/solution.py
+++ b/solution.py
@@ -18,16 +18,22 @@
 OFFSETS = tuple((*d, 0) for d in FAR) + tuple((*d, 1) for d in FAR) + ((0, 0, 1),)
 
 
-def prepare_kernel(chosen, pool, queries, key_up, pages, q_own, sems, nope_s, wide_s):
-    def copy(o):
-        return pltpu.make_async_copy(pool.at[chosen[o]], pages.at[o], sems.at[o])
+def prepare_kernel(groups, lengths, starts, table, pool, queries, key_up, pages, q_own, sems, nope_s, wide_s):
+    me = lax.axis_index("xfer") * groups + lax.axis_index("head")
+    per_owner = lengths.shape[0] // pages.shape[0]
+    page = pages.shape[1]
 
     def begin(o, c):
-        copy(o).start()
+        slot = 0
+        for i in range(per_owner):
+            r = o * per_owner + i
+            j = (me - starts[r]) & (table.shape[1] - 1)
+            slot = jnp.where(j * page < lengths[r], table[r, j], slot)
+        pltpu.make_async_copy(pool.at[slot], pages.at[o], sems.at[o]).start()
         return c
 
     def end(o, c):
-        copy(o).wait()
+        pltpu.make_async_copy(pool.at[0], pages.at[o], sems.at[o]).wait()
         return c
 
     lax.fori_loop(0, pages.shape[0], begin, 0)
@@ -51,14 +57,14 @@
     lax.fori_loop(0, pages.shape[0], end, 0)
 
 
-def prepare(chosen, pool, queries, key_up):
-    n = chosen.shape[0]
+def prepare(lengths, starts, table, pool, queries, key_up, n, groups):
     rows, heads, width = queries.shape
     nope, rank = key_up.shape[1:]
     vmem = pl.BlockSpec(memory_space=pltpu.VMEM)
+    smem = pl.BlockSpec(memory_space=pltpu.SMEM)
     return pl.pallas_call(
-        prepare_kernel,
-        in_specs=[pl.BlockSpec(memory_space=pltpu.SMEM), pl.BlockSpec(memory_space=pl.ANY), vmem, vmem],
+        functools.partial(prepare_kernel, groups),
+        in_specs=[smem, smem, smem, pl.BlockSpec(memory_space=pl.ANY), vmem, vmem],
         out_specs=[vmem, vmem],
         out_shape=[
             jax.ShapeDtypeStruct((n, *pool.shape[1:]), pool.dtype),
@@ -70,7 +76,7 @@
             pltpu.VMEM((rank // 128, rows * heads, 128), jnp.float32),
         ],
         compiler_params=pltpu.CompilerParams(vmem_limit_bytes=56 * MIB),
-    )(chosen, pool, queries, key_up)
+    )(lengths, starts, table, pool, queries, key_up)
 
 
 def exchange_kernel(pages, q_own, keys, q_all, q_s, page_s, p_send, p_recv, z_send, z_recv, own_sem):
@@ -174,9 +180,9 @@
     )(pages, q_own)
 
 
-def attend_kernel(scale, lengths, starts, place, q, keys, acc, stats, q_s, k_s, acc_s, st_s, m_s, l_s, k_sem, q_sem, o_sem):
-    member = place[0]
-    requests = lengths.shape[0]
+def attend_kernel(scale, requests, lengths, starts, q, keys, acc, stats, q_s, k_s, acc_s, st_s, m_s, l_s, k_sem, q_sem, o_sem):
+    member = lax.axis_index("head")
+    base = lax.axis_index("xfer") * requests
     slots, page, latent = keys.shape
     rows = q.shape[1] // requests
     many = q.shape[0] * rows
@@ -197,7 +203,7 @@
         c.wait()
     stores = []
     for r in range(requests):
-        length, start = lengths[r], starts[r]
+        length, start = lengths[base + r], starts[base + r]
         pages = (length + page - 1) // page
         skip = (member - start) & 7
         slot = ((start + skip) & 255) >> 3
@@ -249,17 +255,16 @@
         c.wait()
 
 
-def attend(lengths, starts, place, q, keys, rank, scale):
+def attend(lengths, starts, q, keys, requests, rank, scale):
     smem = pl.BlockSpec(memory_space=pltpu.SMEM)
     hbm = pl.BlockSpec(memory_space=pl.ANY)
-    requests = lengths.shape[0]
     chunks, rows = q.shape[0], q.shape[1] // requests
     many = chunks * rows
     slots, page, latent = keys.shape
     dma = pltpu.SemaphoreType.DMA
     return pl.pallas_call(
-        functools.partial(attend_kernel, scale),
-        in_specs=[smem, smem, smem, hbm, hbm],
+        functools.partial(attend_kernel, scale, requests),
+        in_specs=[smem, smem, hbm, hbm],
         out_specs=[hbm, hbm],
         out_shape=[
             jax.ShapeDtypeStruct((*q.shape[:2], rank), jnp.float32),
@@ -277,7 +282,7 @@
             dma((2, requests)),
         ],
         compiler_params=pltpu.CompilerParams(vmem_limit_bytes=56 * MIB),
-    )(lengths, starts, place, q, keys)
+    )(lengths, starts, q, keys)
 
 
 def combine(m_a, l_a, acc_a, m_b, l_b, acc_b):
@@ -288,7 +293,7 @@
 
 def finish_kernel(
     scale, acc_h, stats_h, q_own_h, fresh_h, value_up_h, out_proj_h, out,
-    acc, stats, q_own, fresh, value_up, out_proj, acc_sem, in_sem, sent, sent_st, got, got_st, own, own_st, held, share, parts, z_send, z_recv, x_send, x_recv, o_send, o_recv,
+    acc, stats, q_own, fresh, value_up, out_proj, acc_sem, in_sem, sent, sent_st, got, got_st, own, own_st, lat_s, held, share, parts, z_send, z_recv, x_send, x_recv, o_send, o_recv,
 ):
     z = lax.axis_index("head")
     xfer = lax.axis_index("xfer")
@@ -307,9 +312,9 @@
         return pltpu.make_async_copy(acc_h.at[at], acc.at[at], acc_sem.at[at])
 
     loads[0].start()
-    for distance in (4, 3, 5, 0, 2, 6, 1, 7):
-        for half in (0, 1):
-            load_acc(lax.rem(z + distance, groups) * 2 + half).start()
+    for half in (0, 1):
+        for i in range(groups):
+            load_acc(2 * i + half).start()
     for c in loads[1:]:
         c.start()
 
@@ -328,54 +333,62 @@
         pl.semaphore_signal(barrier, inc=1, device_id=peer, device_id_type=MESH)
     pl.semaphore_wait(barrier, len(peers))
 
-    def z_copies(way, half, hop):
+    rows = half_rows // 2
+
+    def z_copies(way, piece, hop):
         to = along(1 if way == 0 else 7)
         return [
             pltpu.make_async_remote_copy(
-                src_ref=src.at[way, half, hop],
-                dst_ref=dst.at[way, half, hop],
-                send_sem=z_send.at[way, half, hop, i],
-                recv_sem=z_recv.at[way, half, hop, i],
+                src_ref=src.at[way, piece, hop],
+                dst_ref=dst.at[way, piece, hop],
+                send_sem=z_send.at[way, piece, hop, i],
+                recv_sem=z_recv.at[way, piece, hop, i],
                 device_id=to,
                 device_id_type=MESH,
             )
             for i, (src, dst) in enumerate(((sent, got), (sent_st, got_st)))
         ]
 
-    def index_of(way, half, distance):
+    def index_of(way, piece, distance):
         d = lax.rem(z + distance if way == 0 else z + groups - distance, groups)
-        return d * 2 + half
+        return d * 2 + piece // 2
+
+    def rows_of(piece):
+        return slice(piece % 2 * rows, (piece % 2 + 1) * rows)
 
     odd = lax.broadcasted_iota(jnp.int32, (half_rows, 128), 1) % 2
 
-    def arrived(way, half, hop):
-        for c in z_copies(way, half, hop):
+    def as_rows(st):
+        return jnp.concatenate([st, st], axis=0).T[0:8]
+
+    def arrived(way, piece, hop):
+        for c in z_copies(way, piece, hop):
             c.wait_recv()
-        st = jnp.tile(got_st[way, half, hop], (half_rows // 8, 1)).T
-        return st[:, 0:1], st[:, 1:2], got[way, half, hop].astype(jnp.float32)
+        st = jnp.tile(got_st[way, piece, hop], (half_rows // 8, 1)).T[0:rows]
+        return st[:, 0:1], st[:, 1:2], got[way, piece, hop].astype(jnp.float32)
 
     started = []
 
-    def send_on(way, half, hop):
-        at = index_of(way, half, 4 - hop)
-        mine = stats[at]
-        load_acc(at).wait()
-        if hop == (0 if way == half else 1):
-            sent[way, half, hop] = acc[at].astype(jnp.bfloat16)
-            sent_st[way, half, hop] = mine.T[0:8]
+    def send_on(way, piece, hop):
+        at = index_of(way, piece, 4 - hop)
+        part = rows_of(piece)
+        mine = stats[at, part]
+        if hop == (0 if way == piece % 2 else 1):
+            sent[way, piece, hop] = acc[at, part].astype(jnp.bfloat16)
+            sent_st[way, piece, hop] = as_rows(mine)
         else:
-            m, l, total = combine(*arrived(way, half, hop - 1), mine[:, 0:1], mine[:, 1:2], acc[at])
-            sent[way, half, hop] = total.astype(jnp.bfloat16)
-            sent_st[way, half, hop] = jnp.where(odd == 0, m, l).T[0:8]
-        for c in z_copies(way, half, hop):
+            m, l, total = combine(*arrived(way, piece, hop - 1), mine[:, 0:1], mine[:, 1:2], acc[at, part])
+            sent[way, piece, hop] = total.astype(jnp.bfloat16)
+            sent_st[way, piece, hop] = as_rows(jnp.where(odd[0:rows] == 0, m, l))
+        for c in z_copies(way, piece, hop):
             c.start()
             started.append(c)
 
     def take_fresh(half):
-        rows = slice(half * half_rows, (half + 1) * half_rows)
+        part = slice(half * half_rows, (half + 1) * half_rows)
         s = (
             lax.dot_general(
-                q_own[rows, :], fresh[...], (((1,), (1,)), ((), ())), preferred_element_type=jnp.float32
+                q_own[part, :], fresh[...], (((1,), (1,)), ((), ())), preferred_element_type=jnp.float32
             )
             * scale
         )
@@ -388,26 +401,22 @@
         more = jnp.dot(w.astype(jnp.bfloat16), fresh[:, :rank], preferred_element_type=jnp.float32)
         at = z * 2 + half
         mine = stats[at]
-        load_acc(at).wait()
         m, l, total = combine(m, l, more, mine[:, 0:1], mine[:, 1:2], acc[at])
         own[half] = total
         own_st[half] = jnp.where(odd == 0, m, l)
 
-    loads[0].wait()
-    send_on(0, 0, 0)
-    send_on(1, 1, 0)
-    send_on(0, 1, 1)
-    send_on(1, 0, 1)
-    loads[1].wait()
-    loads[2].wait()
-    take_fresh(0)
-    take_fresh(1)
-    for hop in (1, 2, 3):
-        send_on(0, 0, hop)
-        send_on(1, 1, hop)
-        if hop < 3:
-            send_on(0, 1, hop + 1)
-            send_on(1, 0, hop + 1)
+    def chain(half, part):
+        a, b = 2 * half, 2 * half + 1
+        steps = (
+            ((0, a, 0), (1, b, 0), (0, b, 1), (1, a, 1)),
+            ((0, a, 1), (1, b, 1)),
+            ((0, b, 2), (1, a, 2)),
+            ((0, a, 2), (1, b, 2)),
+            ((0, b, 3), (1, a, 3)),
+            ((0, a, 3), (1, b, 3)),
+        )
+        for step in steps[part]:
+            send_on(*step)
 
     def spread(half, kind, a, b, block, to):
         return pltpu.make_async_remote_copy(
@@ -440,12 +449,15 @@
     def pass_core(half, a, b):
         start(spread(half, 2, a, b, block_of(half, a, b) + core, near(0, 0, True)))
 
-    loads[3].wait()
-    for half in (1, 0):
-        m, l, total = own_st[half][:, 0:1], own_st[half][:, 1:2], own[half]
-        for way in (0, 1):
-            m, l, total = combine(m, l, total, *arrived(way, half, 3))
-        latent = (total / l).astype(jnp.bfloat16)
+    def values(half):
+        for piece in (2 * half, 2 * half + 1):
+            part = rows_of(piece)
+            st = own_st[half, part]
+            m, l, total = st[:, 0:1], st[:, 1:2], own[half, part]
+            for way in (0, 1):
+                m, l, total = combine(m, l, total, *arrived(way, piece, 3))
+            lat_s[part] = (total / l).astype(jnp.bfloat16)
+        latent = lat_s[...]
         heads = half_rows // fresh.shape[0]
         for h in range(heads):
             full = jnp.dot(latent, value_up[half * heads + h], preferred_element_type=jnp.float32)
@@ -456,30 +468,59 @@
             start(spread(half, 0, 0, k, xfer, to_first(half, k)))
         pass_second(half, 0)
         pass_core(half, 0, 0)
-    for a in range(1, 4):
-        for half in (1, 0):
+
+    def spread_first(half):
+        for a in range(1, 4):
             spread(half, 0, 0, a, xfer, near(0, 0, True)).wait_recv()
             pass_second(half, a)
             pass_core(half, a, 0)
-    for a in range(4):
-        for b in range(1, 4):
-            for half in (1, 0):
+
+    def spread_second(half):
+        for a in range(4):
+            for b in range(1, 4):
                 spread(half, 1, a, b, xfer, near(0, 0, True)).wait_recv()
                 pass_core(half, a, b)
-    for half in (1, 0):
+
+    def project(half):
         for a in range(4):
             for b in range(4):
                 spread(half, 2, a, b, xfer, near(0, 0, True)).wait_recv()
-
-    loads[4].wait()
-    depth = held.shape[3]
-    total = None
-    for half in (0, 1):
+        depth = held.shape[3]
         left = held[half].reshape(-1, depth)
         right = out_proj[:, half * depth : (half + 1) * depth]
         piece = lax.dot_general(left, right, (((1,), (1,)), ((), ())), preferred_element_type=jnp.float32)
-        total = piece if total is None else total + piece
-    parts[...] = total.reshape(parts.shape)
+        return piece.reshape(parts.shape)
+
+    loads[0].wait()
+    for half in (0, 1):
+        for i in range(groups):
+            load_acc(2 * i + half).wait()
+        if half == 0:
+            chain(0, 0)
+            loads[1].wait()
+            loads[2].wait()
+            take_fresh(0)
+    for part in (1, 2, 3):
+        chain(0, part)
+    chain(1, 0)
+    take_fresh(1)
+    chain(0, 4)
+    chain(0, 5)
+    chain(1, 1)
+    loads[3].wait()
+    values(0)
+    chain(1, 2)
+    chain(1, 3)
+    spread_first(0)
+    chain(1, 4)
+    spread_second(0)
+    chain(1, 5)
+    loads[4].wait()
+    parts[...] = project(0)
+    values(1)
+    spread_first(1)
+    spread_second(1)
+    parts[...] += project(1)
 
     def final(k):
         return pltpu.make_async_remote_copy(
@@ -520,17 +561,18 @@
             *(pltpu.VMEM(a.shape, a.dtype) for a in operands),
             dma((2 * groups,)),
             dma((5,)),
-            pltpu.VMEM((2, 2, 4, half_rows, rank), jnp.bfloat16),
-            pltpu.VMEM((2, 2, 4, 8, 128), jnp.float32),
-            pltpu.VMEM((2, 2, 4, half_rows, rank), jnp.bfloat16),
-            pltpu.VMEM((2, 2, 4, 8, 128), jnp.float32),
+            pltpu.VMEM((2, 4, 4, half_rows // 2, rank), jnp.bfloat16),
+            pltpu.VMEM((2, 4, 4, 8, 128), jnp.float32),
+            pltpu.VMEM((2, 4, 4, half_rows // 2, rank), jnp.bfloat16),
+            pltpu.VMEM((2, 4, 4, 8, 128), jnp.float32),
             pltpu.VMEM((2, half_rows, rank), jnp.float32),
             pltpu.VMEM((2, half_rows, 128), jnp.float32),
+            pltpu.VMEM((half_rows, rank), jnp.bfloat16),
             pltpu.VMEM((2, owners, rows, depth // 2), jnp.bfloat16),
             pltpu.VMEM((2, groups, piece, width), jnp.bfloat16),
             pltpu.VMEM((groups, piece, width), jnp.float32),
-            dma((2, 2, 4, 2)),
-            dma((2, 2, 4, 2)),
+            dma((2, 4, 4, 2)),
+            dma((2, 4, 4, 2)),
             dma((2, 3, 4, 4)),
             dma((2, 3, 4, 4)),
             dma((groups,)),
@@ -547,35 +589,15 @@
 ):
     owners = lax.axis_size("xfer")
     groups = lax.axis_size("head")
-    devices = owners * groups
-    owner_idx = lax.axis_index("xfer")
-    member = lax.axis_index("head")
-    local_device = owner_idx * groups + member
-    page_len = kv_pool.shape[1]
     latent = kv_pool.shape[2]
     lat_rank = value_up.shape[1]
-    per_owner = lengths.shape[0] // owners
-    table_width = page_table.shape[1]
     row_count, heads = queries.shape[:2]
     score_scale = queries.shape[2] ** (-0.5)
-    page_counts = (lengths + page_len - 1) // page_len
-    column = jnp.arange(table_width, dtype=jnp.int32)
-    located = ((start_device[:, None] + column[None, :]) % devices == local_device) & (
-        column[None, :] < page_counts[:, None]
-    )
-    chosen = (
-        jnp.sum(jnp.where(located, page_table, 0), axis=1).reshape(owners, per_owner).sum(axis=1)
-    )
-    first_req = owner_idx * per_owner
-    my_lengths = lax.dynamic_slice_in_dim(lengths, first_req, per_owner, 0)
-    my_starts = lax.dynamic_slice_in_dim(start_device, first_req, per_owner, 0)
-    pages, q_own = prepare(chosen, kv_pool, queries, key_up)
-    arrived, every = exchange(pages, q_own.reshape(2, row_count * heads // 2, latent), groups)
-    every = every.reshape(groups * 2, row_count * heads // 2, latent)
-    acc, stats = attend(
-        my_lengths, my_starts, member.reshape(1), every, arrived,
-        lat_rank, score_scale,
-    )
+    half_rows = row_count * heads // 2
+    pages, q_own = prepare(lengths, start_device, page_table, kv_pool, queries, key_up, owners, groups)
+    keys, every = exchange(pages, q_own.reshape(2, half_rows, latent), groups)
+    every = every.reshape(groups * 2, half_rows, latent)
+    acc, stats = attend(lengths, start_device, every, keys, lengths.shape[0] // owners, lat_rank, score_scale)
     return finish(acc, stats, q_own, new_latent, value_up, out_proj.T, owners, groups, score_scale)
 
 

time: 121 us -> 128 us (1.058)
  Pallas kernels: 114 us -> 126 us
  local copies, waits for them, and re-layouts: 3.98 us -> 1.38 us
  other arithmetic: 2.58 us -> 0 us
    pallas_call x1, Pallas kernels: 55.8 us -> 64.1 us  [finish(): pl.pallas_call(functools.partial(finish_kernel, scale), in_specs=[pl.Bloc...]
    pallas_call x2, Pallas kernels: 16.1 us -> 20.3 us  [the longest x1 10.9 us: attend(): pl.pallas_call(functools.partial(attend_kernel, scale, requests), in_spec...]
    dynamic_slice x2 -> x0, local copies, waits for them, and re-layouts: 2.52 us -> none  [the longest x1 1.26 us: body(): my_starts = lax.dynamic_slice_in_dim(start_device, first_req, per_owner, 0)]
    reduce_sum x2 -> x0, other arithmetic: 1.9 us -> none  [body(): jnp.sum(jnp.where(located, page_table, 0), axis=1)]
where the time goes in v5:
time: 128 us
  Pallas kernels  126 us (98%)
  local copies, waits for them, and re-layouts  1.38 us (1%)
    pallas_call x1, Pallas kernels, finish(): pl.pallas_call(functools.partial(finish_kernel, scale), in_specs=[pl.Bloc...  64.1 us
    pallas_call x1, Pallas kernels, exchange(): pl.pallas_call(exchange_kernel, in_specs=[hbm, hbm], out_specs=[hbm, hbm]...  41.8 us
    pallas_call x1, Pallas kernels, attend(): pl.pallas_call(functools.partial(attend_kernel, scale, requests), in_spec...  10.9 us
    pallas_call x1, Pallas kernels, prepare(): pl.pallas_call(functools.partial(prepare_kernel, groups), in_specs=[smem,...  9.4 us

profile of v5, /device:TPU:1, one launch (start us, length us, event | category | flops | bytes accessed | tf_op | source)
XLA Modules:
  0.0 127.6 jit_solution(4789041532455553848)
XLA Ops:
  0.0 9.4 %shard_map.91 = (bf16[32,64,576]{2,1,0:T(8,128)(2,1)}, bf16[256,576]{1,0:T(8,128)(2,1)}) custom-call(s32[256]{0:T(256)} %lengths.3, s32[256]{0:T(256)} %starts.3, s32[256,256]{1,0:T(8,128)} %table.1, bf16[32,64,576]{2,1,0:T(8,128)(2,1)} %pool.1, bf16[16,16,192]{2,1,0:T(8,128)(2,1)} %queries.1, bf16[16,128,512]{2,1,0:T(8,128)(2,1)} %key_up.1), custom_call_target="tpu_custom_call" | custom-call | tf_op jit(solution)/shard_map/pallas_call | solution.py:65
  9.4 41.8 %shard_map.92 = (bf16[32,64,576]{2,1,0:T(8,128)(2,1)}, bf16[8,2,128,576]{3,2,1,0:T(8,128)(2,1)}) custom-call(bf16[32,64,576]{2,1,0:T(8,128)(2,1)} %get-tuple-element.11.pages, bf16[2,128,576]{2,1,0:T(8,128)(2,1)} %bitcast.4), custom_call_target="tpu_custom_call" | custom-call | tf_op jit(solution)/shard_map/pallas_call | solution.py:160
  51.2 10.9 %shard_map.93 = (f32[16,128,512]{2,1,0:T(8,128)}, f32[16,128,128]{2,1,0:T(8,128)}) custom-call(s32[256]{0:T(256)} %lengths.3, s32[256]{0:T(256)} %starts.3, bf16[16,128,576]{2,1,0:T(8,128)(2,1)} %bitcast.3, bf16[32,64,576]{2,1,0:T(8,128)(2,1)} %get-tuple-element.14.keys), custom_call_target="tpu_custom_call" | custom-call | tf_op jit(solution)/shard_map/pallas_call | solution.py:265
  62.0 64.1 %shard_map.94 = bf16[64,224]{1,0:T(8,128)(2,1)} custom-call(f32[16,128,512]{2,1,0:T(8,128)} %get-tuple-element.15.acc_h, f32[16,128,128]{2,1,0:T(8,128)} %get-tuple-element.16.stats_h, bf16[256,576]{1,0:T(8,128)(2,1)} %get-tuple-element.12.q_own_h, bf16[16,576]{1,0:T(8,128)(2,1)} %fresh_h.1, bf16[16,512,128]{2,1,0:T(8,128)(2,1)} %value_up_h.1, ...), custom_call_target="tpu_custom_call" | custom-call | tf_op jit(solution)/shard_map/pallas_call | solution.py:555
  126.2 1.4 %copy.11 = bf16[64,224]{1,0:T(8,128)(2,1)} copy(bf16[64,224]{1,0:T(8,128)(2,1)} %shard_map.94) | data formatting | bytes 57344

commit v6 on v4

--- a/solution.py
+++ b/solution.py
@@ -10,7 +10,7 @@
 MESH = pl.DeviceIdType.MESH
 STEPS = 2
 LOW = -1e30
-BLOCK = 256
+FIRST, NEXT = 4, 8
 MIB = 1024 * 1024
 
 
@@ -18,25 +18,46 @@
 OFFSETS = tuple((*d, 0) for d in FAR) + tuple((*d, 1) for d in FAR) + ((0, 0, 1),)
 
 
-def prepare_kernel(chosen, pool, queries, key_up, pages, q_own, sems, nope_s, wide_s):
-    def copy(o):
-        return pltpu.make_async_copy(pool.at[chosen[o]], pages.at[o], sems.at[o])
+def prepare_kernel(which, table, pool, queries, key_up_h, pages, q_own, raw, packed, key_up, sems, out_sems, up_sem, nope_s, wide_s):
+    shift = table.shape[1]
+    load_up = pltpu.make_async_copy(key_up_h, key_up, up_sem.at[0])
+
+    def fetch(o, slot):
+        return pltpu.make_async_copy(pool.at[slot], raw.at[o], sems.at[o])
+
+    def store(o):
+        return pltpu.make_async_copy(packed.at[o], pages.at[o], out_sems.at[o])
 
     def begin(o, c):
-        copy(o).start()
+        e = which[o]
+        fetch(o, table[e // shift, e % shift]).start()
         return c
 
+    page = pool.shape[1]
+
+    def pack(o, c):
+        fetch(o, 0).wait()
+        for i in range(rank // 128):
+            packed[o, i * page : (i + 1) * page, :] = raw[o, :, i * 128 : (i + 1) * 128]
+        top, low = raw[o, : page // 2, rank:], raw[o, page // 2 :, rank:]
+        packed[o, rank // 128 * page :, :] = jnp.concatenate([top, low], axis=1)
+        store(o).start()
+        return c
+
     def end(o, c):
-        copy(o).wait()
+        store(o).wait()
         return c
 
     lax.fori_loop(0, pages.shape[0], begin, 0)
+    load_up.start()
     rows, heads, width = queries.shape
     nope, rank = key_up.shape[1:]
     half = heads // 2
     flat = queries[...].reshape(rows * heads, width).astype(jnp.float32)
     nope_s[...] = flat[:, :nope]
     rope = flat[:, nope:].reshape(rows, 2, half, width - nope)
+    lax.fori_loop(0, pages.shape[0], pack, 0)
+    load_up.wait()
     for h in range(heads):
         mine = nope_s[pl.ds(h, rows, stride=heads), :].astype(jnp.bfloat16)
         full = jnp.dot(mine, key_up[h], preferred_element_type=jnp.float32)
@@ -51,26 +72,36 @@
     lax.fori_loop(0, pages.shape[0], end, 0)
 
 
-def prepare(chosen, pool, queries, key_up):
-    n = chosen.shape[0]
+def prepare(which, table, pool, queries, key_up):
+    n = which.shape[0]
     rows, heads, width = queries.shape
     nope, rank = key_up.shape[1:]
+    page, latent = pool.shape[1:]
     vmem = pl.BlockSpec(memory_space=pltpu.VMEM)
+    smem = pl.BlockSpec(memory_space=pltpu.SMEM)
+    hbm = pl.BlockSpec(memory_space=pl.ANY)
+    tall = page * latent // 128
+    dma = pltpu.SemaphoreType.DMA
     return pl.pallas_call(
         prepare_kernel,
-        in_specs=[pl.BlockSpec(memory_space=pltpu.SMEM), pl.BlockSpec(memory_space=pl.ANY), vmem, vmem],
-        out_specs=[vmem, vmem],
+        in_specs=[smem, smem, hbm, vmem, hbm],
+        out_specs=[hbm, vmem],
         out_shape=[
-            jax.ShapeDtypeStruct((n, *pool.shape[1:]), pool.dtype),
+            jax.ShapeDtypeStruct((n, tall, 128), pool.dtype),
             jax.ShapeDtypeStruct((rows * heads, rank + width - nope), queries.dtype),
         ],
         scratch_shapes=[
-            pltpu.SemaphoreType.DMA((n,)),
+            pltpu.VMEM((n, page, latent), pool.dtype),
+            pltpu.VMEM((n, tall, 128), pool.dtype),
+            pltpu.VMEM(key_up.shape, key_up.dtype),
+            dma((n,)),
+            dma((n,)),
+            dma((1,)),
             pltpu.VMEM((rows * heads, nope), jnp.float32),
             pltpu.VMEM((rank // 128, rows * heads, 128), jnp.float32),
         ],
         compiler_params=pltpu.CompilerParams(vmem_limit_bytes=56 * MIB),
-    )(chosen, pool, queries, key_up)
+    )(which, table, pool, queries, key_up)
 
 
 def exchange_kernel(pages, q_own, keys, q_all, q_s, page_s, p_send, p_recv, z_send, z_recv, own_sem):
@@ -174,50 +205,61 @@
     )(pages, q_own)
 
 
-def attend_kernel(scale, lengths, starts, place, q, keys, acc, stats, q_s, k_s, acc_s, st_s, m_s, l_s, k_sem, q_sem, o_sem):
-    member = place[0]
-    requests = lengths.shape[0]
-    slots, page, latent = keys.shape
+def attend_kernel(scale, requests, lengths, starts, q, keys, acc, stats, q_s, k_s, acc_s, st_s, m_s, l_s, k_sem, q_sem, o_sem):
+    member = lax.axis_index("head")
+    base = lax.axis_index("xfer") * requests
+    slots = keys.shape[0]
+    latent, rank = q.shape[2], acc.shape[2]
+    page = keys.shape[1] * 128 // latent
     rows = q.shape[1] // requests
     many = q.shape[0] * rows
-    rank = acc.shape[2]
-    width = BLOCK // page
+    more = k_s.shape[0] - slots
     loads = [
         pltpu.make_async_copy(keys, k_s.at[pl.ds(0, slots)], k_sem.at[0]),
-        pltpu.make_async_copy(keys.at[pl.ds(0, width)], k_s.at[pl.ds(slots, width)], k_sem.at[1]),
+        pltpu.make_async_copy(keys.at[pl.ds(0, more)], k_s.at[pl.ds(slots, more)], k_sem.at[1]),
     ]
     q_loads = [
         pltpu.make_async_copy(q.at[:, pl.ds(r * rows, rows)], q_s.at[r], q_sem.at[r]) for r in range(requests)
     ]
     for c in loads + q_loads:
         c.start()
-    lane = lax.broadcasted_iota(jnp.int32, (1, BLOCK), 1)
     odd = lax.broadcasted_iota(jnp.int32, (many, 128), 1) % 2
     for c in loads:
         c.wait()
     stores = []
     for r in range(requests):
-        length, start = lengths[r], starts[r]
+        length, start = lengths[base + r], starts[base + r]
         pages = (length + page - 1) // page
         skip = (member - start) & 7
         slot = ((start + skip) & 255) >> 3
         count = jnp.maximum(pages - skip + 7, 0) >> 3
         q_loads[r].wait()
 
-        def window(i):
-            first = (slot + i * width) & (slots - 1)
-            k = k_s[pl.ds(first, width)].reshape(BLOCK, latent)
+        def window(nth, size):
+            k = k_s[pl.ds((slot + nth) & (slots - 1), size)]
+            columns = [k[:, i * page : (i + 1) * page].reshape(size * page, 128) for i in range(rank // 128)]
+            wide = jnp.concatenate(columns, axis=1)
+            folded = k[:, rank // 128 * page :]
+            narrow = jnp.concatenate([folded[:, :, : latent - rank], folded[:, :, latent - rank :]], axis=1)
+            mine = q_s[r].reshape(many, latent)
             s = lax.dot_general(
-                q_s[r].reshape(many, latent), k, (((1,), (1,)), ((), ())), preferred_element_type=jnp.float32
+                mine[:, :rank], wide, (((1,), (1,)), ((), ())), preferred_element_type=jnp.float32
             )
-            nth = i * width + lane // page
-            seen = (nth < count) & ((skip + nth * 8) * page + lane % page < length)
-            return jnp.where(seen, s * scale, LOW), seen, k[:, :rank]
+            s += lax.dot_general(
+                mine[:, rank:],
+                narrow.reshape(size * page, latent - rank),
+                (((1,), (1,)), ((), ())),
+                preferred_element_type=jnp.float32,
+            )
+            lane = lax.broadcasted_iota(jnp.int32, (1, size * page), 1)
+            at = nth + lane // page
+            seen = (at < count) & ((skip + at * 8) * page + lane % page < length)
+            return jnp.where(seen, s * scale, LOW), seen, wide
 
         def weigh(w, v):
             return jnp.dot(w.astype(jnp.bfloat16), v, preferred_element_type=jnp.float32)
 
-        s, seen, v = window(0)
+        s, seen, v = window(0, FIRST)
         m = jnp.max(s, axis=1, keepdims=True)
         w = jnp.where(seen, jnp.exp(s - m), 0.0)
         m_s[...] = jnp.broadcast_to(m, m_s.shape)
@@ -225,7 +267,7 @@
         acc_s[r] = weigh(w, v).reshape(acc_s.shape[1:])
 
         def step(i, c):
-            s, _, v = window(i)
+            s, _, v = window(FIRST + i * NEXT, NEXT)
             m_old = m_s[:, :1]
             m_new = jnp.maximum(m_old, jnp.max(s, axis=1, keepdims=True))
             keep = jnp.exp(m_old - m_new)
@@ -236,7 +278,7 @@
             acc_s[r] = (old * keep + weigh(w, v)).reshape(acc_s.shape[1:])
             return c
 
-        lax.fori_loop(1, (count + width - 1) // width, step, 0)
+        lax.fori_loop(0, (jnp.maximum(count - FIRST, 0) + NEXT - 1) // NEXT, step, 0)
         st_s[r] = jnp.where(odd == 0, m_s[...], l_s[...]).reshape(st_s.shape[1:])
         part = pl.ds(r * rows, rows)
         stores += [
@@ -249,17 +291,17 @@
         c.wait()
 
 
-def attend(lengths, starts, place, q, keys, rank, scale):
+def attend(lengths, starts, q, keys, requests, rank, scale):
     smem = pl.BlockSpec(memory_space=pltpu.SMEM)
     hbm = pl.BlockSpec(memory_space=pl.ANY)
-    requests = lengths.shape[0]
     chunks, rows = q.shape[0], q.shape[1] // requests
     many = chunks * rows
-    slots, page, latent = keys.shape
+    slots, tall = keys.shape[:2]
+    latent = q.shape[2]
     dma = pltpu.SemaphoreType.DMA
     return pl.pallas_call(
-        functools.partial(attend_kernel, scale),
-        in_specs=[smem, smem, smem, hbm, hbm],
+        functools.partial(attend_kernel, scale, requests),
+        in_specs=[smem, smem, hbm, hbm],
         out_specs=[hbm, hbm],
         out_shape=[
             jax.ShapeDtypeStruct((*q.shape[:2], rank), jnp.float32),
@@ -267,7 +309,7 @@
         ],
         scratch_shapes=[
             pltpu.VMEM((requests, chunks, rows, latent), q.dtype),
-            pltpu.VMEM((slots + BLOCK // page, page, latent), keys.dtype),
+            pltpu.VMEM((slots + NEXT, tall, 128), keys.dtype),
             pltpu.VMEM((requests, chunks, rows, rank), jnp.float32),
             pltpu.VMEM((requests, chunks, rows, 128), jnp.float32),
             pltpu.VMEM((many, 128), jnp.float32),
@@ -277,7 +319,7 @@
             dma((2, requests)),
         ],
         compiler_params=pltpu.CompilerParams(vmem_limit_bytes=56 * MIB),
-    )(lengths, starts, place, q, keys)
+    )(lengths, starts, q, keys)
 
 
 def combine(m_a, l_a, acc_a, m_b, l_b, acc_b):
@@ -547,35 +589,20 @@
 ):
     owners = lax.axis_size("xfer")
     groups = lax.axis_size("head")
-    devices = owners * groups
-    owner_idx = lax.axis_index("xfer")
-    member = lax.axis_index("head")
-    local_device = owner_idx * groups + member
-    page_len = kv_pool.shape[1]
     latent = kv_pool.shape[2]
     lat_rank = value_up.shape[1]
-    per_owner = lengths.shape[0] // owners
-    table_width = page_table.shape[1]
     row_count, heads = queries.shape[:2]
     score_scale = queries.shape[2] ** (-0.5)
-    page_counts = (lengths + page_len - 1) // page_len
-    column = jnp.arange(table_width, dtype=jnp.int32)
-    located = ((start_device[:, None] + column[None, :]) % devices == local_device) & (
-        column[None, :] < page_counts[:, None]
-    )
-    chosen = (
-        jnp.sum(jnp.where(located, page_table, 0), axis=1).reshape(owners, per_owner).sum(axis=1)
-    )
-    first_req = owner_idx * per_owner
-    my_lengths = lax.dynamic_slice_in_dim(lengths, first_req, per_owner, 0)
-    my_starts = lax.dynamic_slice_in_dim(start_device, first_req, per_owner, 0)
-    pages, q_own = prepare(chosen, kv_pool, queries, key_up)
-    arrived, every = exchange(pages, q_own.reshape(2, row_count * heads // 2, latent), groups)
-    every = every.reshape(groups * 2, row_count * heads // 2, latent)
-    acc, stats = attend(
-        my_lengths, my_starts, member.reshape(1), every, arrived,
-        lat_rank, score_scale,
-    )
+    half_rows = row_count * heads // 2
+    device = lax.axis_index("xfer") * groups + lax.axis_index("head")
+    nth = (device - start_device) % (owners * groups)
+    flat = jnp.arange(lengths.shape[0], dtype=jnp.int32) * page_table.shape[1] + nth
+    here = nth * kv_pool.shape[1] < lengths
+    which = jnp.where(here, flat, 0).reshape(owners, -1).sum(axis=1)
+    pages, q_own = prepare(which, page_table, kv_pool, queries, key_up)
+    keys, every = exchange(pages, q_own.reshape(2, half_rows, latent), groups)
+    every = every.reshape(groups * 2, half_rows, latent)
+    acc, stats = attend(lengths, start_device, every, keys, lengths.shape[0] // owners, lat_rank, score_scale)
     return finish(acc, stats, q_own, new_latent, value_up, out_proj.T, owners, groups, score_scale)
 
 

time: 121 us -> 120 us (level)
  Pallas kernels: 114 us -> 117 us
  local copies, waits for them, and re-layouts: 3.98 us -> 1.46 us
  other arithmetic: 2.58 us -> 1.35 us
    pallas_call x2, Pallas kernels: 16.1 us -> 22.5 us  [the longest x1 11.8 us: attend(): pl.pallas_call(functools.partial(attend_kernel, scale, requests), in_spec...]
    pallas_call x1, Pallas kernels: 55.8 us -> 52.6 us  [finish(): pl.pallas_call(functools.partial(finish_kernel, scale), in_specs=[pl.Bloc...]
    dynamic_slice x2 -> x0, local copies, waits for them, and re-layouts: 2.52 us -> none  [the longest x1 1.26 us: body(): my_starts = lax.dynamic_slice_in_dim(start_device, first_req, per_owner, 0)]
    reduce_sum x2 -> x1, other arithmetic: 1.9 us -> 0.64 us  [body(): which = jnp.where(here, flat, 0).reshape(owners, -1).sum(axis=1)]
where the time goes in v6:
time: 120 us
  Pallas kernels  117 us (98%)
  local copies, waits for them, and re-layouts  1.46 us (1%)
  other arithmetic  1.35 us (1%)
    pallas_call x1, Pallas kernels, finish(): pl.pallas_call(functools.partial(finish_kernel, scale), in_specs=[pl.Bloc...  52.6 us
    pallas_call x1, Pallas kernels, exchange(): pl.pallas_call(exchange_kernel, in_specs=[hbm, hbm], out_specs=[hbm, hbm]...  41.6 us
    pallas_call x1, Pallas kernels, attend(): pl.pallas_call(functools.partial(attend_kernel, scale, requests), in_spec...  11.8 us
    pallas_call x1, Pallas kernels, prepare(): pl.pallas_call(prepare_kernel, in_specs=[smem, smem, hbm, vmem, hbm], out...  10.7 us

profile of v6, /device:TPU:1, one launch (start us, length us, event | category | flops | bytes accessed | tf_op | source)
XLA Modules:
  0.0 119.6 jit_solution(14689118817156430413)
XLA Ops:
  0.0 0.7 compare_select_fusion.2
  0.7 0.1 reshape.9
  0.8 0.6 reduce_sum.9.which
  1.4 10.7 %shard_map.91 = (bf16[32,288,128]{2,1,0:T(8,128)(2,1)}, bf16[256,576]{1,0:T(8,128)(2,1)}) custom-call(s32[32]{0:T(128)} %reduce_sum.9.which, s32[256,256]{1,0:T(8,128)} %table.1, bf16[32,64,576]{2,1,0:T(8,128)(2,1)} %pool.1, bf16[16,16,192]{2,1,0:T(8,128)(2,1)} %queries.1, bf16[16,128,512]{2,1,0:T(8,128)(2,1)} %key_up_h.1), custom_call_target="tpu_custom_call" | custom-call | tf_op jit(solution)/shard_map/pallas_call | solution.py:85
  12.1 41.6 %shard_map.92 = (bf16[32,288,128]{2,1,0:T(8,128)(2,1)}, bf16[8,2,128,576]{3,2,1,0:T(8,128)(2,1)}) custom-call(bf16[32,288,128]{2,1,0:T(8,128)(2,1)} %get-tuple-element.11.pages, bf16[2,128,576]{2,1,0:T(8,128)(2,1)} %bitcast.4), custom_call_target="tpu_custom_call" | custom-call | tf_op jit(solution)/shard_map/pallas_call | solution.py:185
  53.7 11.8 %shard_map.93 = (f32[16,128,512]{2,1,0:T(8,128)}, f32[16,128,128]{2,1,0:T(8,128)}) custom-call(s32[256]{0:T(256)} %lengths.1, s32[256]{0:T(256)} %starts.1, bf16[16,128,576]{2,1,0:T(8,128)(2,1)} %bitcast.3, bf16[32,288,128]{2,1,0:T(8,128)(2,1)} %get-tuple-element.14.keys), custom_call_target="tpu_custom_call" | custom-call | tf_op jit(solution)/shard_map/pallas_call | solution.py:302
  65.6 52.6 %shard_map.94 = bf16[64,224]{1,0:T(8,128)(2,1)} custom-call(f32[16,128,512]{2,1,0:T(8,128)} %get-tuple-element.15.acc_h, f32[16,128,128]{2,1,0:T(8,128)} %get-tuple-element.16.stats_h, bf16[256,576]{1,0:T(8,128)(2,1)} %get-tuple-element.12.q_own_h, bf16[16,576]{1,0:T(8,128)(2,1)} %fresh_h.1, bf16[16,512,128]{2,1,0:T(8,128)(2,1)} %value_up_h.1, ...), custom_call_target="tpu_custom_call" | custom-call | tf_op jit(solution)/shard_map/pallas_call | solution.py:556
  118.2 1.4 %copy.11 = bf16[64,224]{1,0:T(8,128)(2,1)} copy(bf16[64,224]{1,0:T(8,128)(2,1)} %shard_map.94) | data formatting | bytes 57344

commit v7 on v6

--- a/solution.py
+++ b/solution.py
@@ -11,6 +11,7 @@
 STEPS = 2
 LOW = -1e30
 FIRST, NEXT = 4, 8
+TOGETHER = 4
 MIB = 1024 * 1024
 
 
@@ -18,8 +19,7 @@
 OFFSETS = tuple((*d, 0) for d in FAR) + tuple((*d, 1) for d in FAR) + ((0, 0, 1),)
 
 
-def prepare_kernel(which, table, pool, queries, key_up_h, pages, q_own, raw, packed, key_up, sems, out_sems, up_sem, nope_s, wide_s):
-    shift = table.shape[1]
+def prepare_kernel(chosen, pool, queries, key_up_h, pages, q_own, raw, packed, key_up, sems, out_sems, up_sem, nope_s, wide_s):
     load_up = pltpu.make_async_copy(key_up_h, key_up, up_sem.at[0])
 
     def fetch(o, slot):
@@ -29,8 +29,7 @@
         return pltpu.make_async_copy(packed.at[o], pages.at[o], out_sems.at[o])
 
     def begin(o, c):
-        e = which[o]
-        fetch(o, table[e // shift, e % shift]).start()
+        fetch(o, chosen[o]).start()
         return c
 
     page = pool.shape[1]
@@ -72,8 +71,8 @@
     lax.fori_loop(0, pages.shape[0], end, 0)
 
 
-def prepare(which, table, pool, queries, key_up):
-    n = which.shape[0]
+def prepare(chosen, pool, queries, key_up):
+    n = chosen.shape[0]
     rows, heads, width = queries.shape
     nope, rank = key_up.shape[1:]
     page, latent = pool.shape[1:]
@@ -84,7 +83,7 @@
     dma = pltpu.SemaphoreType.DMA
     return pl.pallas_call(
         prepare_kernel,
-        in_specs=[smem, smem, hbm, vmem, hbm],
+        in_specs=[smem, hbm, vmem, hbm],
         out_specs=[hbm, vmem],
         out_shape=[
             jax.ShapeDtypeStruct((n, tall, 128), pool.dtype),
@@ -101,7 +100,7 @@
             pltpu.VMEM((rank // 128, rows * heads, 128), jnp.float32),
         ],
         compiler_params=pltpu.CompilerParams(vmem_limit_bytes=56 * MIB),
-    )(which, table, pool, queries, key_up)
+    )(chosen, pool, queries, key_up)
 
 
 def exchange_kernel(pages, q_own, keys, q_all, q_s, page_s, p_send, p_recv, z_send, z_recv, own_sem):
@@ -205,7 +204,7 @@
     )(pages, q_own)
 
 
-def attend_kernel(scale, requests, lengths, starts, q, keys, acc, stats, q_s, k_s, acc_s, st_s, m_s, l_s, k_sem, q_sem, o_sem):
+def attend_kernel(scale, requests, lengths, starts, q, keys, acc, stats, q_s, k_s, acc_s, st_s, k_sem, q_sem, o_sem):
     member = lax.axis_index("head")
     base = lax.axis_index("xfer") * requests
     slots = keys.shape[0]
@@ -224,69 +223,82 @@
     for c in loads + q_loads:
         c.start()
     odd = lax.broadcasted_iota(jnp.int32, (many, 128), 1) % 2
+    def weigh(w, v):
+        return jnp.dot(w.astype(jnp.bfloat16), v, preferred_element_type=jnp.float32)
+
+    def place(r):
+        length, start = lengths[base + r], starts[base + r]
+        skip = (member - start) & 7
+        slot = ((start + skip) & 255) >> 3
+        count = jnp.maximum((length + page - 1) // page - skip + 7, 0) >> 3
+        return length, skip, slot, count
+
+    def window(r, where, nth, size):
+        length, skip, slot, count = where
+        k = k_s[pl.ds((slot + nth) & (slots - 1), size)]
+        columns = [k[:, i * page : (i + 1) * page].reshape(size * page, 128) for i in range(rank // 128)]
+        wide = jnp.concatenate(columns, axis=1)
+        folded = k[:, rank // 128 * page :]
+        narrow = jnp.concatenate([folded[:, :, : latent - rank], folded[:, :, latent - rank :]], axis=1)
+        mine = q_s[r].reshape(many, latent)
+        s = lax.dot_general(
+            mine[:, :rank], wide, (((1,), (1,)), ((), ())), preferred_element_type=jnp.float32
+        )
+        s += lax.dot_general(
+            mine[:, rank:],
+            narrow.reshape(size * page, latent - rank),
+            (((1,), (1,)), ((), ())),
+            preferred_element_type=jnp.float32,
+        )
+        lane = lax.broadcasted_iota(jnp.int32, (1, size * page), 1)
+        at = nth + lane // page
+        seen = (at < count) & ((skip + at * 8) * page + lane % page < length)
+        return jnp.where(seen, s * scale, LOW), seen, wide
+
+    def begin(r):
+        s, seen, v = window(r, place(r), 0, FIRST)
+        m = jnp.max(s, axis=1, keepdims=True)
+        w = jnp.where(seen, jnp.exp(s - m), 0.0)
+        l = jnp.sum(w, axis=1, keepdims=True)
+        st_s[r] = jnp.where(odd == 0, m, l).reshape(st_s.shape[1:])
+        acc_s[r] = weigh(w, v).reshape(acc_s.shape[1:])
+
+    def go_on(r):
+        where = place(r)
+
+        def step(i, c):
+            s, _, v = window(r, where, FIRST + i * NEXT, NEXT)
+            old = st_s[r].reshape(many, 128)
+            m_old, l_old = old[:, 0:1], old[:, 1:2]
+            m = jnp.maximum(m_old, jnp.max(s, axis=1, keepdims=True))
+            keep = jnp.exp(m_old - m)
+            w = jnp.exp(s - m)
+            l = l_old * keep + jnp.sum(w, axis=1, keepdims=True)
+            st_s[r] = jnp.where(odd == 0, m, l).reshape(st_s.shape[1:])
+            old_acc = acc_s[r].reshape(many, rank)
+            acc_s[r] = (old_acc * keep + weigh(w, v)).reshape(acc_s.shape[1:])
+            return c
+
+        lax.fori_loop(0, (jnp.maximum(where[3] - FIRST, 0) + NEXT - 1) // NEXT, step, 0)
+
     for c in loads:
         c.wait()
     stores = []
-    for r in range(requests):
-        length, start = lengths[base + r], starts[base + r]
-        pages = (length + page - 1) // page
-        skip = (member - start) & 7
-        slot = ((start + skip) & 255) >> 3
-        count = jnp.maximum(pages - skip + 7, 0) >> 3
-        q_loads[r].wait()
-
-        def window(nth, size):
-            k = k_s[pl.ds((slot + nth) & (slots - 1), size)]
-            columns = [k[:, i * page : (i + 1) * page].reshape(size * page, 128) for i in range(rank // 128)]
-            wide = jnp.concatenate(columns, axis=1)
-            folded = k[:, rank // 128 * page :]
-            narrow = jnp.concatenate([folded[:, :, : latent - rank], folded[:, :, latent - rank :]], axis=1)
-            mine = q_s[r].reshape(many, latent)
-            s = lax.dot_general(
-                mine[:, :rank], wide, (((1,), (1,)), ((), ())), preferred_element_type=jnp.float32
-            )
-            s += lax.dot_general(
-                mine[:, rank:],
-                narrow.reshape(size * page, latent - rank),
-                (((1,), (1,)), ((), ())),
-                preferred_element_type=jnp.float32,
-            )
-            lane = lax.broadcasted_iota(jnp.int32, (1, size * page), 1)
-            at = nth + lane // page
-            seen = (at < count) & ((skip + at * 8) * page + lane % page < length)
-            return jnp.where(seen, s * scale, LOW), seen, wide
-
-        def weigh(w, v):
-            return jnp.dot(w.astype(jnp.bfloat16), v, preferred_element_type=jnp.float32)
-
-        s, seen, v = window(0, FIRST)
-        m = jnp.max(s, axis=1, keepdims=True)
-        w = jnp.where(seen, jnp.exp(s - m), 0.0)
-        m_s[...] = jnp.broadcast_to(m, m_s.shape)
-        l_s[...] = jnp.broadcast_to(jnp.sum(w, axis=1, keepdims=True), l_s.shape)
-        acc_s[r] = weigh(w, v).reshape(acc_s.shape[1:])
-
-        def step(i, c):
-            s, _, v = window(FIRST + i * NEXT, NEXT)
-            m_old = m_s[:, :1]
-            m_new = jnp.maximum(m_old, jnp.max(s, axis=1, keepdims=True))
-            keep = jnp.exp(m_old - m_new)
-            w = jnp.exp(s - m_new)
-            l_s[...] = l_s[...] * keep + jnp.sum(w, axis=1, keepdims=True)
-            m_s[...] = jnp.broadcast_to(m_new, m_s.shape)
-            old = acc_s[r].reshape(many, rank)
-            acc_s[r] = (old * keep + weigh(w, v)).reshape(acc_s.shape[1:])
-            return c
-
-        lax.fori_loop(0, (jnp.maximum(count - FIRST, 0) + NEXT - 1) // NEXT, step, 0)
-        st_s[r] = jnp.where(odd == 0, m_s[...], l_s[...]).reshape(st_s.shape[1:])
-        part = pl.ds(r * rows, rows)
-        stores += [
-            pltpu.make_async_copy(acc_s.at[r], acc.at[:, part], o_sem.at[0, r]),
-            pltpu.make_async_copy(st_s.at[r], stats.at[:, part], o_sem.at[1, r]),
-        ]
-        for c in stores[-2:]:
-            c.start()
+    for group in range(0, requests, TOGETHER):
+        members = range(group, group + TOGETHER)
+        for r in members:
+            q_loads[r].wait()
+        for r in members:
+            begin(r)
+        for r in members:
+            go_on(r)
+            part = pl.ds(r * rows, rows)
+            stores += [
+                pltpu.make_async_copy(acc_s.at[r], acc.at[:, part], o_sem.at[0, r]),
+                pltpu.make_async_copy(st_s.at[r], stats.at[:, part], o_sem.at[1, r]),
+            ]
+            for c in stores[-2:]:
+                c.start()
     for c in stores:
         c.wait()
 
@@ -295,7 +307,6 @@
     smem = pl.BlockSpec(memory_space=pltpu.SMEM)
     hbm = pl.BlockSpec(memory_space=pl.ANY)
     chunks, rows = q.shape[0], q.shape[1] // requests
-    many = chunks * rows
     slots, tall = keys.shape[:2]
     latent = q.shape[2]
     dma = pltpu.SemaphoreType.DMA
@@ -312,8 +323,6 @@
             pltpu.VMEM((slots + NEXT, tall, 128), keys.dtype),
             pltpu.VMEM((requests, chunks, rows, rank), jnp.float32),
             pltpu.VMEM((requests, chunks, rows, 128), jnp.float32),
-            pltpu.VMEM((many, 128), jnp.float32),
-            pltpu.VMEM((many, 128), jnp.float32),
             dma((2,)),
             dma((requests,)),
             dma((2, requests)),
@@ -596,10 +605,11 @@
     half_rows = row_count * heads // 2
     device = lax.axis_index("xfer") * groups + lax.axis_index("head")
     nth = (device - start_device) % (owners * groups)
-    flat = jnp.arange(lengths.shape[0], dtype=jnp.int32) * page_table.shape[1] + nth
     here = nth * kv_pool.shape[1] < lengths
-    which = jnp.where(here, flat, 0).reshape(owners, -1).sum(axis=1)
-    pages, q_own = prepare(which, page_table, kv_pool, queries, key_up)
+    column = jnp.arange(page_table.shape[1], dtype=jnp.int32)
+    picked = (column[None, :] == nth[:, None]) & here[:, None]
+    chosen = jnp.where(picked, page_table, 0).reshape(owners, -1, page_table.shape[1]).sum(axis=(1, 2))
+    pages, q_own = prepare(chosen, kv_pool, queries, key_up)
     keys, every = exchange(pages, q_own.reshape(2, half_rows, latent), groups)
     every = every.reshape(groups * 2, half_rows, latent)
     acc, stats = attend(lengths, start_device, every, keys, lengths.shape[0] // owners, lat_rank, score_scale)

time: 120 us -> 116 us (0.967)
  Pallas kernels: 117 us -> 112 us
    pallas_call x1, Pallas kernels: 10.7 us -> 6.87 us  [prepare(): pl.pallas_call(prepare_kernel, in_specs=[smem, hbm, vmem, hbm], out_specs...]
where the time goes in v7:
time: 116 us
  Pallas kernels  112 us (97%)
  other arithmetic  2.52 us (2%)
  local copies, waits for them, and re-layouts  1.45 us (1%)
    pallas_call x1, Pallas kernels, finish(): pl.pallas_call(functools.partial(finish_kernel, scale), in_specs=[pl.Bloc...  52.4 us
    pallas_call x1, Pallas kernels, exchange(): pl.pallas_call(exchange_kernel, in_specs=[hbm, hbm], out_specs=[hbm, hbm]...  41.3 us
    pallas_call x1, Pallas kernels, attend(): pl.pallas_call(functools.partial(attend_kernel, scale, requests), in_spec...  11.4 us
    pallas_call x1, Pallas kernels, prepare(): pl.pallas_call(prepare_kernel, in_specs=[smem, hbm, vmem, hbm], out_specs...  6.87 us

profile of v7, /device:TPU:1, one launch (start us, length us, event | category | flops | bytes accessed | tf_op | source)
XLA Modules:
  0.0 116.1 jit_solution(4175105336806197881)
XLA Ops:
  0.0 0.7 multiply_compare_fusion
  0.7 1.2 %select_reduce_fusion = s32[256]{0:T(256)S(1)} fusion(s32[256,256]{1,0:T(8,128)} %param.12, s32[256]{0:T(256)S(1)} %get-tuple-element.18, pred[256]{0:T(512)(128)(4,1)S(1)} %get-tuple-element.17), kind=kLoop, calls=%fused_computation | loop fusion | flops 261888 | bytes 264448 | tf_op jit(solution)/shard_map/reduce_sum | solution.py:611
  1.9 0.1 reduce_sum.14
  2.0 0.6 reduce_sum.18.chosen
  2.6 6.9 %shard_map.91 = (bf16[32,288,128]{2,1,0:T(8,128)(2,1)}, bf16[256,576]{1,0:T(8,128)(2,1)}) custom-call(s32[32]{0:T(128)} %reduce_sum.18.chosen, bf16[32,64,576]{2,1,0:T(8,128)(2,1)} %pool.1, bf16[16,16,192]{2,1,0:T(8,128)(2,1)} %queries.1, bf16[16,128,512]{2,1,0:T(8,128)(2,1)} %key_up_h.1), custom_call_target="tpu_custom_call" | custom-call | tf_op jit(solution)/shard_map/pallas_call | solution.py:84
  9.5 41.3 %shard_map.92 = (bf16[32,288,128]{2,1,0:T(8,128)(2,1)}, bf16[8,2,128,576]{3,2,1,0:T(8,128)(2,1)}) custom-call(bf16[32,288,128]{2,1,0:T(8,128)(2,1)} %get-tuple-element.11.pages, bf16[2,128,576]{2,1,0:T(8,128)(2,1)} %bitcast.4), custom_call_target="tpu_custom_call" | custom-call | tf_op jit(solution)/shard_map/pallas_call | solution.py:184
  50.8 11.4 %shard_map.93 = (f32[16,128,512]{2,1,0:T(8,128)}, f32[16,128,128]{2,1,0:T(8,128)}) custom-call(s32[256]{0:T(256)} %lengths.1, s32[256]{0:T(256)} %starts.1, bf16[16,128,576]{2,1,0:T(8,128)(2,1)} %bitcast.3, bf16[32,288,128]{2,1,0:T(8,128)(2,1)} %get-tuple-element.14.keys), custom_call_target="tpu_custom_call" | custom-call | tf_op jit(solution)/shard_map/pallas_call | solution.py:313
  62.3 52.4 %shard_map.94 = bf16[64,224]{1,0:T(8,128)(2,1)} custom-call(f32[16,128,512]{2,1,0:T(8,128)} %get-tuple-element.15.acc_h, f32[16,128,128]{2,1,0:T(8,128)} %get-tuple-element.16.stats_h, bf16[256,576]{1,0:T(8,128)(2,1)} %get-tuple-element.12.q_own_h, bf16[16,576]{1,0:T(8,128)(2,1)} %fresh_h.1, bf16[16,512,128]{2,1,0:T(8,128)(2,1)} %value_up_h.1, ...), custom_call_target="tpu_custom_call" | custom-call | tf_op jit(solution)/shard_map/pallas_call | solution.py:565
  114.7 1.4 %copy.11 = bf16[64,224]{1,0:T(8,128)(2,1)} copy(bf16[64,224]{1,0:T(8,128)(2,1)} %shard_map.94) | data formatting | bytes 57344

commit v8 on v7

--- a/solution.py
+++ b/solution.py
@@ -10,8 +10,8 @@
 MESH = pl.DeviceIdType.MESH
 STEPS = 2
 LOW = -1e30
-FIRST, NEXT = 4, 8
-TOGETHER = 4
+FLOOR = -1e29
+BLOCK = 512
 MIB = 1024 * 1024
 
 
@@ -204,133 +204,6 @@
     )(pages, q_own)
 
 
-def attend_kernel(scale, requests, lengths, starts, q, keys, acc, stats, q_s, k_s, acc_s, st_s, k_sem, q_sem, o_sem):
-    member = lax.axis_index("head")
-    base = lax.axis_index("xfer") * requests
-    slots = keys.shape[0]
-    latent, rank = q.shape[2], acc.shape[2]
-    page = keys.shape[1] * 128 // latent
-    rows = q.shape[1] // requests
-    many = q.shape[0] * rows
-    more = k_s.shape[0] - slots
-    loads = [
-        pltpu.make_async_copy(keys, k_s.at[pl.ds(0, slots)], k_sem.at[0]),
-        pltpu.make_async_copy(keys.at[pl.ds(0, more)], k_s.at[pl.ds(slots, more)], k_sem.at[1]),
-    ]
-    q_loads = [
-        pltpu.make_async_copy(q.at[:, pl.ds(r * rows, rows)], q_s.at[r], q_sem.at[r]) for r in range(requests)
-    ]
-    for c in loads + q_loads:
-        c.start()
-    odd = lax.broadcasted_iota(jnp.int32, (many, 128), 1) % 2
-    def weigh(w, v):
-        return jnp.dot(w.astype(jnp.bfloat16), v, preferred_element_type=jnp.float32)
-
-    def place(r):
-        length, start = lengths[base + r], starts[base + r]
-        skip = (member - start) & 7
-        slot = ((start + skip) & 255) >> 3
-        count = jnp.maximum((length + page - 1) // page - skip + 7, 0) >> 3
-        return length, skip, slot, count
-
-    def window(r, where, nth, size):
-        length, skip, slot, count = where
-        k = k_s[pl.ds((slot + nth) & (slots - 1), size)]
-        columns = [k[:, i * page : (i + 1) * page].reshape(size * page, 128) for i in range(rank // 128)]
-        wide = jnp.concatenate(columns, axis=1)
-        folded = k[:, rank // 128 * page :]
-        narrow = jnp.concatenate([folded[:, :, : latent - rank], folded[:, :, latent - rank :]], axis=1)
-        mine = q_s[r].reshape(many, latent)
-        s = lax.dot_general(
-            mine[:, :rank], wide, (((1,), (1,)), ((), ())), preferred_element_type=jnp.float32
-        )
-        s += lax.dot_general(
-            mine[:, rank:],
-            narrow.reshape(size * page, latent - rank),
-            (((1,), (1,)), ((), ())),
-            preferred_element_type=jnp.float32,
-        )
-        lane = lax.broadcasted_iota(jnp.int32, (1, size * page), 1)
-        at = nth + lane // page
-        seen = (at < count) & ((skip + at * 8) * page + lane % page < length)
-        return jnp.where(seen, s * scale, LOW), seen, wide
-
-    def begin(r):
-        s, seen, v = window(r, place(r), 0, FIRST)
-        m = jnp.max(s, axis=1, keepdims=True)
-        w = jnp.where(seen, jnp.exp(s - m), 0.0)
-        l = jnp.sum(w, axis=1, keepdims=True)
-        st_s[r] = jnp.where(odd == 0, m, l).reshape(st_s.shape[1:])
-        acc_s[r] = weigh(w, v).reshape(acc_s.shape[1:])
-
-    def go_on(r):
-        where = place(r)
-
-        def step(i, c):
-            s, _, v = window(r, where, FIRST + i * NEXT, NEXT)
-            old = st_s[r].reshape(many, 128)
-            m_old, l_old = old[:, 0:1], old[:, 1:2]
-            m = jnp.maximum(m_old, jnp.max(s, axis=1, keepdims=True))
-            keep = jnp.exp(m_old - m)
-            w = jnp.exp(s - m)
-            l = l_old * keep + jnp.sum(w, axis=1, keepdims=True)
-            st_s[r] = jnp.where(odd == 0, m, l).reshape(st_s.shape[1:])
-            old_acc = acc_s[r].reshape(many, rank)
-            acc_s[r] = (old_acc * keep + weigh(w, v)).reshape(acc_s.shape[1:])
-            return c
-
-        lax.fori_loop(0, (jnp.maximum(where[3] - FIRST, 0) + NEXT - 1) // NEXT, step, 0)
-
-    for c in loads:
-        c.wait()
-    stores = []
-    for group in range(0, requests, TOGETHER):
-        members = range(group, group + TOGETHER)
-        for r in members:
-            q_loads[r].wait()
-        for r in members:
-            begin(r)
-        for r in members:
-            go_on(r)
-            part = pl.ds(r * rows, rows)
-            stores += [
-                pltpu.make_async_copy(acc_s.at[r], acc.at[:, part], o_sem.at[0, r]),
-                pltpu.make_async_copy(st_s.at[r], stats.at[:, part], o_sem.at[1, r]),
-            ]
-            for c in stores[-2:]:
-                c.start()
-    for c in stores:
-        c.wait()
-
-
-def attend(lengths, starts, q, keys, requests, rank, scale):
-    smem = pl.BlockSpec(memory_space=pltpu.SMEM)
-    hbm = pl.BlockSpec(memory_space=pl.ANY)
-    chunks, rows = q.shape[0], q.shape[1] // requests
-    slots, tall = keys.shape[:2]
-    latent = q.shape[2]
-    dma = pltpu.SemaphoreType.DMA
-    return pl.pallas_call(
-        functools.partial(attend_kernel, scale, requests),
-        in_specs=[smem, smem, hbm, hbm],
-        out_specs=[hbm, hbm],
-        out_shape=[
-            jax.ShapeDtypeStruct((*q.shape[:2], rank), jnp.float32),
-            jax.ShapeDtypeStruct((*q.shape[:2], 128), jnp.float32),
-        ],
-        scratch_shapes=[
-            pltpu.VMEM((requests, chunks, rows, latent), q.dtype),
-            pltpu.VMEM((slots + NEXT, tall, 128), keys.dtype),
-            pltpu.VMEM((requests, chunks, rows, rank), jnp.float32),
-            pltpu.VMEM((requests, chunks, rows, 128), jnp.float32),
-            dma((2,)),
-            dma((requests,)),
-            dma((2, requests)),
-        ],
-        compiler_params=pltpu.CompilerParams(vmem_limit_bytes=56 * MIB),
-    )(lengths, starts, q, keys)
-
-
 def combine(m_a, l_a, acc_a, m_b, l_b, acc_b):
     m = jnp.maximum(m_a, m_b)
     f_a, f_b = jnp.exp(m_a - m), jnp.exp(m_b - m)
@@ -338,8 +211,8 @@
 
 
 def finish_kernel(
-    scale, acc_h, stats_h, q_own_h, fresh_h, value_up_h, out_proj_h, out,
-    acc, stats, q_own, fresh, value_up, out_proj, acc_sem, in_sem, sent, sent_st, got, got_st, own, own_st, held, share, parts, z_send, z_recv, x_send, x_recv, o_send, o_recv,
+    scale, lengths, starts, keys_h, q_h, fresh_h, value_up_h, out_proj_h, out,
+    packed, q, fresh, value_up, out_proj, in_sem, wide, narrow, bias, s_s, w_s, acc, stats, sent, sent_st, got, got_st, own, own_st, held, share, parts, z_send, z_recv, x_send, x_recv, o_send, o_recv,
 ):
     z = lax.axis_index("head")
     xfer = lax.axis_index("xfer")
@@ -350,18 +223,10 @@
     loads = [
         pltpu.make_async_copy(src, dst, in_sem.at[i])
         for i, (src, dst) in enumerate(
-            ((stats_h, stats), (q_own_h, q_own), (fresh_h, fresh), (value_up_h, value_up), (out_proj_h, out_proj))
+            ((keys_h, packed), (q_h, q), (fresh_h, fresh), (value_up_h, value_up), (out_proj_h, out_proj))
         )
     ]
-
-    def load_acc(at):
-        return pltpu.make_async_copy(acc_h.at[at], acc.at[at], acc_sem.at[at])
-
-    loads[0].start()
-    for distance in (4, 3, 5, 0, 2, 6, 1, 7):
-        for half in (0, 1):
-            load_acc(lax.rem(z + distance, groups) * 2 + half).start()
-    for c in loads[1:]:
+    for c in loads:
         c.start()
 
     def near(dx, dy, flip):
@@ -410,7 +275,6 @@
     def send_on(way, half, hop):
         at = index_of(way, half, 4 - hop)
         mine = stats[at]
-        load_acc(at).wait()
         if hop == (0 if way == half else 1):
             sent[way, half, hop] = acc[at].astype(jnp.bfloat16)
             sent_st[way, half, hop] = mine.T[0:8]
@@ -423,10 +287,9 @@
             started.append(c)
 
     def take_fresh(half):
-        rows = slice(half * half_rows, (half + 1) * half_rows)
         s = (
             lax.dot_general(
-                q_own[rows, :], fresh[...], (((1,), (1,)), ((), ())), preferred_element_type=jnp.float32
+                q[z * 2 + half], fresh[...], (((1,), (1,)), ((), ())), preferred_element_type=jnp.float32
             )
             * scale
         )
@@ -439,26 +302,84 @@
         more = jnp.dot(w.astype(jnp.bfloat16), fresh[:, :rank], preferred_element_type=jnp.float32)
         at = z * 2 + half
         mine = stats[at]
-        load_acc(at).wait()
         m, l, total = combine(m, l, more, mine[:, 0:1], mine[:, 1:2], acc[at])
         own[half] = total
         own_st[half] = jnp.where(odd == 0, m, l)
 
+    requests = lengths.shape[0] // 32
+    page = packed.shape[1] * 128 // q.shape[2]
+    keys = wide.shape[0]
+    lane = lax.broadcasted_iota(jnp.int32, (1, keys), 1)
+
+    def unpack():
+        pages = packed.shape[0]
+        for i in range(rank // 128):
+            wide[:, i * 128 : (i + 1) * 128] = packed[:, i * page : (i + 1) * page].reshape(keys, 128)
+        folded = packed[:, rank // 128 * page :]
+        thin = narrow.shape[1]
+        both = jnp.concatenate([folded[:, :, :thin], folded[:, :, thin:]], axis=1)
+        narrow[...] = both.reshape(keys, thin)
+        for r in range(requests):
+            length, start = lengths[xfer * requests + r], starts[xfer * requests + r]
+            at = (lane // page * groups + z - start) & (pages * groups - 1)
+            seen = at * page + lane % page < length
+            many = half_rows // requests
+            bias[r * many : (r + 1) * many] = jnp.broadcast_to(jnp.where(seen, 0.0, LOW), (many, keys))
+
+    def attend(distance):
+        d = lax.rem(z + distance, groups)
+        mine = q[pl.ds(d * 2, 2)].reshape(2 * half_rows, q.shape[2])
+        top = None
+        for b in range(0, keys, BLOCK):
+            part = slice(b, b + BLOCK)
+            s = lax.dot_general(
+                mine[:, :rank], wide[part], (((1,), (1,)), ((), ())), preferred_element_type=jnp.float32
+            )
+            s += lax.dot_general(
+                mine[:, rank:], narrow[part], (((1,), (1,)), ((), ())), preferred_element_type=jnp.float32
+            )
+            s = (s * scale).reshape(2, half_rows, BLOCK) + bias[:, part][None]
+            s = s.reshape(2 * half_rows, BLOCK)
+            s_s[:, part] = s
+            most = jnp.max(s, axis=1, keepdims=True)
+            top = most if top is None else jnp.maximum(top, most)
+        top = jnp.maximum(top, FLOOR)
+        total = None
+        for b in range(0, keys, BLOCK):
+            part = slice(b, b + BLOCK)
+            w = jnp.exp(s_s[:, part] - top)
+            w_s[:, part] = w.astype(jnp.bfloat16)
+            more = jnp.sum(w, axis=1, keepdims=True)
+            total = more if total is None else total + more
+        summed = jnp.dot(w_s[...], wide[...], preferred_element_type=jnp.float32)
+        acc[pl.ds(d * 2, 2)] = summed.reshape(2, half_rows, rank)
+        both = jnp.where(lax.broadcasted_iota(jnp.int32, (2 * half_rows, 128), 1) % 2 == 0, top, total)
+        stats[pl.ds(d * 2, 2)] = both.reshape(2, half_rows, 128)
+
     loads[0].wait()
+    unpack()
+    loads[1].wait()
+    attend(4)
     send_on(0, 0, 0)
     send_on(1, 1, 0)
-    send_on(0, 1, 1)
-    send_on(1, 0, 1)
-    loads[1].wait()
+    for hop in (1, 2, 3):
+        attend(4 - hop)
+        if hop == 1:
+            send_on(0, 1, 1)
+            attend(4 + hop)
+            send_on(1, 0, 1)
+            send_on(0, 0, 1)
+            send_on(1, 1, 1)
+        else:
+            send_on(0, 1, hop)
+            send_on(0, 0, hop)
+            attend(4 + hop)
+            send_on(1, 0, hop)
+            send_on(1, 1, hop)
+    attend(0)
     loads[2].wait()
     take_fresh(0)
     take_fresh(1)
-    for hop in (1, 2, 3):
-        send_on(0, 0, hop)
-        send_on(1, 1, hop)
-        if hop < 3:
-            send_on(0, 1, hop + 1)
-            send_on(1, 0, hop + 1)
 
     def spread(half, kind, a, b, block, to):
         return pltpu.make_async_remote_copy(
@@ -554,23 +475,32 @@
         c.wait_send()
 
 
-def finish(acc, stats, q_own, fresh, value_up, out_proj, owners, groups, scale):
+def finish(lengths, starts, keys, q, fresh, value_up, out_proj, owners, groups, scale):
     vmem = pl.BlockSpec(memory_space=pltpu.VMEM)
-    operands = (acc, stats, q_own, fresh, value_up, out_proj)
+    operands = (keys, q, fresh, value_up, out_proj)
+    smem = pl.BlockSpec(memory_space=pltpu.SMEM)
     rows = fresh.shape[0]
-    half_rows, rank = acc.shape[1:]
+    half_rows, latent = q.shape[1:]
+    rank = value_up.shape[1]
+    tokens = keys.shape[0] * keys.shape[1] * 128 // latent
     width, depth = out_proj.shape
     piece = owners * rows // groups
     dma = pltpu.SemaphoreType.DMA
     return pl.pallas_call(
         functools.partial(finish_kernel, scale),
-        in_specs=[pl.BlockSpec(memory_space=pl.ANY)] * 6,
+        in_specs=[smem, smem] + [pl.BlockSpec(memory_space=pl.ANY)] * 5,
         out_specs=vmem,
         out_shape=jax.ShapeDtypeStruct((piece, width), jnp.bfloat16),
         scratch_shapes=[
             *(pltpu.VMEM(a.shape, a.dtype) for a in operands),
-            dma((2 * groups,)),
             dma((5,)),
+            pltpu.VMEM((tokens, rank), jnp.bfloat16),
+            pltpu.VMEM((tokens, latent - rank), jnp.bfloat16),
+            pltpu.VMEM((half_rows, tokens), jnp.float32),
+            pltpu.VMEM((2 * half_rows, tokens), jnp.float32),
+            pltpu.VMEM((2 * half_rows, tokens), jnp.bfloat16),
+            pltpu.VMEM((2 * groups, half_rows, rank), jnp.float32),
+            pltpu.VMEM((2 * groups, half_rows, 128), jnp.float32),
             pltpu.VMEM((2, 2, 4, half_rows, rank), jnp.bfloat16),
             pltpu.VMEM((2, 2, 4, 8, 128), jnp.float32),
             pltpu.VMEM((2, 2, 4, half_rows, rank), jnp.bfloat16),
@@ -590,7 +520,7 @@
         compiler_params=pltpu.CompilerParams(
             collective_id=1, has_side_effects=True, vmem_limit_bytes=56 * MIB
         ),
-    )(*operands)
+    )(lengths, starts, *operands)
 
 
 def body(
@@ -612,8 +542,9 @@
     pages, q_own = prepare(chosen, kv_pool, queries, key_up)
     keys, every = exchange(pages, q_own.reshape(2, half_rows, latent), groups)
     every = every.reshape(groups * 2, half_rows, latent)
-    acc, stats = attend(lengths, start_device, every, keys, lengths.shape[0] // owners, lat_rank, score_scale)
-    return finish(acc, stats, q_own, new_latent, value_up, out_proj.T, owners, groups, score_scale)
+    return finish(
+        lengths, start_device, keys, every, new_latent, value_up, out_proj.T, owners, groups, score_scale
+    )
 
 
 def solution(mesh):

time: 116 us -> 111 us (0.957)
  Pallas kernels: 112 us -> 107 us
    pallas_call x2 -> x1, Pallas kernels: 63.9 us -> 58.2 us  [finish(): pl.pallas_call(functools.partial(finish_kernel, scale), in_specs=[smem, s...]
where the time goes in v8:
time: 111 us
  Pallas kernels  107 us (96%)
  other arithmetic  2.52 us (2%)
  local copies, waits for them, and re-layouts  1.45 us (1%)
    pallas_call x1, Pallas kernels, finish(): pl.pallas_call(functools.partial(finish_kernel, scale), in_specs=[smem, s...  58.2 us
    pallas_call x1, Pallas kernels, exchange(): pl.pallas_call(exchange_kernel, in_specs=[hbm, hbm], out_specs=[hbm, hbm]...  41.8 us
    pallas_call x1, Pallas kernels, prepare(): pl.pallas_call(prepare_kernel, in_specs=[smem, hbm, vmem, hbm], out_specs...  6.7 us

profile of v8, /device:TPU:1, one launch (start us, length us, event | category | flops | bytes accessed | tf_op | source)
XLA Modules:
  0.0 110.7 jit_solution(7156155095904504778)
XLA Ops:
  0.0 0.7 multiply_compare_fusion
  0.7 1.2 %select_reduce_fusion = s32[256]{0:T(256)S(1)} fusion(s32[256,256]{1,0:T(8,128)} %param.12, s32[256]{0:T(256)S(1)} %get-tuple-element.14, pred[256]{0:T(512)(128)(4,1)S(1)} %get-tuple-element.13), kind=kLoop, calls=%fused_computation | loop fusion | flops 261888 | bytes 264448 | tf_op jit(solution)/shard_map/reduce_sum | solution.py:541
  1.9 0.1 reduce_sum.14
  2.0 0.6 reduce_sum.18.chosen
  2.6 6.7 %shard_map.91 = (bf16[32,288,128]{2,1,0:T(8,128)(2,1)}, bf16[256,576]{1,0:T(8,128)(2,1)}) custom-call(s32[32]{0:T(128)} %reduce_sum.18.chosen, bf16[32,64,576]{2,1,0:T(8,128)(2,1)} %pool.1, bf16[16,16,192]{2,1,0:T(8,128)(2,1)} %queries.1, bf16[16,128,512]{2,1,0:T(8,128)(2,1)} %key_up_h.1), custom_call_target="tpu_custom_call" | custom-call | tf_op jit(solution)/shard_map/pallas_call | solution.py:84
  9.3 41.8 %shard_map.92 = (bf16[32,288,128]{2,1,0:T(8,128)(2,1)}, bf16[8,2,128,576]{3,2,1,0:T(8,128)(2,1)}) custom-call(bf16[32,288,128]{2,1,0:T(8,128)(2,1)} %get-tuple-element.9.pages, bf16[2,128,576]{2,1,0:T(8,128)(2,1)} %bitcast.5), custom_call_target="tpu_custom_call" | custom-call | tf_op jit(solution)/shard_map/pallas_call | solution.py:184
  51.1 58.2 %shard_map.93 = bf16[64,224]{1,0:T(8,128)(2,1)} custom-call(s32[256]{0:T(256)} %lengths.1, s32[256]{0:T(256)} %starts.1, bf16[32,288,128]{2,1,0:T(8,128)(2,1)} %get-tuple-element.11.keys_h, bf16[16,128,576]{2,1,0:T(8,128)(2,1)} %bitcast.3, bf16[16,576]{1,0:T(8,128)(2,1)} %fresh_h.1, bf16[16,512,128]{2,1,0:T(8,128)(2,1)} %value_up_h.1, bf16[224,2048]{1,0:T(8,128)(2,1)} %bitcast.4), custom_call_target="tpu_custom_call" | custom-call | tf_op jit(solution)/shard_map/pallas_call | solution.py:489
  109.3 1.4 %copy.11 = bf16[64,224]{1,0:T(8,128)(2,1)} copy(bf16[64,224]{1,0:T(8,128)(2,1)} %shard_map.93) | data formatting | bytes 57344

commit v9 on v8

--- a/solution.py
+++ b/solution.py
@@ -103,107 +103,6 @@
     )(chosen, pool, queries, key_up)
 
 
-def exchange_kernel(pages, q_own, keys, q_all, q_s, page_s, p_send, p_recv, z_send, z_recv, own_sem):
-    z = lax.axis_index("head")
-    xfer = lax.axis_index("xfer")
-    x, y, core = xfer // 8, (xfer // 2) % 4, xfer % 2
-    groups = q_all.shape[0]
-
-    def at(offset):
-        dx, dy, dc = offset
-        return (lax.rem(x + dx, 4) * 4 + lax.rem(y + dy, 4)) * 2 + lax.rem(core + dc, 2)
-
-    mine = [
-        pltpu.make_async_copy(q_own, q_s, own_sem.at[0]),
-        pltpu.make_async_copy(pages.at[xfer], page_s, own_sem.at[1]),
-    ]
-    for c in mine:
-        c.start()
-    right, left = (xfer, lax.rem(z + 1, groups)), (xfer, lax.rem(z + groups - 1, groups))
-    barrier = pltpu.get_barrier_semaphore()
-    peers = [right, left] + [(at(offset), z) for offset in OFFSETS]
-    for peer in peers:
-        pl.semaphore_signal(barrier, inc=1, device_id=peer, device_id_type=MESH)
-    pl.semaphore_wait(barrier, len(peers))
-
-    def hop(way, j):
-        block = lax.rem(z + groups - (j - 1), groups) if way == 0 else lax.rem(z + j - 1, groups)
-        src, dst = (q_s if j == 1 else q_all.at[block]), q_all.at[block]
-        if j == groups // 2:
-            src, dst = src.at[way], dst.at[way]
-        return pltpu.make_async_remote_copy(
-            src_ref=src,
-            dst_ref=dst,
-            send_sem=z_send.at[way, j],
-            recv_sem=z_recv.at[way, j],
-            device_id=right if way == 0 else left,
-            device_id_type=MESH,
-        )
-
-    def page(i, offset):
-        to = at(offset)
-        return pltpu.make_async_remote_copy(
-            src_ref=pages.at[to],
-            dst_ref=keys.at[xfer],
-            send_sem=p_send.at[i],
-            recv_sem=p_recv.at[i],
-            device_id=(to, z),
-            device_id_type=MESH,
-        )
-
-    hops = [hop(way, j) for j in range(1, groups // 2 + 1) for way in (0, 1)]
-    copies = [page(i, offset) for i, offset in enumerate(OFFSETS)]
-    for c in mine:
-        c.wait()
-    for c in hops[:2] + copies:
-        c.start()
-    mine = [
-        pltpu.make_async_copy(q_s, q_all.at[z], own_sem.at[2]),
-        pltpu.make_async_copy(page_s, keys.at[xfer], own_sem.at[3]),
-    ]
-    for c in mine:
-        c.start()
-    for j in range(1, groups // 2):
-        for way in (0, 1):
-            hops[(j - 1) * 2 + way].wait_recv()
-            hops[j * 2 + way].start()
-    for c in hops[-2:]:
-        c.wait_recv()
-    for c in copies:
-        c.wait_recv()
-    for c in mine:
-        c.wait()
-    for c in hops + copies:
-        c.wait_send()
-
-
-def exchange(pages, q_own, groups):
-    hbm = pl.BlockSpec(memory_space=pl.ANY)
-    dma = pltpu.SemaphoreType.DMA
-    n = pages.shape[0]
-    return pl.pallas_call(
-        exchange_kernel,
-        in_specs=[hbm, hbm],
-        out_specs=[hbm, hbm],
-        out_shape=[
-            jax.ShapeDtypeStruct(pages.shape, pages.dtype),
-            jax.ShapeDtypeStruct((groups, *q_own.shape), q_own.dtype),
-        ],
-        scratch_shapes=[
-            pltpu.VMEM(q_own.shape, q_own.dtype),
-            pltpu.VMEM(pages.shape[1:], pages.dtype),
-            dma((n,)),
-            dma((n,)),
-            dma((2, 8)),
-            dma((2, 8)),
-            dma((4,)),
-        ],
-        compiler_params=pltpu.CompilerParams(
-            collective_id=0, has_side_effects=True, vmem_limit_bytes=56 * MIB
-        ),
-    )(pages, q_own)
-
-
 def combine(m_a, l_a, acc_a, m_b, l_b, acc_b):
     m = jnp.maximum(m_a, m_b)
     f_a, f_b = jnp.exp(m_a - m), jnp.exp(m_b - m)
@@ -211,8 +110,9 @@
 
 
 def finish_kernel(
-    scale, lengths, starts, keys_h, q_h, fresh_h, value_up_h, out_proj_h, out,
+    scale, lengths, starts, pages_h, q_own_h, fresh_h, value_up_h, out_proj_h, out,
     packed, q, fresh, value_up, out_proj, in_sem, wide, narrow, bias, s_s, w_s, acc, stats, sent, sent_st, got, got_st, own, own_st, held, share, parts, z_send, z_recv, x_send, x_recv, o_send, o_recv,
+    p_send, p_recv, r_send, r_recv,
 ):
     z = lax.axis_index("head")
     xfer = lax.axis_index("xfer")
@@ -223,7 +123,13 @@
     loads = [
         pltpu.make_async_copy(src, dst, in_sem.at[i])
         for i, (src, dst) in enumerate(
-            ((keys_h, packed), (q_h, q), (fresh_h, fresh), (value_up_h, value_up), (out_proj_h, out_proj))
+            (
+                (pages_h.at[xfer], packed.at[xfer]),
+                (q_own_h, q.at[pl.ds(z * 2, 2)]),
+                (fresh_h, fresh),
+                (value_up_h, value_up),
+                (out_proj_h, out_proj),
+            )
         )
     ]
     for c in loads:
@@ -236,13 +142,44 @@
     def along(k):
         return (xfer, lax.rem(z + k, groups))
 
+    def owner_at(offset, sign):
+        dx, dy, dc = offset
+        return (lax.rem(x + 4 + sign * dx, 4) * 4 + lax.rem(y + 4 + sign * dy, 4)) * 2 + lax.rem(core + dc, 2)
+
     barrier = pltpu.get_barrier_semaphore()
-    peers = [along(k) for k in range(1, 8)]
-    peers += [near(k, 0, False) for k in range(1, 4)] + [near(0, k, False) for k in range(1, 4)]
-    peers += [near(0, 0, True)]
+    peers = [along(k) for k in range(1, 8)] + [(owner_at(offset, 1), z) for offset in OFFSETS]
     for peer in peers:
         pl.semaphore_signal(barrier, inc=1, device_id=peer, device_id_type=MESH)
     pl.semaphore_wait(barrier, len(peers))
+
+    def hop_of(way, j):
+        block = lax.rem(z + groups - (j - 1), groups) if way == 0 else lax.rem(z + j - 1, groups)
+        part = q.at[block * 2 + way] if j == groups // 2 else q.at[pl.ds(block * 2, 2)]
+        return pltpu.make_async_remote_copy(
+            src_ref=part,
+            dst_ref=part,
+            send_sem=r_send.at[way, j],
+            recv_sem=r_recv.at[way, j],
+            device_id=along(1 if way == 0 else 7),
+            device_id_type=MESH,
+        )
+
+    def page_to(i, offset):
+        to = owner_at(offset, 1)
+        return pltpu.make_async_remote_copy(
+            src_ref=pages_h.at[to],
+            dst_ref=packed.at[xfer],
+            send_sem=p_send.at[i],
+            recv_sem=p_recv.at[i],
+            device_id=(to, z),
+            device_id_type=MESH,
+        )
+
+    hops = [hop_of(way, j) for j in range(1, groups // 2 + 1) for way in (0, 1)]
+    page_copies = [page_to(i, offset) for i, offset in enumerate(OFFSETS)]
+    loads[1].wait()
+    for c in hops[:2] + page_copies:
+        c.start()
 
     def z_copies(way, half, hop):
         to = along(1 if way == 0 else 7)
@@ -270,7 +207,7 @@
         st = jnp.tile(got_st[way, half, hop], (half_rows // 8, 1)).T
         return st[:, 0:1], st[:, 1:2], got[way, half, hop].astype(jnp.float32)
 
-    started = []
+    started = hops + page_copies
 
     def send_on(way, half, hop):
         at = index_of(way, half, 4 - hop)
@@ -311,17 +248,18 @@
     keys = wide.shape[0]
     lane = lax.broadcasted_iota(jnp.int32, (1, keys), 1)
 
-    def unpack():
-        pages = packed.shape[0]
+    def unpack(slot):
+        to = pl.ds(pl.multiple_of(slot * page, page), page)
         for i in range(rank // 128):
-            wide[:, i * 128 : (i + 1) * 128] = packed[:, i * page : (i + 1) * page].reshape(keys, 128)
-        folded = packed[:, rank // 128 * page :]
+            wide[to, i * 128 : (i + 1) * 128] = packed[slot, i * page : (i + 1) * page, :]
+        folded = packed[slot, rank // 128 * page :, :]
         thin = narrow.shape[1]
-        both = jnp.concatenate([folded[:, :, :thin], folded[:, :, thin:]], axis=1)
-        narrow[...] = both.reshape(keys, thin)
+        narrow[to] = jnp.concatenate([folded[:, :thin], folded[:, thin:]], axis=0)
+
+    def hide():
         for r in range(requests):
             length, start = lengths[xfer * requests + r], starts[xfer * requests + r]
-            at = (lane // page * groups + z - start) & (pages * groups - 1)
+            at = (lane // page * groups + z - start) & (packed.shape[0] * groups - 1)
             seen = at * page + lane % page < length
             many = half_rows // requests
             bias[r * many : (r + 1) * many] = jnp.broadcast_to(jnp.where(seen, 0.0, LOW), (many, keys))
@@ -356,9 +294,19 @@
         both = jnp.where(lax.broadcasted_iota(jnp.int32, (2 * half_rows, 128), 1) % 2 == 0, top, total)
         stats[pl.ds(d * 2, 2)] = both.reshape(2, half_rows, 128)
 
+    for j in range(1, groups // 2):
+        for way in (0, 1):
+            hops[(j - 1) * 2 + way].wait_recv()
+            hops[j * 2 + way].start()
+        if j == 1:
+            hide()
+    for c in hops[-2:]:
+        c.wait_recv()
     loads[0].wait()
-    unpack()
-    loads[1].wait()
+    unpack(xfer)
+    for c, offset in zip(page_copies, OFFSETS):
+        c.wait_recv()
+        unpack(owner_at(offset, -1))
     attend(4)
     send_on(0, 0, 0)
     send_on(1, 1, 0)
@@ -475,14 +423,14 @@
         c.wait_send()
 
 
-def finish(lengths, starts, keys, q, fresh, value_up, out_proj, owners, groups, scale):
+def finish(lengths, starts, pages, q_own, fresh, value_up, out_proj, owners, groups, scale):
     vmem = pl.BlockSpec(memory_space=pltpu.VMEM)
-    operands = (keys, q, fresh, value_up, out_proj)
+    operands = (pages, q_own, fresh, value_up, out_proj)
     smem = pl.BlockSpec(memory_space=pltpu.SMEM)
     rows = fresh.shape[0]
-    half_rows, latent = q.shape[1:]
+    half_rows, latent = q_own.shape[1:]
     rank = value_up.shape[1]
-    tokens = keys.shape[0] * keys.shape[1] * 128 // latent
+    tokens = pages.shape[0] * pages.shape[1] * 128 // latent
     width, depth = out_proj.shape
     piece = owners * rows // groups
     dma = pltpu.SemaphoreType.DMA
@@ -492,7 +440,9 @@
         out_specs=vmem,
         out_shape=jax.ShapeDtypeStruct((piece, width), jnp.bfloat16),
         scratch_shapes=[
-            *(pltpu.VMEM(a.shape, a.dtype) for a in operands),
+            pltpu.VMEM(pages.shape, pages.dtype),
+            pltpu.VMEM((2 * groups, half_rows, latent), q_own.dtype),
+            *(pltpu.VMEM(a.shape, a.dtype) for a in operands[2:]),
             dma((5,)),
             pltpu.VMEM((tokens, rank), jnp.bfloat16),
             pltpu.VMEM((tokens, latent - rank), jnp.bfloat16),
@@ -516,9 +466,13 @@
             dma((2, 3, 4, 4)),
             dma((groups,)),
             dma((groups,)),
+            dma((owners,)),
+            dma((owners,)),
+            dma((2, 8)),
+            dma((2, 8)),
         ],
         compiler_params=pltpu.CompilerParams(
-            collective_id=1, has_side_effects=True, vmem_limit_bytes=56 * MIB
+            collective_id=0, has_side_effects=True, vmem_limit_bytes=56 * MIB
         ),
     )(lengths, starts, *operands)
 
@@ -529,10 +483,8 @@
     owners = lax.axis_size("xfer")
     groups = lax.axis_size("head")
     latent = kv_pool.shape[2]
-    lat_rank = value_up.shape[1]
     row_count, heads = queries.shape[:2]
     score_scale = queries.shape[2] ** (-0.5)
-    half_rows = row_count * heads // 2
     device = lax.axis_index("xfer") * groups + lax.axis_index("head")
     nth = (device - start_device) % (owners * groups)
     here = nth * kv_pool.shape[1] < lengths
@@ -540,10 +492,9 @@
     picked = (column[None, :] == nth[:, None]) & here[:, None]
     chosen = jnp.where(picked, page_table, 0).reshape(owners, -1, page_table.shape[1]).sum(axis=(1, 2))
     pages, q_own = prepare(chosen, kv_pool, queries, key_up)
-    keys, every = exchange(pages, q_own.reshape(2, half_rows, latent), groups)
-    every = every.reshape(groups * 2, half_rows, latent)
+    q_own = q_own.reshape(2, row_count * heads // 2, latent)
     return finish(
-        lengths, start_device, keys, every, new_latent, value_up, out_proj.T, owners, groups, score_scale
+        lengths, start_device, pages, q_own, new_latent, value_up, out_proj.T, owners, groups, score_scale
     )
 
 

time: 111 us -> 108 us (0.973)
  Pallas kernels: 107 us -> 104 us
    pallas_call x1 -> x0, Pallas kernels: 41.8 us -> none  [exchange(): pl.pallas_call(exchange_kernel, in_specs=[hbm, hbm], out_specs=[hbm, hbm]...]
    pallas_call x1, Pallas kernels: 58.2 us -> 98 us  [finish(): pl.pallas_call(functools.partial(finish_kernel, scale), in_specs=[smem, s...]
where the time goes in v9:
time: 108 us
  Pallas kernels  104 us (96%)
  other arithmetic  2.52 us (2%)
  local copies, waits for them, and re-layouts  1.45 us (1%)
    pallas_call x1, Pallas kernels, finish(): pl.pallas_call(functools.partial(finish_kernel, scale), in_specs=[smem, s...  98 us
    pallas_call x1, Pallas kernels, prepare(): pl.pallas_call(prepare_kernel, in_specs=[smem, hbm, vmem, hbm], out_specs...  6.14 us

profile of v9, /device:TPU:1, one launch (start us, length us, event | category | flops | bytes accessed | tf_op | source)
XLA Modules:
  0.0 108.1 jit_solution(7984906917649279967)
XLA Ops:
  0.0 0.7 multiply_compare_fusion
  0.7 1.2 %select_reduce_fusion = s32[256]{0:T(256)S(1)} fusion(s32[256,256]{1,0:T(8,128)} %param.12, s32[256]{0:T(256)S(1)} %get-tuple-element.10, pred[256]{0:T(512)(128)(4,1)S(1)} %get-tuple-element.9), kind=kLoop, calls=%fused_computation | loop fusion | flops 261888 | bytes 264448 | tf_op jit(solution)/shard_map/reduce_sum | solution.py:493
  1.9 0.1 reduce_sum.14
  2.0 0.6 reduce_sum.18.chosen
  2.6 6.1 %shard_map.91 = (bf16[32,288,128]{2,1,0:T(8,128)(2,1)}, bf16[256,576]{1,0:T(8,128)(2,1)}) custom-call(s32[32]{0:T(128)} %reduce_sum.18.chosen, bf16[32,64,576]{2,1,0:T(8,128)(2,1)} %pool.1, bf16[16,16,192]{2,1,0:T(8,128)(2,1)} %queries.1, bf16[16,128,512]{2,1,0:T(8,128)(2,1)} %key_up_h.1), custom_call_target="tpu_custom_call" | custom-call | tf_op jit(solution)/shard_map/pallas_call | solution.py:84
  8.7 98.0 %shard_map.92 = bf16[64,224]{1,0:T(8,128)(2,1)} custom-call(s32[256]{0:T(256)} %lengths.1, s32[256]{0:T(256)} %starts.1, bf16[32,288,128]{2,1,0:T(8,128)(2,1)} %get-tuple-element.7.pages_h, bf16[2,128,576]{2,1,0:T(8,128)(2,1)} %bitcast.3, bf16[16,576]{1,0:T(8,128)(2,1)} %fresh_h.1, bf16[16,512,128]{2,1,0:T(8,128)(2,1)} %value_up_h.1, bf16[224,2048]{1,0:T(8,128)(2,1)} %bitcast.2), custom_call_target="tpu_custom_call" | custom-call | tf_op jit(solution)/shard_map/pallas_call | solution.py:437
  106.7 1.4 %copy.11 = bf16[64,224]{1,0:T(8,128)(2,1)} copy(bf16[64,224]{1,0:T(8,128)(2,1)} %shard_map.92) | data formatting | bytes 57344

commit v10 on v9

--- a/solution.py
+++ b/solution.py
@@ -111,7 +111,7 @@
 
 def finish_kernel(
     scale, lengths, starts, pages_h, q_own_h, fresh_h, value_up_h, out_proj_h, out,
-    packed, q, fresh, value_up, out_proj, in_sem, wide, narrow, bias, s_s, w_s, acc, stats, sent, sent_st, got, got_st, own, own_st, held, share, parts, z_send, z_recv, x_send, x_recv, o_send, o_recv,
+    pages_v, packed, q, fresh, value_up, out_proj, in_sem, wide, narrow, bias, s_s, w_s, acc, stats, sent, sent_st, got, got_st, own, own_st, held, share, parts, z_send, z_recv, x_send, x_recv, o_send, o_recv,
     p_send, p_recv, r_send, r_recv,
 ):
     z = lax.axis_index("head")
@@ -124,7 +124,7 @@
         pltpu.make_async_copy(src, dst, in_sem.at[i])
         for i, (src, dst) in enumerate(
             (
-                (pages_h.at[xfer], packed.at[xfer]),
+                (pages_h, pages_v),
                 (q_own_h, q.at[pl.ds(z * 2, 2)]),
                 (fresh_h, fresh),
                 (value_up_h, value_up),
@@ -135,16 +135,20 @@
     for c in loads:
         c.start()
 
+    xs = [x] + [lax.rem(x + k, 4) for k in range(1, 4)]
+    ys = [y] + [lax.rem(y + k, 4) for k in range(1, 4)]
+    zs = [z] + [lax.rem(z + k, groups) for k in range(1, groups)]
+
     def near(dx, dy, flip):
         c = 1 - core if flip else core
-        return ((lax.rem(x + dx, 4) * 4 + lax.rem(y + dy, 4)) * 2 + c, z)
+        return ((xs[dx] * 4 + ys[dy]) * 2 + c, z)
 
     def along(k):
-        return (xfer, lax.rem(z + k, groups))
+        return (xfer, zs[k])
 
     def owner_at(offset, sign):
         dx, dy, dc = offset
-        return (lax.rem(x + 4 + sign * dx, 4) * 4 + lax.rem(y + 4 + sign * dy, 4)) * 2 + lax.rem(core + dc, 2)
+        return (xs[sign * dx % 4] * 4 + ys[sign * dy % 4]) * 2 + (1 - core if dc else core)
 
     barrier = pltpu.get_barrier_semaphore()
     peers = [along(k) for k in range(1, 8)] + [(owner_at(offset, 1), z) for offset in OFFSETS]
@@ -153,7 +157,7 @@
     pl.semaphore_wait(barrier, len(peers))
 
     def hop_of(way, j):
-        block = lax.rem(z + groups - (j - 1), groups) if way == 0 else lax.rem(z + j - 1, groups)
+        block = zs[(1 - j) % groups] if way == 0 else zs[j - 1]
         part = q.at[block * 2 + way] if j == groups // 2 else q.at[pl.ds(block * 2, 2)]
         return pltpu.make_async_remote_copy(
             src_ref=part,
@@ -167,7 +171,7 @@
     def page_to(i, offset):
         to = owner_at(offset, 1)
         return pltpu.make_async_remote_copy(
-            src_ref=pages_h.at[to],
+            src_ref=pages_v.at[to],
             dst_ref=packed.at[xfer],
             send_sem=p_send.at[i],
             recv_sem=p_recv.at[i],
@@ -178,7 +182,10 @@
     hops = [hop_of(way, j) for j in range(1, groups // 2 + 1) for way in (0, 1)]
     page_copies = [page_to(i, offset) for i, offset in enumerate(OFFSETS)]
     loads[1].wait()
-    for c in hops[:2] + page_copies:
+    for c in hops[:2]:
+        c.start()
+    loads[0].wait()
+    for c in page_copies:
         c.start()
 
     def z_copies(way, half, hop):
@@ -196,7 +203,7 @@
         ]
 
     def index_of(way, half, distance):
-        d = lax.rem(z + distance if way == 0 else z + groups - distance, groups)
+        d = zs[distance] if way == 0 else zs[groups - distance]
         return d * 2 + half
 
     odd = lax.broadcasted_iota(jnp.int32, (half_rows, 128), 1) % 2
@@ -248,11 +255,11 @@
     keys = wide.shape[0]
     lane = lax.broadcasted_iota(jnp.int32, (1, keys), 1)
 
-    def unpack(slot):
+    def unpack(source, slot):
         to = pl.ds(pl.multiple_of(slot * page, page), page)
         for i in range(rank // 128):
-            wide[to, i * 128 : (i + 1) * 128] = packed[slot, i * page : (i + 1) * page, :]
-        folded = packed[slot, rank // 128 * page :, :]
+            wide[to, i * 128 : (i + 1) * 128] = source[slot, i * page : (i + 1) * page, :]
+        folded = source[slot, rank // 128 * page :, :]
         thin = narrow.shape[1]
         narrow[to] = jnp.concatenate([folded[:, :thin], folded[:, thin:]], axis=0)
 
@@ -265,7 +272,7 @@
             bias[r * many : (r + 1) * many] = jnp.broadcast_to(jnp.where(seen, 0.0, LOW), (many, keys))
 
     def attend(distance):
-        d = lax.rem(z + distance, groups)
+        d = zs[distance]
         mine = q[pl.ds(d * 2, 2)].reshape(2 * half_rows, q.shape[2])
         top = None
         for b in range(0, keys, BLOCK):
@@ -302,11 +309,10 @@
             hide()
     for c in hops[-2:]:
         c.wait_recv()
-    loads[0].wait()
-    unpack(xfer)
+    unpack(pages_v, xfer)
     for c, offset in zip(page_copies, OFFSETS):
         c.wait_recv()
-        unpack(owner_at(offset, -1))
+        unpack(packed, owner_at(offset, -1))
     attend(4)
     send_on(0, 0, 0)
     send_on(1, 1, 0)
@@ -341,7 +347,7 @@
 
     def block_of(half, a, b):
         dx, dy = (a, b) if half == 0 else (b, a)
-        return (lax.rem(x + 4 - dx, 4) * 4 + lax.rem(y + 4 - dy, 4)) * 2
+        return (xs[-dx % 4] * 4 + ys[-dy % 4]) * 2
 
     def to_first(half, k):
         return near(k, 0, False) if half == 0 else near(0, k, False)
@@ -412,7 +418,7 @@
         )
 
     for k in (4, 3, 5, 2, 6, 1, 7):
-        share[0, k] = parts[lax.rem(z + k, groups)].astype(jnp.bfloat16)
+        share[0, k] = parts[zs[k]].astype(jnp.bfloat16)
         start(final(k))
     done = parts[z]
     for k in (1, 7, 2, 6, 3, 5, 4):
@@ -440,6 +446,7 @@
         out_specs=vmem,
         out_shape=jax.ShapeDtypeStruct((piece, width), jnp.bfloat16),
         scratch_shapes=[
+            pltpu.VMEM(pages.shape, pages.dtype),
             pltpu.VMEM(pages.shape, pages.dtype),
             pltpu.VMEM((2 * groups, half_rows, latent), q_own.dtype),
             *(pltpu.VMEM(a.shape, a.dtype) for a in operands[2:]),

time: 108 us -> 109 us (level)
  no operation moved by 1% of the time
where the time goes in v10:
time: 109 us
  Pallas kernels  105 us (96%)
  other arithmetic  2.52 us (2%)
  local copies, waits for them, and re-layouts  1.45 us (1%)
    pallas_call x1, Pallas kernels, finish(): pl.pallas_call(functools.partial(finish_kernel, scale), in_specs=[smem, s...  98.5 us
    pallas_call x1, Pallas kernels, prepare(): pl.pallas_call(prepare_kernel, in_specs=[smem, hbm, vmem, hbm], out_specs...  6.14 us

profile of v10, /device:TPU:1, one launch (start us, length us, event | category | flops | bytes accessed | tf_op | source)
XLA Modules:
  0.0 108.6 jit_solution(5255682008776265807)
XLA Ops:
  0.0 0.7 multiply_compare_fusion
  0.7 1.2 %select_reduce_fusion = s32[256]{0:T(256)S(1)} fusion(s32[256,256]{1,0:T(8,128)} %param.12, s32[256]{0:T(256)S(1)} %get-tuple-element.10, pred[256]{0:T(512)(128)(4,1)S(1)} %get-tuple-element.9), kind=kLoop, calls=%fused_computation | loop fusion | flops 261888 | bytes 264448 | tf_op jit(solution)/shard_map/reduce_sum | solution.py:500
  1.9 0.1 reduce_sum.14
  2.0 0.6 reduce_sum.18.chosen
  2.6 6.1 %shard_map.91 = (bf16[32,288,128]{2,1,0:T(8,128)(2,1)}, bf16[256,576]{1,0:T(8,128)(2,1)}) custom-call(s32[32]{0:T(128)} %reduce_sum.18.chosen, bf16[32,64,576]{2,1,0:T(8,128)(2,1)} %pool.1, bf16[16,16,192]{2,1,0:T(8,128)(2,1)} %queries.1, bf16[16,128,512]{2,1,0:T(8,128)(2,1)} %key_up_h.1), custom_call_target="tpu_custom_call" | custom-call | tf_op jit(solution)/shard_map/pallas_call | solution.py:84
  8.7 98.5 %shard_map.92 = bf16[64,224]{1,0:T(8,128)(2,1)} custom-call(s32[256]{0:T(256)} %lengths.1, s32[256]{0:T(256)} %starts.1, bf16[32,288,128]{2,1,0:T(8,128)(2,1)} %get-tuple-element.7.pages_h, bf16[2,128,576]{2,1,0:T(8,128)(2,1)} %bitcast.3, bf16[16,576]{1,0:T(8,128)(2,1)} %fresh_h.1, bf16[16,512,128]{2,1,0:T(8,128)(2,1)} %value_up_h.1, bf16[224,2048]{1,0:T(8,128)(2,1)} %bitcast.2), custom_call_target="tpu_custom_call" | custom-call | tf_op jit(solution)/shard_map/pallas_call | solution.py:443
  107.2 1.4 %copy.11 = bf16[64,224]{1,0:T(8,128)(2,1)} copy(bf16[64,224]{1,0:T(8,128)(2,1)} %shard_map.92) | data formatting | bytes 57344
